TPU v7x, 256 devices: a whole 4x4x8 slice. The times are simulated.
256 devices in a mesh: grp: 2 (over x_hi), pb: 8 (over y, core), ha: 16 (over x_lo, z).
Axes of the slice: x: 4 (x_hi: 2, x_lo: 2; x = x_hi * 2 + x_lo), y: 4, z: 8, core: 2. Of those that a mesh axis runs over, the one named last changes fastest.
Arguments:
- hyena_proj: bfloat16 [3, 4096, 4096], P(None, 'ha', ('grp', 'pb')), may hold values from -6 to 6
- dskip: float32 [4096], P(('grp', 'pb')), may hold values from -1 to 1
- filters: float32 [3, 2, 4096, 4096], P(None, None, ('grp', 'pb', 'ha')), may hold values from -6 to 6
- resident: float32 [2, 2, 4096, 4096], P(None, None, ('grp', 'pb', 'ha')), may hold values from -384 to 384
- cache_kv: bfloat16 [2, 4096, 4096], P(None, 'ha', ('grp', 'pb'))
- norm_gain: float32 [4096], replicated, may hold values from 0.5 to 1.5
- w_qkv: bfloat16 [4096, 3, 4096], P(None, None, ('grp', 'pb'))
- w_out: bfloat16 [4096, 4096], P(None, ('grp', 'pb')), may hold values from -0.09375 to 0.09375
Outputs:
- mixed: bfloat16 [4096, 4096], P('ha', ('grp', 'pb'))
- block_spectrum: float32 [2, 4096, 4096], P(None, ('grp', 'pb', 'ha'))
All inputs are finite; a program needn't handle non-finite values.
Results may differ from a plain program's by a relative error of at most 0.015.
Values may be sent and summed in bfloat16 or wider, within the bound.
No kernel may reach another device: no remote copies, remote signals or barrier semaphores. Data moves between devices by JAX's collectives and lax.ppermute only.
A program may use at most 128 MiB of HBM per device.

v0:
```python
import math

import jax
import jax.numpy as jnp
from jax import lax
from jax.sharding import PartitionSpec as P

HEAD = 128


highest = lax.Precision.HIGHEST


def wave(count_a, count_b, modulus):
    first = lax.broadcasted_iota(jnp.int32, (count_a, count_b), 0)
    second = lax.broadcasted_iota(jnp.int32, (count_a, count_b), 1)
    angles = 2.0 * math.pi / modulus * (first * second % modulus).astype(jnp.float32)
    return (jnp.cos(angles), jnp.sin(angles))


def split_table(table):
    leading = table.astype(jnp.bfloat16)
    remainder = table - lax.optimization_barrier(leading).astype(jnp.float32)
    middle = remainder.astype(jnp.bfloat16)
    trailing = (remainder - lax.optimization_barrier(middle).astype(jnp.float32)).astype(
        jnp.bfloat16
    )
    return (leading, middle, trailing)


def rotate(values, positions):
    half = values.shape[-1] // 2
    freqs = 10000.0 ** (-jnp.arange(half, dtype=jnp.float32) / half)
    angles = positions.astype(jnp.float32)[:, None] * freqs[None, :]
    cosine = jnp.cos(angles)[:, None, :]
    sine = jnp.sin(angles)[:, None, :]
    first = values[..., :half]
    second = values[..., half:]
    return jnp.concatenate(
        [first * cosine - second * sine, first * sine + second * cosine], axis=-1
    )


def forward_transform(signal):
    chans, length = signal.shape
    nfft = 2 * length
    blocks = nfft // 128
    shaped = signal.reshape(chans, 64, blocks)
    cos_one, sin_one = wave(64, 128, 128)
    table = jnp.concatenate([cos_one, -sin_one], axis=1)
    section = jnp.zeros((chans, blocks, 256), jnp.float32)
    for piece in split_table(table):
        section = section + jnp.einsum(
            "cab,ak->cbk", shaped, piece, preferred_element_type=jnp.float32
        )
    part_real = section[:, :, :128]
    part_imag = section[:, :, 128:]
    cos_tw, sin_tw = wave(blocks, 128, nfft)
    turn_real = part_real * cos_tw + part_imag * sin_tw
    turn_imag = part_imag * cos_tw - part_real * sin_tw
    cos_two, sin_two = wave(blocks, blocks // 2, blocks)
    out_real = jnp.einsum("cbk,bm->cmk", turn_real, cos_two, precision=highest) + jnp.einsum(
        "cbk,bm->cmk", turn_imag, sin_two, precision=highest
    )
    out_imag = jnp.einsum("cbk,bm->cmk", turn_imag, cos_two, precision=highest) - jnp.einsum(
        "cbk,bm->cmk", turn_real, sin_two, precision=highest
    )
    return (out_real.reshape(chans, length), out_imag.reshape(chans, length))


def inverse_transform(spec_real, spec_imag):
    chans, length = spec_real.shape
    nfft = 2 * length
    blocks = nfft // 128
    weight_bins = jnp.where(jnp.arange(length) == 0, 1.0, 2.0).astype(jnp.float32)[None, :] / nfft
    scaled_real = (spec_real * weight_bins).reshape(chans, blocks // 2, 128)
    scaled_imag = (spec_imag * weight_bins).reshape(chans, blocks // 2, 128)
    cos_two, sin_two = wave(blocks // 2, blocks, blocks)
    step_real = jnp.einsum("cmk,mj->cjk", scaled_real, cos_two, precision=highest) - jnp.einsum(
        "cmk,mj->cjk", scaled_imag, sin_two, precision=highest
    )
    step_imag = jnp.einsum("cmk,mj->cjk", scaled_real, sin_two, precision=highest) + jnp.einsum(
        "cmk,mj->cjk", scaled_imag, cos_two, precision=highest
    )
    cos_tw, sin_tw = wave(blocks, 128, nfft)
    turn_real = step_real * cos_tw - step_imag * sin_tw
    turn_imag = step_real * sin_tw + step_imag * cos_tw
    cos_one, sin_one = wave(128, 64, 128)
    result = jnp.einsum("cjk,kt->ctj", turn_real, cos_one, precision=highest) - jnp.einsum(
        "cjk,kt->ctj", turn_imag, sin_one, precision=highest
    )
    return result.reshape(chans, length)


def absorb(carry, queries, keys_piece, values_piece, allowed):
    top_old, total_old, accum_old = carry
    scores = jnp.einsum(
        "rhd,shd->hrs", queries, keys_piece, preferred_element_type=jnp.float32
    ) / jnp.sqrt(jnp.float32(queries.shape[-1]))
    scores = jnp.where(allowed[None], scores, jnp.float32(-1e30))
    top_new = jnp.maximum(top_old, jnp.max(scores, axis=2))
    factor = jnp.exp(top_old - top_new)
    expd = jnp.where(allowed[None], jnp.exp(scores - top_new[:, :, None]), jnp.float32(0.0))
    total_new = total_old * factor + jnp.sum(expd, axis=2)
    accum_new = accum_old * factor[:, :, None] + jnp.einsum(
        "hrs,shd->hrd", expd.astype(jnp.bfloat16), values_piece, preferred_element_type=jnp.float32
    )
    return (top_new, total_new, accum_new)


def local(hyena_proj, dskip, filters, resident, cache_kv, norm_gain, w_qkv, w_out):
    row_count = hyena_proj.shape[1]
    head_cols = w_qkv.shape[2]
    head_size = HEAD
    heads_here = head_cols // head_size
    width = w_qkv.shape[0]
    ha_count = lax.axis_size("ha")
    ha_index = lax.axis_index("ha")
    gated = (hyena_proj[1].astype(jnp.float32) * hyena_proj[2].astype(jnp.float32)).astype(
        jnp.bfloat16
    )
    columns = lax.all_to_all(gated.T, "ha", split_axis=0, concat_axis=1, tiled=True)
    real_part, imag_part = forward_transform(columns)
    sum_real = real_part * filters[0, 0] - imag_part * filters[0, 1]
    sum_imag = real_part * filters[0, 1] + imag_part * filters[0, 0]
    for which in (1, 2):
        old_real = resident[which - 1, 0]
        old_imag = resident[which - 1, 1]
        sum_real = sum_real + old_real * filters[which, 0] - old_imag * filters[which, 1]
        sum_imag = sum_imag + old_real * filters[which, 1] + old_imag * filters[which, 0]
    conv_cols = inverse_transform(sum_real, sum_imag).astype(jnp.bfloat16)
    conv = lax.all_to_all(conv_cols, "ha", split_axis=1, concat_axis=0, tiled=True).T
    hyena_out = (
        hyena_proj[0].astype(jnp.float32)
        * (conv.astype(jnp.float32) + dskip * gated.astype(jnp.float32))
    ).astype(jnp.bfloat16)
    whole = lax.all_gather(hyena_out, ("grp", "pb"), axis=1, tiled=True).astype(jnp.float32)
    meansq = jnp.mean(whole * whole, axis=1, keepdims=True)
    normed = (whole * lax.rsqrt(meansq + 1e-05) * norm_gain).astype(jnp.bfloat16)
    qkv = jnp.dot(normed, w_qkv.reshape(width, 3 * head_cols), preferred_element_type=jnp.float32)
    qkv = qkv.reshape(row_count, 3, heads_here, head_size)
    cache_rows = cache_kv.shape[1]
    cache_len = cache_rows * ha_count
    local_rows = ha_index * row_count + jnp.arange(row_count, dtype=jnp.int32)
    queries = rotate(qkv[:, 0], cache_len + local_rows).astype(jnp.bfloat16)
    keys_now = rotate(qkv[:, 1], cache_len + local_rows).astype(jnp.bfloat16)
    values_now = qkv[:, 2].astype(jnp.bfloat16)
    start_carry = (
        jnp.full((heads_here, row_count), -1e30, jnp.float32),
        jnp.zeros((heads_here, row_count), jnp.float32),
        jnp.zeros((heads_here, row_count, head_size), jnp.float32),
    )
    pieces = (
        lax.all_gather(cache_kv[0], "ha", axis=0, tiled=True),
        lax.all_gather(cache_kv[1], "ha", axis=0, tiled=True),
    )
    keys_piece = pieces[0].reshape(-1, heads_here, head_size)
    values_piece = pieces[1].reshape(-1, heads_here, head_size)
    allowed = jnp.ones((row_count, keys_piece.shape[0]), bool)
    carry = absorb(start_carry, queries, keys_piece, values_piece, allowed)
    pieces = (
        lax.all_gather(keys_now, "ha", axis=0, tiled=True),
        lax.all_gather(values_now, "ha", axis=0, tiled=True),
    )
    keys_piece = pieces[0]
    values_piece = pieces[1]
    key_rows = jnp.arange(keys_piece.shape[0], dtype=jnp.int32)
    allowed = key_rows[None, :] <= local_rows[:, None]
    top_fin, total_fin, accum_fin = absorb(carry, queries, keys_piece, values_piece, allowed)
    heads_out = (accum_fin / total_fin[:, :, None]).astype(jnp.bfloat16)
    heads_out = jnp.transpose(heads_out, (1, 0, 2)).reshape(row_count, head_cols)
    attended = jnp.dot(
        lax.all_gather(heads_out, ("grp", "pb"), axis=1, tiled=True),
        w_out,
        preferred_element_type=jnp.float32,
    )
    mixed = (hyena_out.astype(jnp.float32) + attended).astype(jnp.bfloat16)
    block_spectrum = jnp.stack([real_part, imag_part])
    return (mixed, block_spectrum)


def solution(mesh):
    return jax.shard_map(
        local,
        mesh=mesh,
        in_specs=(
            P(None, "ha", ("grp", "pb")),
            P(("grp", "pb")),
            P(None, None, ("grp", "pb", "ha"), None),
            P(None, None, ("grp", "pb", "ha"), None),
            P(None, "ha", ("grp", "pb")),
            P(),
            P(None, None, ("grp", "pb")),
            P(None, ("grp", "pb")),
        ),
        out_specs=(P("ha", ("grp", "pb")), P(None, ("grp", "pb", "ha"), None)),
        check_vma=False,
    )
```

profile of v0, /device:TPU:1, one launch (start us, length us, event | category | flops | bytes accessed | tf_op | source)
XLA Modules:
  0.0 471.7 jit_solution(15275120879116100120)
XLA Ops:
  7.2 1.2 fusion.99
  8.3 0.8 copy.15
  9.1 10.0 %all-to-all-start = ((bf16[16,16,256]{2,1,0:T(8,128)(2,1)}), bf16[16,16,256]{2,1,0:T(8,128)(2,1)S(1)}, u32[]{:S(2)}, u32[]{:S(2)}) async-start(bf16[16,16,256]{2,1,0:T(8,128)(2,1)} %bitcast.6), calls=%async_computation | async-start | bytes 262144 | tf_op jit(solution)/shard_map/all_to_all | solution.py:122
  19.2 0.1 sine_negate_fusion
  19.4 1.9 multiply_bitcast_fusion.3
  21.3 0.1 copy.38
  21.4 0.7 copy.39
  22.1 0.8 copy.40
  22.9 0.8 copy.41
  23.6 0.8 copy.42
  24.4 0.8 copy.43
  25.2 0.8 copy.44
  26.0 0.8 copy.45
  26.7 0.8 copy.46
  27.5 0.8 copy.47
  28.3 0.1 fusion.116
  28.5 0.2 reshape.235
  28.7 0.3 fusion.84
  29.0 0.3 convolution_add_fusion.1
  29.3 0.3 convolution_add_fusion
  29.7 0.5 fusion.70
  30.2 0.5 fusion.69
  30.7 0.5 fusion.23
  31.3 2.7 fusion.58
  33.9 0.7 fusion.114
  34.6 0.7 fusion.106
  35.4 0.7 convolution_subtract_fusion
  36.1 0.7 convolution_add_fusion.2
  36.8 1.7 fusion.50
  38.5 1.7 fusion.22
  40.2 0.2 convert_element_type.170
  40.5 14.8 %all_to_all.26 = bf16[16,16,256]{2,0,1:T(8,128)(2,1)S(1)} all-to-all(bf16[16,16,256]{2,0,1:T(8,128)(2,1)S(1)} %copy.20), channel_id=1, replica_groups=mesh['grp'=2,'pb'=8,'ha'=16] {'ha'}, dimensions={1} | all-to-all | bytes 262144 | tf_op jit(solution)/shard_map/all_to_all | solution.py:132
  55.3 0.1 copy.21
  55.4 0.7 fusion.62
  56.2 0.0 all-gather.18.cloned.1.call-start
  56.2 1.6 fusion.192
  58.0 0.8 copy.37
  58.7 0.2 all-gather.12.cloned.1.call-start
  59.0 8.7 %copy.22 = bf16[4096,3,256]{0,2,1:T(8,128)(2,1)} copy(bf16[4096,3,256]{2,0,1:T(8,128)(2,1)} %param.14) | data formatting | bytes 12582912 | tf_op args[6]
  67.7 0.3 multiply_cosine_fusion
  68.1 40.0 %all-gather.10.cloned.1.call-done = bf16[256,4096]{1,0:T(8,128)(2,1)} async-done(((bf16[256,256]{1,0:T(8,128)(2,1)}), bf16[256,4096]{1,0:T(8,128)(2,1)}) %all-gather.10.cloned.1.call-update) | async-done | bytes 2097168 | tf_op jit(solution)/shard_map/all_gather | solution.py:137
  108.1 2.1 fusion.5
  110.2 5.3 %fusion.16 = f32[256,3,2,128]{0,3,2,1:T(8,128)S(1)} fusion(bf16[3,2,128,4096]{3,2,1,0:T(8,128)(2,1)} %bitcast.226, bf16[256,4096]{1,0:T(8,128)(2,1)} %all-gather.10.cloned.1.call-done, f32[4096]{0:T(1024)S(1)} %copy-done.14, f32[256]{0:T(256)S(1)} %add_rsqrt_fusion), kind=kOutput, calls=%fused_computation.21 | convolution fusion | flops 1614807040 | bytes 9192448 | tf_op jit(solution)/shard_map/dot_general | solution.py:140
  115.5 0.1 subtract_convert_fusion.1
  115.6 0.7 pad_maximum_fusion.2
  116.4 0.7 slice.164
  117.1 0.0 all-gather.14.cloned.1.call-start
  117.1 0.7 iota_compare_fusion
  117.8 51.7 %all-gather.18.cloned.1.call-done = bf16[1,4096,256]{2,1,0:T(8,128)(2,1)} async-done(((bf16[1,256,256]{2,1,0:T(8,128)(2,1)}), bf16[1,4096,256]{2,1,0:T(8,128)(2,1)}) %all-gather.18.cloned.1.call-update) | async-done | bytes 2097168 | tf_op jit(solution)/shard_map/all_gather | solution.py:155
  169.5 4.1 copy.26
  173.7 66.8 %all-gather.16.cloned.1.call-done = bf16[1,4096,256]{1,2,0:T(8,128)(2,1)} async-done(((bf16[1,256,256]{1,2,0:T(8,128)(2,1)}), bf16[1,4096,256]{1,2,0:T(8,128)(2,1)}) %all-gather.16.cloned.1.call-update) | async-done | bytes 2097168 | tf_op jit(solution)/shard_map/all_gather | solution.py:154
  240.5 6.2 %multiply_reduce_fusion = (f32[2,256]{1,0:T(2,128)S(1)}, f32[2,256,4096]{2,1,0:T(8,128)}) fusion(bf16[4096,2,128]{0,2,1:T(8,128)(2,1)} %bitcast.228, bf16[256,2,64]{0,2,1:T(8,128)(2,1)S(1)} %get-tuple-element.19, bf16[256,2,64]{0,2,1:T(8,128)(2,1)S(1)} %get-tuple-element.18), kind=kOutput, calls=%fused_computation.3 | convolution fusion | flops 541326848 | bytes 10618880 | tf_op jit(solution)/shard_map/rhd,shd->hrs/dot_general | solution.py:97
  246.7 67.3 %all-gather.12.cloned.1.call-done = bf16[4096,2,128]{0,2,1:T(8,128)(2,1)} async-done(((bf16[256,2,128]{0,2,1:T(8,128)(2,1)}), bf16[4096,2,128]{0,2,1:T(8,128)(2,1)}) %all-gather.12.cloned.1.call-update) | async-done | bytes 2097168 | tf_op jit(solution)/shard_map/all_gather | solution.py:162
  314.0 4.0 fusion
  318.0 1.5 fusion.1
  319.5 2.7 fusion.3
  322.2 65.2 %all-gather.20.cloned.1.call-done = bf16[4096,1,2,128]{0,3,2,1:T(8,128)(2,1)} async-done(((bf16[256,1,2,128]{0,3,2,1:T(8,128)(2,1)}), bf16[4096,1,2,128]{0,3,2,1:T(8,128)(2,1)}) %all-gather.20.cloned.1.call-update) | async-done | bytes 2097168 | tf_op jit(solution)/shard_map/all_gather | solution.py:163
  387.4 5.8 %fusion.25 = f32[256,2,128]{0,2,1:T(8,128)S(1)} fusion(bf16[4096,1,2,128]{0,3,2,1:T(8,128)(2,1)} %all-gather.20.cloned.1.call-done, f32[2,256,4096]{2,1,0:T(8,128)} %copy-done.2, f32[2,256]{1,0:T(2,128)S(1)} %get-tuple-element.28, pred[256,4096]{1,0:T(8,128)(4,1)S(1)} %iota_compare_fusion), kind=kOutput, calls=%fused_computation.36 | convolution fusion | flops 547356672 | bytes 11798528 | tf_op jit(solution)/shard_map/hrs,shd->hrd/dot_general | solution.py:105
  393.2 5.9 %fusion.46 = bf16[256,2,128]{0,2,1:T(8,128)(2,1)} fusion(f32[256,2,128]{0,2,1:T(8,128)S(1)} %fusion.25, bf16[4096,2,128]{0,2,1:T(8,128)(2,1)S(1)} %bitcast.227, f32[2,256,4096]{2,1,0:T(8,128)} %get-tuple-element.33, f32[2,256]{1,0:T(2,128)S(1)} %get-tuple-element.27, f32[256,2]{0,1:T(2,128)S(1)} %get-tuple-element.2, f32[256,2]{0,1:T(2,128)S(1)} %get-tuple-element.3, ...), kind=kOutput, calls=%fused_computation.44 | convolution fusion | flops 543490048 | bytes 10887168 | tf_op jit(solution)/shard_map/hrs,shd->hrd/dot_general | solution.py:105
  399.2 0.1 stack_reshape.7
  399.2 0.1 stack_reshape.6
  399.3 0.8 pad_maximum_fusion
  400.1 61.7 %all-gather.14.cloned.1.call-done = bf16[256,4096]{0,1:T(8,128)(2,1)} async-done(((bf16[256,256]{0,1:T(8,128)(2,1)}), bf16[256,4096]{0,1:T(8,128)(2,1)}) %all-gather.14.cloned.1.call-update) | async-done | bytes 2097168 | tf_op jit(solution)/shard_map/all_gather | solution.py:173
  461.9 3.0 fusion.42
  (53 shorter events, 0.5 us)
Async XLA Ops:
  7.2 454.7 %copy-start = (bf16[4096,256]{1,0:T(8,128)(2,1)S(1)}, bf16[4096,256]{1,0:T(8,128)(2,1)}, u32[]{:S(2)}) copy-start(bf16[4096,256]{1,0:T(8,128)(2,1)} %param.15) | copy-start | bytes 6291460
  9.1 19.3 %all-to-all-start = ((bf16[16,16,256]{2,1,0:T(8,128)(2,1)}), bf16[16,16,256]{2,1,0:T(8,128)(2,1)S(1)}, u32[]{:S(2)}, u32[]{:S(2)}) async-start(bf16[16,16,256]{2,1,0:T(8,128)(2,1)} %bitcast.6), calls=%async_computation | async-start | bytes 262144 | tf_op jit(solution)/shard_map/all_to_all | solution.py:122
  19.1 88.9 %all-gather.10.cloned.1.call-start = ((), (), s32[]{:S(2)}) async-start(), calls=%async_computation.2 | async-start | bytes 2228224 | tf_op jit(solution)/shard_map/all_gather | solution.py:137
  28.6 2.6 copy-start.6
  28.6 2.6 copy-start.7
  28.6 2.6 copy-start.8
  28.7 2.6 copy-start.9
  28.7 2.6 copy-start.10
  28.7 2.6 copy-start.11
  31.3 24.2 %copy-start.4 = (bf16[3,256,256]{2,1,0:T(8,128)(2,1)S(1)}, bf16[3,256,256]{2,1,0:T(8,128)(2,1)}, u32[]{:S(2)}) copy-start(bf16[3,256,256]{2,1,0:T(8,128)(2,1)} %param.8) | copy-start | bytes 1179652
  31.3 24.2 %copy-start.13 = (f32[256]{0:T(256)S(1)}, f32[256]{0:T(256)}, u32[]{:S(2)}) copy-start(f32[256]{0:T(256)} %param.9) | copy-start | bytes 3076
  56.2 113.4 %all-gather.18.cloned.1.call-start = ((), (), s32[]{:S(2)}) async-start(), calls=%async_computation.6 | async-start | bytes 2228224 | tf_op jit(solution)/shard_map/all_gather | solution.py:155
  57.9 182.6 %all-gather.16.cloned.1.call-start = ((), (), s32[]{:S(2)}) async-start(), calls=%async_computation.5 | async-start | bytes 2228224 | tf_op jit(solution)/shard_map/all_gather | solution.py:154
  58.7 255.2 %all-gather.12.cloned.1.call-start = ((), (), s32[]{:S(2)}) async-start(), calls=%async_computation.3 | async-start | bytes 2228224 | tf_op jit(solution)/shard_map/all_gather | solution.py:162
  59.0 51.2 %copy-start.14 = (f32[4096]{0:T(1024)S(1)}, f32[4096]{0:T(1024)}, u32[]{:S(2)}) copy-start(f32[4096]{0:T(1024)} %param.13) | copy-start | bytes 49156
  116.3 271.1 %all-gather.20.cloned.1.call-start = ((), (), s32[]{:S(2)}) async-start(), calls=%async_computation.7 | async-start | bytes 2228224 | tf_op jit(solution)/shard_map/all_gather | solution.py:163
  117.1 344.8 %all-gather.14.cloned.1.call-start = ((), (), s32[]{:S(2)}) async-start(), calls=%async_computation.4 | async-start | bytes 2228224 | tf_op jit(solution)/shard_map/all_gather | solution.py:173
  314.0 4.0 copy-start.1
  318.0 4.2 copy-start.2
  387.4 5.8 %copy-start.3 = (bf16[1,4096,256]{1,2,0:T(8,128)(2,1)S(1)}, bf16[1,4096,256]{1,2,0:T(8,128)(2,1)}, u32[]{:S(2)}) copy-start(bf16[1,4096,256]{1,2,0:T(8,128)(2,1)} %copy.26) | copy-start | bytes 6291460
  393.2 6.1 %copy-start.5 = (f32[16,32,128]{2,1,0:T(8,128)S(1)}, f32[16,32,128]{2,1,0:T(8,128)}, u32[]{:S(2)}) copy-start(f32[16,32,128]{2,1,0:T(8,128)} %get-tuple-element.31) | copy-start | bytes 786436
  393.2 68.7 %copy-start.12 = (bf16[256,256]{1,0:T(8,128)(2,1)S(1)}, bf16[256,256]{1,0:T(8,128)(2,1)}, u32[]{:S(2)}) copy-start(bf16[256,256]{1,0:T(8,128)(2,1)} %fusion.62) | copy-start | bytes 393220
Sparse Core Ops, SparseCore 0:
  56.3 51.6 all-gather.9
  109.8 59.6 all-gather.17
  171.3 69.1 all-gather.15
  242.1 71.8 all-gather.11
  315.5 71.8 all-gather.19
  399.3 62.5 all-gather.13
where the time goes:
time: 472 us
  waiting for transfers between devices  353 us (75%)
  matrix products  41.6 us (9%)
  local copies, waits for them, and re-layouts  24.4 us (5%)
  blocking collectives  14.8 us (3%)
  between operations  14.6 us (3%)
  other arithmetic  13 us (3%)
  starting transfers between devices  10.5 us (2%)
    all_gather x1, waiting for transfers between devices, local(): lax.all_gather(keys_now, 'ha', axis=0, tiled=True)  67.3 us
    all_gather x1, waiting for transfers between devices, local(): lax.all_gather(cache_kv[0], 'ha', axis=0, tiled=True)  66.8 us
    all_gather x1, waiting for transfers between devices, local(): lax.all_gather(values_now, 'ha', axis=0, tiled=True)  65.2 us
    all_gather x1, waiting for transfers between devices, local(): lax.all_gather(heads_out, ('grp', 'pb'), axis=1, tiled=True)  61.7 us
    all_gather x1, waiting for transfers between devices, local(): lax.all_gather(cache_kv[1], 'ha', axis=0, tiled=True)  51.7 us
    all_gather x1, waiting for transfers between devices, local(): lax.all_gather(hyena_out, ('grp', 'pb'), axis=1, tiled=True)  40 us
    unnamed x42, local copies, waits for them, and re-layouts  16.5 us
    all_to_all x1, blocking collectives, local(): lax.all_to_all(conv_cols, 'ha', split_axis=1, concat_axis=0, tiled=True)  14.8 us
  transfers between devices with their start and end apart: 7, of which 6 were waited for; matrix products, arithmetic and copies ran while one was open for 11% of the time, Pallas kernels for 0%

commit v1 on v0

--- a/solution.py
+++ b/solution.py
@@ -92,29 +92,41 @@
     return result.reshape(chans, length)
 
 
-def absorb(carry, queries, keys_piece, values_piece, allowed):
-    top_old, total_old, accum_old = carry
-    scores = jnp.einsum(
-        "rhd,shd->hrs", queries, keys_piece, preferred_element_type=jnp.float32
-    ) / jnp.sqrt(jnp.float32(queries.shape[-1]))
-    scores = jnp.where(allowed[None], scores, jnp.float32(-1e30))
-    top_new = jnp.maximum(top_old, jnp.max(scores, axis=2))
-    factor = jnp.exp(top_old - top_new)
-    expd = jnp.where(allowed[None], jnp.exp(scores - top_new[:, :, None]), jnp.float32(0.0))
-    total_new = total_old * factor + jnp.sum(expd, axis=2)
-    accum_new = accum_old * factor[:, :, None] + jnp.einsum(
-        "hrs,shd->hrd", expd.astype(jnp.bfloat16), values_piece, preferred_element_type=jnp.float32
-    )
-    return (top_new, total_new, accum_new)
+QUADS = [[2 * k, 2 * k + 1, 8 + 2 * k, 9 + 2 * k] for k in range(4)]
+RINGS = [list(range(8)), list(range(8, 16))]
+SAME_CORE = [[8 * g + 2 * y + c for g in range(2) for y in range(4)] for c in range(2)]
+OTHER_CORE = [(j, j ^ 1) for j in range(8)]
+GP = ("grp", "pb")
+
+
+def pieces_of(values):
+    leading = values.astype(jnp.bfloat16)
+    remainder = values - lax.optimization_barrier(leading).astype(jnp.float32)
+    middle = remainder.astype(jnp.bfloat16)
+    trailing = (remainder - lax.optimization_barrier(middle).astype(jnp.float32)).astype(jnp.bfloat16)
+    return (leading, middle, trailing)
+
+
+def gather_features(block):
+    copies = jnp.broadcast_to(block[None], (8,) + block.shape)
+    own = lax.all_to_all(copies, GP, 0, 0, axis_index_groups=SAME_CORE)
+    other = lax.ppermute(own, "pb", OTHER_CORE)
+    return own, other
+
+
+def by_core(own, other):
+    flag = lax.axis_index("pb") % 2 == 0
+    first = jnp.where(flag, own, other)
+    second = jnp.where(flag, other, own)
+    both = jnp.stack([first, second], axis=1)
+    return jnp.transpose(both, (2, 0, 1, 3)).reshape(both.shape[2], -1)
 
 
 def local(hyena_proj, dskip, filters, resident, cache_kv, norm_gain, w_qkv, w_out):
     row_count = hyena_proj.shape[1]
     head_cols = w_qkv.shape[2]
-    head_size = HEAD
-    heads_here = head_cols // head_size
+    heads_here = head_cols // HEAD
     width = w_qkv.shape[0]
-    ha_count = lax.axis_size("ha")
     ha_index = lax.axis_index("ha")
     gated = (hyena_proj[1].astype(jnp.float32) * hyena_proj[2].astype(jnp.float32)).astype(
         jnp.bfloat16
@@ -134,45 +146,61 @@
         hyena_proj[0].astype(jnp.float32)
         * (conv.astype(jnp.float32) + dskip * gated.astype(jnp.float32))
     ).astype(jnp.bfloat16)
-    whole = lax.all_gather(hyena_out, ("grp", "pb"), axis=1, tiled=True).astype(jnp.float32)
+    whole = by_core(*gather_features(hyena_out)).astype(jnp.float32)
     meansq = jnp.mean(whole * whole, axis=1, keepdims=True)
     normed = (whole * lax.rsqrt(meansq + 1e-05) * norm_gain).astype(jnp.bfloat16)
     qkv = jnp.dot(normed, w_qkv.reshape(width, 3 * head_cols), preferred_element_type=jnp.float32)
-    qkv = qkv.reshape(row_count, 3, heads_here, head_size)
-    cache_rows = cache_kv.shape[1]
-    cache_len = cache_rows * ha_count
+    qkv = qkv.reshape(row_count, 3, heads_here, HEAD)
+    cache_len = 16 * row_count
     local_rows = ha_index * row_count + jnp.arange(row_count, dtype=jnp.int32)
     queries = rotate(qkv[:, 0], cache_len + local_rows).astype(jnp.bfloat16)
     keys_now = rotate(qkv[:, 1], cache_len + local_rows).astype(jnp.bfloat16)
     values_now = qkv[:, 2].astype(jnp.bfloat16)
-    start_carry = (
-        jnp.full((heads_here, row_count), -1e30, jnp.float32),
-        jnp.zeros((heads_here, row_count), jnp.float32),
-        jnp.zeros((heads_here, row_count, head_size), jnp.float32),
-    )
-    pieces = (
-        lax.all_gather(cache_kv[0], "ha", axis=0, tiled=True),
-        lax.all_gather(cache_kv[1], "ha", axis=0, tiled=True),
-    )
-    keys_piece = pieces[0].reshape(-1, heads_here, head_size)
-    values_piece = pieces[1].reshape(-1, heads_here, head_size)
-    allowed = jnp.ones((row_count, keys_piece.shape[0]), bool)
-    carry = absorb(start_carry, queries, keys_piece, values_piece, allowed)
-    pieces = (
-        lax.all_gather(keys_now, "ha", axis=0, tiled=True),
-        lax.all_gather(values_now, "ha", axis=0, tiled=True),
-    )
-    keys_piece = pieces[0]
-    values_piece = pieces[1]
-    key_rows = jnp.arange(keys_piece.shape[0], dtype=jnp.int32)
-    allowed = key_rows[None, :] <= local_rows[:, None]
-    top_fin, total_fin, accum_fin = absorb(carry, queries, keys_piece, values_piece, allowed)
-    heads_out = (accum_fin / total_fin[:, :, None]).astype(jnp.bfloat16)
-    heads_out = jnp.transpose(heads_out, (1, 0, 2)).reshape(row_count, head_cols)
+    half = ha_index // 8
+    quarter = (ha_index % 8) // 2
+    to_ring = jnp.transpose(queries, (1, 0, 2))
+    to_ring = jnp.broadcast_to(to_ring[None], (4,) + to_ring.shape).reshape(8, row_count, HEAD)
+    q_all = lax.all_to_all(to_ring, "ha", 0, 0, axis_index_groups=RINGS).reshape(8 * row_count, HEAD)
+
+    def spread(keys, values):
+        both = jnp.stack([jnp.transpose(keys, (1, 0, 2)), jnp.transpose(values, (1, 0, 2))], axis=1)
+        both = jnp.broadcast_to(both[None], (2,) + both.shape).reshape(4, 2, row_count, HEAD)
+        both = lax.all_to_all(both, "ha", 0, 0, axis_index_groups=QUADS)
+        return both[:, 0].reshape(-1, HEAD), both[:, 1].reshape(-1, HEAD)
+
+    cache = cache_kv.reshape(2, row_count, heads_here, HEAD)
+    k_old, v_old = spread(cache[0], cache[1])
+    k_new, v_new = spread(keys_now, values_now)
+    keys = jnp.concatenate([k_old, k_new])
+    values = jnp.concatenate([v_old, v_new])
+    blocks = 2 * quarter + jnp.array([0, 1, 8, 9], jnp.int32)
+    key_rows = (blocks[:, None] * row_count + jnp.arange(row_count, dtype=jnp.int32)[None]).reshape(-1)
+    key_rows = jnp.concatenate([jnp.full((4 * row_count,), -1, jnp.int32), key_rows])
+    query_rows = half * 8 * row_count + jnp.arange(8 * row_count, dtype=jnp.int32)
+    allowed = key_rows[:, None] <= query_rows[None, :]
+    scores = jnp.einsum("kd,qd->kq", keys, q_all, preferred_element_type=jnp.float32) / jnp.sqrt(
+        jnp.float32(HEAD)
+    )
+    scores = jnp.where(allowed, scores, jnp.float32(-1e30))
+    top = jnp.max(scores, axis=0)
+    expd = jnp.exp(scores - top[None])
+    total = jnp.sum(expd, axis=0)
+    partial = jnp.einsum(
+        "kd,kq->dq", values, expd.astype(jnp.bfloat16), preferred_element_type=jnp.float32
+    )
+    partial = (partial / total[None]).astype(jnp.bfloat16)
+    level = jnp.stack(pieces_of(top + jnp.log(total)))
+    sent = jnp.concatenate([partial, level, jnp.zeros((13, 8 * row_count), jnp.bfloat16)])
+    sent = jnp.transpose(sent.reshape(HEAD + 16, 8, row_count), (1, 0, 2))
+    got = lax.all_to_all(sent, "ha", 0, 0, axis_index_groups=RINGS).astype(jnp.float32)
+    got = got.reshape(4, 2, HEAD + 16, row_count)
+    level = got[:, :, HEAD] + got[:, :, HEAD + 1] + got[:, :, HEAD + 2]
+    share = jnp.exp(level - jnp.max(level, axis=0))
+    share = share / jnp.sum(share, axis=0)
+    heads_out = jnp.sum(got[:, :, :HEAD] * share[:, :, None], axis=0)
+    heads_out = heads_out.reshape(head_cols, row_count).T.astype(jnp.bfloat16)
     attended = jnp.dot(
-        lax.all_gather(heads_out, ("grp", "pb"), axis=1, tiled=True),
-        w_out,
-        preferred_element_type=jnp.float32,
+        by_core(*gather_features(heads_out)), w_out, preferred_element_type=jnp.float32
     )
     mixed = (hyena_out.astype(jnp.float32) + attended).astype(jnp.bfloat16)
     block_spectrum = jnp.stack([real_part, imag_part])

time: 472 us -> 217 us (0.46)
  waiting for transfers between devices: 353 us -> 20 us
  blocking collectives: 14.8 us -> 66.9 us
  starting transfers between devices: 10.5 us -> 32.1 us
  local copies, waits for them, and re-layouts: 24.4 us -> 42 us
  between operations: 14.6 us -> 1.42 us
  matrix products: 41.6 us -> 31.5 us
  other arithmetic: 13 us -> 21.4 us
    all_gather x6 -> x0, waiting for transfers between devices: 353 us -> none  [the longest x1 67.3 us: local(): lax.all_gather(keys_now, 'ha', axis=0, tiled=True)]
    all_to_all x0 -> x3, blocking collectives: none -> 52.1 us  [the longest x2 34 us: gather_features(): own = lax.all_to_all(copies, GP, 0, 0, axis_index_groups=SAME_CORE)]
    all_to_all x0 -> x3, waiting for transfers between devices: none -> 20 us  [the longest x1 12.6 us: local(): lax.all_to_all(to_ring, 'ha', 0, 0, axis_index_groups=RINGS)]
    all_to_all x0 -> x3, starting transfers between devices: none -> 11.3 us  [the longest x2 7.8 us: spread(): both = lax.all_to_all(both, 'ha', 0, 0, axis_index_groups=QUADS)]
    ppermute x0 -> x2, starting transfers between devices: none -> 10.8 us  [gather_features(): other = lax.ppermute(own, 'pb', OTHER_CORE)]
    dot_general x5 -> x3, matrix products: 24.9 us -> 16.1 us  [the longest x1 8.7 us: local(): jnp.einsum('kd,kq->dq', values, expd.astype(jnp.bfloat16), preferred_elem...]
    unnamed x42 -> x53, local copies, waits for them, and re-layouts: 16.5 us -> 15.8 us
  transfers between devices with their start and end apart: 7 -> 6, of which waited for: 6 -> 2; matrix products, arithmetic and copies ran while one was open for 11% -> 22% of each run, Pallas kernels for 0% -> 0%
where the time goes in v1:
time: 217 us; the launch traced here: 215 us
  blocking collectives  66.9 us (31%)
  local copies, waits for them, and re-layouts  42 us (19%)
  starting transfers between devices  32.1 us (15%)
  matrix products  31.5 us (15%)
  other arithmetic  21.4 us (10%)
  waiting for transfers between devices  20 us (9%)
    all_to_all x2, blocking collectives, gather_features(): own = lax.all_to_all(copies, GP, 0, 0, axis_index_groups=SAME_CORE)  34 us
    all_to_all x1, blocking collectives, local(): lax.all_to_all(sent, 'ha', 0, 0, axis_index_groups=RINGS)  18.1 us
    unnamed x53, local copies, waits for them, and re-layouts  15.8 us
    all_to_all x1, blocking collectives, local(): lax.all_to_all(conv_cols, 'ha', split_axis=1, concat_axis=0, tiled=True)  14.8 us
    all_to_all x1, waiting for transfers between devices, local(): lax.all_to_all(to_ring, 'ha', 0, 0, axis_index_groups=RINGS)  12.6 us
    ppermute x2, starting transfers between devices, gather_features(): other = lax.ppermute(own, 'pb', OTHER_CORE)  10.8 us
    all_to_all x1, starting transfers between devices, local(): lax.all_to_all(gated.T, 'ha', split_axis=0, concat_axis=1, tiled=True)  10 us
    dot_general x1, matrix products, local(): jnp.einsum('kd,kq->dq', values, expd.astype(jnp.bfloat16), preferred_elem...  8.7 us
  transfers between devices with their start and end apart: 6, of which 2 were waited for; matrix products, arithmetic and copies ran while one was open for 22% of the time, Pallas kernels for 0%

profile of v1, /device:TPU:1, one launch (start us, length us, event | category | flops | bytes accessed | tf_op | source)
XLA Modules:
  0.0 215.3 jit_solution(14152868166045709916)
XLA Ops:
  0.6 1.2 fusion.77
  1.8 0.8 copy.82
  2.6 10.0 %all-to-all-start = ((bf16[16,16,256]{2,1,0:T(8,128)(2,1)}), bf16[16,16,256]{2,1,0:T(8,128)(2,1)S(1)}, u32[]{:S(2)}, u32[]{:S(2)}) async-start(bf16[16,16,256]{2,1,0:T(8,128)(2,1)} %bitcast.6), calls=%async_computation | async-start | bytes 262144 | tf_op jit(solution)/shard_map/all_to_all | solution.py:134
  12.8 1.9 multiply_bitcast_fusion.3
  14.9 0.8 copy.115
  15.6 0.8 copy.116
  16.4 0.8 copy.117
  17.1 0.8 copy.118
  17.9 0.7 copy.119
  18.7 0.7 copy.120
  19.4 0.8 copy.121
  20.1 0.8 copy.122
  23.4 0.5 fusion.17
  24.0 1.4 fusion.37
  25.4 0.7 fusion.92
  26.1 0.7 fusion.84
  26.8 0.7 convolution_subtract_fusion
  27.5 0.7 convolution_add_fusion.2
  28.2 1.7 fusion.29
  30.0 1.7 fusion.16
  31.9 14.8 %all_to_all.56 = bf16[16,16,256]{2,0,1:T(8,128)(2,1)S(1)} all-to-all(bf16[16,16,256]{2,0,1:T(8,128)(2,1)S(1)} %copy.87), channel_id=1, replica_groups=mesh['grp'=2,'pb'=8,'ha'=16] {'ha'}, dimensions={1} | all-to-all | bytes 262144 | tf_op jit(solution)/shard_map/all_to_all | solution.py:144
  47.1 19.4 %all_to_all.57 = bf16[8,256,256]{2,1,0:T(8,128)(2,1)S(1)} all-to-all(bf16[8,256,256]{2,1,0:T(8,128)(2,1)S(1)} %broadcast_in_dim.26), channel_id=1, replica_groups={{0,32,64,96,128,160,192,224},{16,48,80,112,144,176,208,240},{1,33,65,97..., dimensions={0} | all-to-all | bytes 2097152 | tf_op jit(solution)/shard_map/all_to_all | solution.py:112
  66.5 4.8 %collective-permute-start = (bf16[8,256,256]{2,1,0:T(8,128)(2,1)S(1)}, bf16[8,256,256]{2,1,0:T(8,128)(2,1)}, u32[]{:S(2)}, u32[]{:S(2)}) collective-permute-start(bf16[8,256,256]{2,1,0:T(8,128)(2,1)S(1)} %all_to_all.57), channel_id=1, source_target_pairs={{0,16},{16,0},{32,48},{48,32},{64,80},{80,64},{96,112},{112,96},{1... | collective-permute-start | bytes 3145736 | tf_op jit(solution)/shard_map/ppermute | solution.py:113
  71.3 1.7 fusion.169
  73.0 1.6 squeeze.14
  74.6 1.6 squeeze.15
  76.2 1.4 pad_maximum_fusion.2
  77.6 0.9 broadcast_in_dim.25
  78.5 4.3 %all-to-all-start.2 = ((bf16[4,2,256,128]{3,2,1,0:T(8,128)(2,1)}), bf16[4,2,256,128]{3,2,1,0:T(8,128)(2,1)}, u32[]{:S(2)}, u32[]{:S(2)}) async-start(bf16[4,2,256,128]{3,2,1,0:T(8,128)(2,1)} %bitcast.248), calls=%async_computation.2 | async-start | bytes 1048576 | tf_op jit(solution)/shard_map/all_to_all | solution.py:168
  82.8 0.6 mul.476
  83.5 0.7 copy.90
  84.2 8.7 %copy.92 = bf16[4096,3,256]{0,2,1:T(8,128)(2,1)} copy(bf16[4096,3,256]{2,0,1:T(8,128)(2,1)} %param.15) | data formatting | bytes 12582912 | tf_op args[6]
  92.9 0.9 multiply_cosine_fusion
  93.8 1.4 select_bitcast_fusion.3
  95.2 0.5 fusion.5
  95.7 2.0 fusion.8
  97.7 4.0 %copy.91 = bf16[256,8,2,256]{0,3,2,1:T(8,128)(2,1)} copy(bf16[256,8,2,256]{3,0,1,2:T(8,128)(2,1)} %fusion.8) | data formatting | bytes 4194304 | tf_op jit(solution)/shard_map/convert_element_type | solution.py:151
  101.7 5.2 %fusion.170 = f32[256,3,2,128]{0,3,2,1:T(8,128)S(1)} fusion(bf16[256,4096,1,1]{0,1,3,2:T(8,128)(2,1)} %bitcast.246, bf16[3,2,128,4096]{3,2,1,0:T(8,128)(2,1)} %bitcast.243), kind=kOutput, calls=%fused_computation.251 | convolution fusion | flops 1610612736 | bytes 9175040 | tf_op jit(solution)/shard_map/dot_general | solution.py:152
  107.4 0.9 broadcast_in_dim.27
  108.3 3.5 %all-to-all-start.4 = ((bf16[4,2,256,128]{3,2,1,0:T(8,128)(2,1)}), bf16[4,2,256,128]{3,2,1,0:T(8,128)(2,1)S(1)}, u32[]{:S(2)}, u32[]{:S(2)}) async-start(bf16[4,2,256,128]{3,2,1,0:T(8,128)(2,1)} %bitcast.42), calls=%async_computation.4 | async-start | bytes 1048576 | tf_op jit(solution)/shard_map/all_to_all | solution.py:168
  111.9 7.4 %all-to-all-done.4 = bf16[4,2,256,128]{3,2,1,0:T(8,128)(2,1)S(1)} async-done(((bf16[4,2,256,128]{3,2,1,0:T(8,128)(2,1)}), bf16[4,2,256,128]{3,2,1,0:T(8,128)(2,1)S(1)}, u32[]{:S(2)}, u32[]{:S(2)}) %all-to-all-start.4) | async-done | bytes 524320 | tf_op jit(solution)/shard_map/all_to_all | solution.py:168
  119.3 0.9 broadcast_in_dim.28
  120.2 3.5 %all-to-all-start.5 = ((bf16[8,256,128]{2,1,0:T(8,128)(2,1)}), bf16[8,256,128]{2,1,0:T(8,128)(2,1)S(1)}, u32[]{:S(2)}, u32[]{:S(2)}) async-start(bf16[8,256,128]{2,1,0:T(8,128)(2,1)} %bitcast.48), calls=%async_computation.5 | async-start | bytes 1048576 | tf_op jit(solution)/shard_map/all_to_all | solution.py:163
  123.8 0.6 iota_add_fusion
  124.4 1.9 fusion.167
  126.2 0.8 fusion.168
  127.1 12.6 %all-to-all-done.5 = bf16[8,256,128]{2,1,0:T(8,128)(2,1)S(1)} async-done(((bf16[8,256,128]{2,1,0:T(8,128)(2,1)}), bf16[8,256,128]{2,1,0:T(8,128)(2,1)S(1)}, u32[]{:S(2)}, u32[]{:S(2)}) %all-to-all-start.5) | async-done | bytes 524320 | tf_op jit(solution)/shard_map/all_to_all | solution.py:163
  139.7 4.4 %fusion.2 = (f32[2048]{0:T(1024)S(1)}, f32[2048,2048]{1,0:T(8,128)S(1)}) fusion(s32[2048]{0:T(1024)} %iota_add_fusion, s32[2048]{0:T(1024)S(1)} %concatenate.33, bf16[2048,128]{1,0:T(8,128)(2,1)S(1)} %bitcast.250, bf16[1024,128]{1,0:T(8,128)(2,1)} %bitcast.259, bf16[1024,128]{1,0:T(8,128)(2,1)} %bitcast.258), kind=kOutput, calls=%fused_computation.4 | convolution fusion | flops 1091565568 | bytes 17850368 | tf_op jit(solution)/shard_map/kd,qd->kq/dot_general | solution.py:181
  144.1 4.8 %fusion = f32[2048]{0:T(1024)S(1)} fusion(f32[2048,2048]{1,0:T(8,128)S(1)} %get-tuple-element.38, f32[2048]{0:T(1024)S(1)} %get-tuple-element.37, s32[2048]{0:T(1024)S(1)} %copy-done.15, s32[2048]{0:T(1024)S(1)} %concatenate.33), kind=kLoop, calls=%fused_computation.2 | loop fusion | flops 20969472 | bytes 16809984 | tf_op jit(solution)/shard_map/reduce_sum | solution.py:187
  149.0 0.9 copy-done.1
  150.0 8.7 %fusion.12 = bf16[128,2048]{1,0:T(8,128)(2,1)S(1)} fusion(f32[2048,2048]{1,0:T(8,128)} %copy-done.1, f32[2048]{0:T(1024)S(1)} %get-tuple-element.37, s32[2048]{0:T(1024)S(1)} %copy-done.16, s32[2048]{0:T(1024)S(1)} %concatenate.33, bf16[1024,128]{1,0:T(8,128)(2,1)S(1)} %bitcast.257, bf16[1024,128]{1,0:T(8,128)(2,1)S(1)} %bitcast.256, f32[2048]{0:T(1024)S(1)} %fusion), kind=kOutput, calls=%fused_computation.15 | convolution fusion | flops 1096286208 | bytes 17858560 | tf_op jit(solution)/shard_map/kd,kq->dq/dot_general | solution.py:188
  158.7 0.8 copy.130
  159.5 2.2 %concatenate.39 = bf16[144,8,256]{2,0,1:T(8,128)(2,1)S(1)} concatenate(bf16[128,8,256]{2,0,1:T(8,128)(2,1)} %bitcast.245, bf16[1,8,256]{2,0,1:T(2,128)(2,1)S(1)} %convert_element_type.241, bf16[1,8,256]{2,0,1:T(2,128)(2,1)S(1)} %concatenate.40, bf16[1,8,256]{2,0,1:T(2,128)(2,1)S(1)} %concatenate.41, bf16[13,8,256]{2,0,1:T(8,128)(2,1)S(1)} %broadcast_in_dim.30), dimensions={0} | concatenate | bytes 1179648 | tf_op jit(solution)/shard_map/concatenate | solution.py:193
  161.7 18.1 %all_to_all.58 = bf16[8,144,256]{2,1,0:T(8,128)(2,1)S(1)} all-to-all(bf16[8,144,256]{2,1,0:T(8,128)(2,1)S(1)} %bitcast.244), channel_id=1, replica_groups={{0,1,2,3,4,5,6,7},{8,9,10,11,12,13,14,15},{16,17,18,19,20,21,22,23},{24..., dimensions={0} | all-to-all | bytes 1179648 | tf_op jit(solution)/shard_map/all_to_all | solution.py:195
  180.1 1.2 fusion.20
  181.5 14.6 %all_to_all.59 = bf16[8,256,256]{2,1,0:T(8,128)(2,1)S(1)} all-to-all(bf16[8,256,256]{2,1,0:T(8,128)(2,1)S(1)} %broadcast_in_dim.31), channel_id=1, replica_groups={{0,32,64,96,128,160,192,224},{16,48,80,112,144,176,208,240},{1,33,65,97..., dimensions={0} | all-to-all | bytes 2097152 | tf_op jit(solution)/shard_map/all_to_all | solution.py:112
  196.0 6.0 %collective-permute-start.1 = (bf16[8,256,256]{2,1,0:T(8,128)(2,1)S(1)}, bf16[8,256,256]{2,1,0:T(8,128)(2,1)}, u32[]{:S(2)}, u32[]{:S(2)}) collective-permute-start(bf16[8,256,256]{2,1,0:T(8,128)(2,1)S(1)} %all_to_all.59), channel_id=1, source_target_pairs={{0,16},{16,0},{32,48},{48,32},{64,80},{80,64},{96,112},{112,96},{1... | collective-permute-start | bytes 3145736 | tf_op jit(solution)/shard_map/ppermute | solution.py:113
  202.0 0.8 stack_reshape.7
  202.8 1.0 stack_reshape.6
  203.8 1.8 pad_maximum_fusion.1
  205.5 1.4 select_bitcast_fusion.1
  206.9 1.5 maximum_bitcast_fusion
  208.4 3.9 %copy.103 = bf16[256,8,2,256]{0,3,2,1:T(8,128)(2,1)} copy(bf16[256,8,2,256]{3,0,1,2:T(8,128)(2,1)} %maximum_bitcast_fusion) | data formatting | bytes 4194304 | tf_op jit(solution)/shard_map/transpose | solution.py:122
  212.3 3.0 %fusion.19 = bf16[256,256]{1,0:T(8,128)(2,1)} fusion(bf16[256,4096]{0,1:T(8,128)(2,1)} %bitcast.247, bf16[4096,256]{1,0:T(8,128)(2,1)S(1)} %copy-done, bf16[256,256]{1,0:T(8,128)(2,1)S(1)} %fusion.41), kind=kOutput, calls=%fused_computation.28 | convolution fusion | flops 537067520 | bytes 4456448 | tf_op jit(solution)/shard_map/dot_general | solution.py:202
  (95 shorter events, 4.4 us)
Async XLA Ops:
  0.6 211.7 %copy-start = (bf16[4096,256]{1,0:T(8,128)(2,1)S(1)}, bf16[4096,256]{1,0:T(8,128)(2,1)}, u32[]{:S(2)}) copy-start(bf16[4096,256]{1,0:T(8,128)(2,1)} %param.16) | copy-start | bytes 6291460
  2.6 18.5 %all-to-all-start = ((bf16[16,16,256]{2,1,0:T(8,128)(2,1)}), bf16[16,16,256]{2,1,0:T(8,128)(2,1)S(1)}, u32[]{:S(2)}, u32[]{:S(2)}) async-start(bf16[16,16,256]{2,1,0:T(8,128)(2,1)} %bitcast.6), calls=%async_computation | async-start | bytes 262144 | tf_op jit(solution)/shard_map/all_to_all | solution.py:134
  21.3 2.6 %copy-start.3 = (f32[2,8,32,128]{3,2,1,0:T(8,128)S(1)}, f32[2,8,32,128]{3,2,1,0:T(8,128)}, u32[]{:S(2)}) copy-start(f32[2,8,32,128]{3,2,1,0:T(8,128)} %copy.115) | copy-start | bytes 786436
  21.3 2.6 %copy-start.4 = (f32[2,8,32,128]{3,2,1,0:T(8,128)S(1)}, f32[2,8,32,128]{3,2,1,0:T(8,128)}, u32[]{:S(2)}) copy-start(f32[2,8,32,128]{3,2,1,0:T(8,128)} %copy.116) | copy-start | bytes 786436
  21.3 2.6 %copy-start.5 = (f32[2,8,32,128]{3,2,1,0:T(8,128)S(1)}, f32[2,8,32,128]{3,2,1,0:T(8,128)}, u32[]{:S(2)}) copy-start(f32[2,8,32,128]{3,2,1,0:T(8,128)} %copy.117) | copy-start | bytes 786436
  21.3 2.6 %copy-start.6 = (f32[2,8,32,128]{3,2,1,0:T(8,128)S(1)}, f32[2,8,32,128]{3,2,1,0:T(8,128)}, u32[]{:S(2)}) copy-start(f32[2,8,32,128]{3,2,1,0:T(8,128)} %copy.118) | copy-start | bytes 786436
  21.3 2.6 %copy-start.7 = (f32[2,8,32,128]{3,2,1,0:T(8,128)S(1)}, f32[2,8,32,128]{3,2,1,0:T(8,128)}, u32[]{:S(2)}) copy-start(f32[2,8,32,128]{3,2,1,0:T(8,128)} %copy.119) | copy-start | bytes 786436
  21.3 2.6 %copy-start.8 = (f32[2,8,32,128]{3,2,1,0:T(8,128)S(1)}, f32[2,8,32,128]{3,2,1,0:T(8,128)}, u32[]{:S(2)}) copy-start(f32[2,8,32,128]{3,2,1,0:T(8,128)} %copy.120) | copy-start | bytes 786436
  21.3 2.6 %copy-start.9 = (f32[2,8,32,128]{3,2,1,0:T(8,128)S(1)}, f32[2,8,32,128]{3,2,1,0:T(8,128)}, u32[]{:S(2)}) copy-start(f32[2,8,32,128]{3,2,1,0:T(8,128)} %copy.121) | copy-start | bytes 786436
  21.4 2.6 %copy-start.10 = (f32[2,8,32,128]{3,2,1,0:T(8,128)S(1)}, f32[2,8,32,128]{3,2,1,0:T(8,128)}, u32[]{:S(2)}) copy-start(f32[2,8,32,128]{3,2,1,0:T(8,128)} %copy.122) | copy-start | bytes 786436
  26.8 20.1 %copy-start.2 = (bf16[3,256,256]{2,1,0:T(8,128)(2,1)S(1)}, bf16[3,256,256]{2,1,0:T(8,128)(2,1)}, u32[]{:S(2)}) copy-start(bf16[3,256,256]{2,1,0:T(8,128)(2,1)} %param.9) | copy-start | bytes 1179652
  26.8 20.1 %copy-start.18 = (f32[256]{0:T(256)S(1)}, f32[256]{0:T(256)}, u32[]{:S(2)}) copy-start(f32[256]{0:T(256)} %param.10) | copy-start | bytes 3076
  46.8 36.1 %copy-start.17 = (f32[4096]{0:T(1024)S(1)}, f32[4096]{0:T(1024)}, u32[]{:S(2)}) copy-start(f32[4096]{0:T(1024)} %param.14) | copy-start | bytes 49156
  66.5 27.3 %collective-permute-start = (bf16[8,256,256]{2,1,0:T(8,128)(2,1)S(1)}, bf16[8,256,256]{2,1,0:T(8,128)(2,1)}, u32[]{:S(2)}, u32[]{:S(2)}) collective-permute-start(bf16[8,256,256]{2,1,0:T(8,128)(2,1)S(1)} %all_to_all.57), channel_id=1, source_target_pairs={{0,16},{16,0},{32,48},{48,32},{64,80},{80,64},{96,112},{112,96},{1... | collective-permute-start | bytes 3145736 | tf_op jit(solution)/shard_map/ppermute | solution.py:113
  78.5 28.9 %all-to-all-start.2 = ((bf16[4,2,256,128]{3,2,1,0:T(8,128)(2,1)}), bf16[4,2,256,128]{3,2,1,0:T(8,128)(2,1)}, u32[]{:S(2)}, u32[]{:S(2)}) async-start(bf16[4,2,256,128]{3,2,1,0:T(8,128)(2,1)} %bitcast.248), calls=%async_computation.2 | async-start | bytes 1048576 | tf_op jit(solution)/shard_map/all_to_all | solution.py:168
  101.7 5.3 %copy-start.11 = (f32[256,64]{0,1:T(8,128)S(1)}, f32[256,64]{0,1:T(8,128)}, u32[]{:S(2)}) copy-start(f32[256,64]{0,1:T(8,128)} %get-tuple-element.34) | copy-start | bytes 196612
  101.7 5.3 %copy-start.12 = (f32[256,64]{0,1:T(8,128)S(1)}, f32[256,64]{0,1:T(8,128)}, u32[]{:S(2)}) copy-start(f32[256,64]{0,1:T(8,128)} %get-tuple-element.35) | copy-start | bytes 196612
  107.0 16.7 %copy-start.19 = (s32[4]{0:T(128)S(1)}, s32[4]{0:T(128)}, u32[]{:S(2)}) copy-start(s32[4]{0:T(128)} %constant.161.clone) | copy-start | bytes 52
  108.3 11.1 %all-to-all-start.4 = ((bf16[4,2,256,128]{3,2,1,0:T(8,128)(2,1)}), bf16[4,2,256,128]{3,2,1,0:T(8,128)(2,1)S(1)}, u32[]{:S(2)}, u32[]{:S(2)}) async-start(bf16[4,2,256,128]{3,2,1,0:T(8,128)(2,1)} %bitcast.42), calls=%async_computation.4 | async-start | bytes 1048576 | tf_op jit(solution)/shard_map/all_to_all | solution.py:168
  120.2 19.5 %all-to-all-start.5 = ((bf16[8,256,128]{2,1,0:T(8,128)(2,1)}), bf16[8,256,128]{2,1,0:T(8,128)(2,1)S(1)}, u32[]{:S(2)}, u32[]{:S(2)}) async-start(bf16[8,256,128]{2,1,0:T(8,128)(2,1)} %bitcast.48), calls=%async_computation.5 | async-start | bytes 1048576 | tf_op jit(solution)/shard_map/all_to_all | solution.py:163
  139.7 4.4 %copy-start.15 = (s32[2048]{0:T(1024)S(1)}, s32[2048]{0:T(1024)}, u32[]{:S(2)}) copy-start(s32[2048]{0:T(1024)} %iota_add_fusion) | copy-start | bytes 24580
  144.1 5.8 %copy-start.1 = (f32[2048,2048]{1,0:T(8,128)}, f32[2048,2048]{1,0:T(8,128)S(1)}, u32[]{:S(2)}) copy-start(f32[2048,2048]{1,0:T(8,128)S(1)} %get-tuple-element.38) | copy-start | bytes 50331652
  144.1 5.8 %copy-start.13 = (bf16[4,1,256,128]{3,2,1,0:T(8,128)(2,1)S(1)}, bf16[4,1,256,128]{3,2,1,0:T(8,128)(2,1)}, u32[]{:S(2)}) copy-start(bf16[4,1,256,128]{3,2,1,0:T(8,128)(2,1)} %get-tuple-element.22) | copy-start | bytes 786436
  144.1 5.8 %copy-start.14 = (bf16[4,1,256,128]{3,2,1,0:T(8,128)(2,1)S(1)}, bf16[4,1,256,128]{3,2,1,0:T(8,128)(2,1)}, u32[]{:S(2)}) copy-start(bf16[4,1,256,128]{3,2,1,0:T(8,128)(2,1)} %get-tuple-element.24) | copy-start | bytes 786436
  144.1 5.8 %copy-start.16 = (s32[2048]{0:T(1024)S(1)}, s32[2048]{0:T(1024)}, u32[]{:S(2)}) copy-start(s32[2048]{0:T(1024)} %iota_add_fusion) | copy-start | bytes 24580
  196.0 9.5 %collective-permute-start.1 = (bf16[8,256,256]{2,1,0:T(8,128)(2,1)S(1)}, bf16[8,256,256]{2,1,0:T(8,128)(2,1)}, u32[]{:S(2)}, u32[]{:S(2)}) collective-permute-start(bf16[8,256,256]{2,1,0:T(8,128)(2,1)S(1)} %all_to_all.59), channel_id=1, source_target_pairs={{0,16},{16,0},{32,48},{48,32},{64,80},{80,64},{96,112},{112,96},{1... | collective-permute-start | bytes 3145736 | tf_op jit(solution)/shard_map/ppermute | solution.py:113

commit v2 on v0

v2 whole, which is shorter than its diff:
```python
import functools
import math

import jax
import jax.numpy as jnp
import ml_dtypes
import numpy as np
from jax import lax
from jax.experimental import pallas as pl
from jax.experimental.pallas import tpu as pltpu
from jax.sharding import PartitionSpec as P

HEAD = 128
BF = jnp.bfloat16
F32 = jnp.float32
GP = ("grp", "pb")
QUADS = [[2 * k, 2 * k + 1, 8 + 2 * k, 9 + 2 * k] for k in range(4)]
RINGS = [list(range(8)), list(range(8, 16))]
SAME_CORE = [[8 * g + 2 * y + c for g in range(2) for y in range(4)] for c in range(2)]
OTHER_CORE = [(j, j ^ 1) for j in range(8)]
SMEM = pl.BlockSpec(memory_space=pltpu.SMEM)


def params(mib):
    return pltpu.CompilerParams(vmem_limit_bytes=mib * 2**20)


def pair(table):
    high = table.astype(ml_dtypes.bfloat16)
    low = (table - high.astype(np.float64)).astype(ml_dtypes.bfloat16)
    return high, low


@functools.cache
def tables():
    s, k1, t = np.arange(16), np.arange(32), np.arange(256)
    eye = np.eye(16)
    angle = 2 * np.pi / 32 * (np.outer(k1, s) % 32)
    first = np.stack([np.cos(angle), -np.sin(angle)])
    first = np.einsum("rks,cd->rcksd", first, eye).reshape(1024, 256)
    angle = 2 * np.pi / 8192 * np.outer(k1, t)
    turn = np.stack([np.cos(angle), np.sin(angle)]).astype(np.float32)
    k2 = (4 * np.arange(32)[None, :] + np.arange(4)[:, None]).reshape(-1)
    angle = 2 * np.pi / 256 * (np.outer(t, k2) % 256)
    cos, sin = np.cos(angle), np.sin(angle)
    second = np.block([[cos, -sin], [sin, cos]])
    return (
        np.stack(pair(first)),
        np.stack(pair(second)),
        np.stack(pair(second.T.copy())),
        np.stack(pair(first.T.copy() / 4096.0)),
        turn,
    )


def split(values):
    high = values.astype(BF)
    return high, (values - high.astype(F32)).astype(BF)


def mul(a, b):
    return jnp.dot(a, b, preferred_element_type=F32)


def gate_kernel(proj_ref, out_ref):
    gated = (proj_ref[1].astype(F32) * proj_ref[2].astype(F32)).astype(BF).astype(F32)
    out_ref[...] = gated.T.astype(BF)


def to_tiles(nat):
    out = []
    cube = nat.reshape(16, 32, 128)
    for g in range(4):
        tile = cube[4 * g : 4 * g + 4].reshape(128, 128).T
        for c in range(4):
            out.append(
                jnp.concatenate(
                    [tile[32 * q : 32 * q + 32, 32 * c : 32 * c + 32] for q in range(4)], axis=1
                )
            )
    return jnp.concatenate(out, axis=0)


def from_tiles(tiles):
    out = []
    for g in range(4):
        part = tiles[128 * g : 128 * g + 128]
        swapped = jnp.concatenate(
            [
                jnp.concatenate(
                    [part[32 * c : 32 * c + 32, 32 * q : 32 * q + 32] for c in range(4)], axis=1
                )
                for q in range(4)
            ],
            axis=0,
        )
        out.append(swapped.T.reshape(4, 32, 128))
    return jnp.concatenate(out, axis=0).reshape(16, 4096)


def prepare_kernel(filters_ref, resident_ref, out_ref):
    lane = lax.broadcasted_iota(jnp.int32, (512, 128), 1)
    row = lax.broadcasted_iota(jnp.int32, (512, 128), 0)
    weight = jnp.where((lane == 0) & (row % 32 == 0), 0.5, 1.0)
    real = jnp.zeros((16, 4096), F32)
    imag = jnp.zeros((16, 4096), F32)
    for m in range(2):
        ar, ai = resident_ref[m, 0], resident_ref[m, 1]
        br, bi = filters_ref[m + 1, 0], filters_ref[m + 1, 1]
        real = real + ar * br - ai * bi
        imag = imag + ar * bi + ai * br
    out_ref[0] = to_tiles(filters_ref[0, 0]) * weight
    out_ref[1] = to_tiles(filters_ref[0, 1]) * weight
    out_ref[2] = to_tiles(real) * weight
    out_ref[3] = to_tiles(imag) * weight


def restore_kernel(tiles_ref, out_ref):
    out_ref[0] = from_tiles(tiles_ref[0])
    out_ref[1] = from_tiles(tiles_ref[1])


def conv_kernel(x_ref, prep_ref, first_ref, second_ref, third_ref, fourth_ref, turn_ref, conv_ref, spec_ref):
    x = x_ref[...]
    part = mul(first_ref[0], x) + mul(first_ref[1], x)
    cos, sin = turn_ref[0], turn_ref[1]
    real = part[:512].reshape(16, 32, 256)
    imag = part[512:].reshape(16, 32, 256)
    turned = jnp.concatenate(
        [(real * cos + imag * sin).reshape(512, 256), (imag * cos - real * sin).reshape(512, 256)], axis=1
    )
    high, low = split(turned)
    spec = mul(high, second_ref[0]) + mul(low, second_ref[0]) + mul(high, second_ref[1])
    real, imag = spec[:, :128], spec[:, 128:]
    spec_ref[0] = real
    spec_ref[1] = imag
    z = jnp.concatenate(
        [
            real * prep_ref[0] - imag * prep_ref[1] + prep_ref[2],
            real * prep_ref[1] + imag * prep_ref[0] + prep_ref[3],
        ],
        axis=1,
    )
    high, low = split(z)
    back = mul(high, third_ref[0]) + mul(low, third_ref[0]) + mul(high, third_ref[1])
    real = back[:, :256].reshape(16, 32, 256)
    imag = back[:, 256:].reshape(16, 32, 256)
    turned = jnp.concatenate(
        [(real * cos - imag * sin).reshape(512, 256), (real * sin + imag * cos).reshape(512, 256)], axis=0
    )
    high, low = split(turned)
    conv = mul(fourth_ref[0], high) + mul(fourth_ref[0], low) + mul(fourth_ref[1], high)
    conv_ref[...] = conv.astype(BF)


def hyena_kernel(conv_ref, proj_ref, dskip_ref, out_ref):
    conv = conv_ref[...].astype(F32).T
    gated = (proj_ref[1].astype(F32) * proj_ref[2].astype(F32)).astype(BF).astype(F32)
    value = (proj_ref[0].astype(F32) * (conv + dskip_ref[...] * gated)).astype(BF)
    for copy in range(8):
        out_ref[copy] = value


def qkv_kernel(core_ref, own_ref, other_ref, w_ref, gain_ref, turn_ref, q_ref, kv_ref, acc_ref, square_ref):
    step = pl.program_id(0)
    core = core_ref[0]

    @pl.when(step == 0)
    def _():
        acc_ref[...] = jnp.zeros_like(acc_ref)
        square_ref[...] = jnp.zeros_like(square_ref)

    for x_ref, which in ((own_ref, core), (other_ref, 1 - core)):
        x = x_ref[0].astype(F32)
        square_ref[...] += jnp.sum(x * x, axis=1, keepdims=True)
        scaled = (x * gain_ref[0, which]).astype(BF)
        for part in range(3):
            acc_ref[part] += mul(scaled, w_ref[part, 0, which])

    @pl.when(step == 7)
    def _():
        scale = lax.rsqrt(square_ref[...] / 4096.0 + 1e-05)
        cos, sin = turn_ref[0], turn_ref[1]
        for h in range(2):
            cols = slice(128 * h, 128 * h + 128)
            q = acc_ref[0, :, cols] * scale
            k = acc_ref[1, :, cols] * scale
            v = (acc_ref[2, :, cols] * scale).astype(BF)
            q = (q * cos + pltpu.roll(q, 64, 1) * sin).astype(BF)
            k = (k * cos + pltpu.roll(k, 64, 1) * sin).astype(BF)
            for dest in range(4):
                q_ref[2 * dest + h] = q
            for dest in range(2):
                kv_ref[2 * dest + h, 0] = k
                kv_ref[2 * dest + h, 1] = v


def attend_kernel(place_ref, q_ref, old_ref, new_ref, out_ref, keys_ref, values_ref):
    half, quarter = place_ref[0], place_ref[1]
    for b in range(4):
        rows = slice(256 * b, 256 * b + 256)
        later = slice(1024 + 256 * b, 1280 + 256 * b)
        keys_ref[rows] = old_ref[b, 0]
        keys_ref[later] = new_ref[b, 0]
        values_ref[:, rows] = old_ref[b, 1].astype(F32).T.astype(BF)
        values_ref[:, later] = new_ref[b, 1].astype(F32).T.astype(BF)
    unit = math.log2(math.e) / math.sqrt(HEAD)
    sub = lax.broadcasted_iota(jnp.int32, (256, 256), 0)
    lane = lax.broadcasted_iota(jnp.int32, (256, 256), 1)
    row16 = lax.broadcasted_iota(jnp.int32, (16, 256), 0)

    def tile(i, used):
        q = q_ref[i]
        count = 1024 + 256 * used
        scores = lax.dot_general(
            keys_ref[:count], q, (((1,), (1,)), ((), ())), preferred_element_type=F32
        )
        if used:
            block = 2 * quarter + (0, 1, 8, 9)[used - 1]
            ahead = (block - (8 * half + i)) * 256
            last = jnp.where(sub + ahead <= lane, scores[count - 256 :], -1e30)
            scores = jnp.concatenate([scores[: count - 256], last], axis=0)
        top = jnp.max(scores, axis=0, keepdims=True)
        expd = jnp.exp2((scores - top) * unit)
        total = jnp.sum(expd, axis=0, keepdims=True)
        part = mul(values_ref[:, :count], expd.astype(BF))
        out_ref[i, :128] = (part / total).astype(BF)
        level = top * unit + jnp.log2(total)
        a = level.astype(BF).astype(F32)
        b = (level - a).astype(BF).astype(F32)
        c = (level - a - b).astype(BF).astype(F32)
        rows = jnp.where(row16 == 0, a, jnp.where(row16 == 1, b, jnp.where(row16 == 2, c, 0.0)))
        out_ref[i, 128:] = rows.astype(BF)

    def body(i, carry):
        mine = 8 * half + i
        used = sum(jnp.where(2 * quarter + off <= mine, 1, 0) for off in (0, 1, 8, 9))
        for n in range(5):
            pl.when(used == n)(functools.partial(tile, i, n))
        return carry

    lax.fori_loop(0, 8, body, 0)


def combine_kernel(got_ref, out_ref):
    outs = []
    for h in range(2):
        levels = [
            jnp.sum(got_ref[2 * k + h, 128:].astype(F32), axis=0, keepdims=True) for k in range(4)
        ]
        top = jnp.maximum(jnp.maximum(levels[0], levels[1]), jnp.maximum(levels[2], levels[3]))
        shares = [jnp.exp2(level - top) for level in levels]
        total = shares[0] + shares[1] + shares[2] + shares[3]
        acc = jnp.zeros((128, 256), F32)
        for k in range(4):
            acc = acc + got_ref[2 * k + h, :128].astype(F32) * (shares[k] / total)
        outs.append(acc.T)
    value = jnp.concatenate(outs, axis=1).astype(BF)
    for copy in range(8):
        out_ref[copy] = value


def output_kernel(core_ref, own_ref, other_ref, w_ref, hyena_ref, out_ref, acc_ref):
    step = pl.program_id(0)
    core = core_ref[0]

    @pl.when(step == 0)
    def _():
        acc_ref[...] = hyena_ref[...].astype(F32)

    acc_ref[...] += mul(own_ref[0], w_ref[0, core]) + mul(other_ref[0], w_ref[0, 1 - core])

    @pl.when(step == 7)
    def _():
        out_ref[...] = acc_ref[...].astype(BF)


def shape(*dims, dtype=BF):
    return jax.ShapeDtypeStruct(dims, dtype)


def gather_features(copies):
    own = lax.all_to_all(copies, GP, 0, 0, axis_index_groups=SAME_CORE)
    return own, lax.ppermute(own, "pb", OTHER_CORE)


def rotation(rows, ha_index):
    freqs = 10000.0 ** (-jnp.arange(64, dtype=F32) / 64)
    places = 16 * rows + ha_index * rows + jnp.arange(rows, dtype=jnp.int32)
    angles = places.astype(F32)[:, None] * freqs[None, :]
    cos, sin = jnp.cos(angles), jnp.sin(angles)
    return jnp.stack([jnp.concatenate([cos, cos], 1), jnp.concatenate([-sin, sin], 1)])


def local(hyena_proj, dskip, filters, resident, cache_kv, norm_gain, w_qkv, w_out):
    ha_index = lax.axis_index("ha")
    core = (lax.axis_index("pb") % 2).astype(jnp.int32).reshape(1)
    place = jnp.stack([ha_index // 8, (ha_index % 8) // 2]).astype(jnp.int32)

    gated_t = pl.pallas_call(gate_kernel, out_shape=shape(256, 256), name="gate")(hyena_proj)
    columns = lax.all_to_all(gated_t.reshape(16, 16, 256), "ha", 0, 0).reshape(256, 256)
    prep = pl.pallas_call(
        prepare_kernel, out_shape=shape(4, 512, 128, dtype=F32), name="prepare", compiler_params=params(24)
    )(filters, resident)
    conv, tiles = pl.pallas_call(
        conv_kernel,
        out_shape=(shape(256, 256), shape(2, 512, 128, dtype=F32)),
        name="convolve",
        compiler_params=params(32),
    )(columns, prep, *(jnp.asarray(t) for t in tables()))
    conv = lax.all_to_all(conv.reshape(16, 16, 256), "ha", 0, 0).reshape(256, 256)
    block_spectrum = pl.pallas_call(
        restore_kernel, out_shape=shape(2, 16, 4096, dtype=F32), name="restore", compiler_params=params(24)
    )(tiles)
    copies = pl.pallas_call(hyena_kernel, out_shape=shape(8, 256, 256), name="hyena")(
        conv, hyena_proj, dskip.reshape(1, 256)
    )
    own, other = gather_features(copies)

    block = pl.BlockSpec((1, 256, 256), lambda s: (s, 0, 0))
    q_msg, kv_msg = pl.pallas_call(
        qkv_kernel,
        grid=(8,),
        in_specs=[
            SMEM,
            block,
            block,
            pl.BlockSpec((3, 1, 2, 256, 256), lambda s: (0, s, 0, 0, 0)),
            pl.BlockSpec((1, 2, 1, 256), lambda s: (s, 0, 0, 0)),
            pl.BlockSpec((2, 256, 128), lambda s: (0, 0, 0)),
        ],
        out_specs=[
            pl.BlockSpec((8, 256, 128), lambda s: (0, 0, 0)),
            pl.BlockSpec((4, 2, 256, 128), lambda s: (0, 0, 0, 0)),
        ],
        out_shape=(shape(8, 256, 128), shape(4, 2, 256, 128)),
        scratch_shapes=[pltpu.VMEM((3, 256, 256), F32), pltpu.VMEM((256, 1), F32)],
        name="project",
        compiler_params=params(24),
    )(
        core,
        own,
        other,
        jnp.transpose(w_qkv, (1, 0, 2)).reshape(3, 8, 2, 256, 256),
        norm_gain.reshape(8, 2, 1, 256),
        rotation(256, ha_index),
    )

    cache = jnp.transpose(cache_kv.reshape(2, 256, 2, 128), (2, 0, 1, 3))
    cache = jnp.broadcast_to(cache[None], (2, 2, 2, 256, 128)).reshape(4, 2, 256, 128)
    old = lax.all_to_all(cache, "ha", 0, 0, axis_index_groups=QUADS)
    queries = lax.all_to_all(q_msg, "ha", 0, 0, axis_index_groups=RINGS)
    new = lax.all_to_all(kv_msg, "ha", 0, 0, axis_index_groups=QUADS)
    partial = pl.pallas_call(
        attend_kernel,
        in_specs=[SMEM] + [pl.BlockSpec()] * 3,
        out_shape=shape(8, 144, 256),
        scratch_shapes=[pltpu.VMEM((2048, 128), BF), pltpu.VMEM((128, 2048), BF)],
        name="attend",
        compiler_params=params(24),
    )(place, queries, old, new)
    got = lax.all_to_all(partial, "ha", 0, 0, axis_index_groups=RINGS)
    copies_out = pl.pallas_call(combine_kernel, out_shape=shape(8, 256, 256), name="combine")(got)
    own, other = gather_features(copies_out)
    mixed = pl.pallas_call(
        output_kernel,
        grid=(8,),
        in_specs=[
            SMEM,
            block,
            block,
            pl.BlockSpec((1, 2, 256, 256), lambda s: (s, 0, 0, 0)),
            pl.BlockSpec((None, 256, 256), lambda s: (0, 0, 0)),
        ],
        out_specs=pl.BlockSpec((256, 256), lambda s: (0, 0)),
        out_shape=shape(256, 256),
        scratch_shapes=[pltpu.VMEM((256, 256), F32)],
        name="output",
        compiler_params=params(16),
    )(core, own, other, w_out.reshape(8, 2, 256, 256), copies)
    return (mixed, block_spectrum)


def solution(mesh):
    return jax.shard_map(
        local,
        mesh=mesh,
        in_specs=(
            P(None, "ha", ("grp", "pb")),
            P(("grp", "pb")),
            P(None, None, ("grp", "pb", "ha"), None),
            P(None, None, ("grp", "pb", "ha"), None),
            P(None, "ha", ("grp", "pb")),
            P(),
            P(None, None, ("grp", "pb")),
            P(None, ("grp", "pb")),
        ),
        out_specs=(P("ha", ("grp", "pb")), P(None, ("grp", "pb", "ha"), None)),
        check_vma=False,
    )
```

time: 472 us -> 167 us (0.35)
  waiting for transfers between devices: 353 us -> 20 us
  blocking collectives: 14.8 us -> 77.4 us
  matrix products: 41.6 us -> 0 us
  Pallas kernels: 0 us -> 28.6 us
  starting transfers between devices: 10.5 us -> 27.6 us
  local copies, waits for them, and re-layouts: 24.4 us -> 9.28 us
  between operations: 14.6 us -> 0.84 us
  other arithmetic: 13 us -> 0.8 us
    all_gather x6 -> x0, waiting for transfers between devices: 353 us -> none  [the longest x1 67.3 us: local(): lax.all_gather(keys_now, 'ha', axis=0, tiled=True)]
    all_to_all x1 -> x5, blocking collectives: 14.8 us -> 77.4 us  [the longest x2 35.7 us: gather_features(): own = lax.all_to_all(copies, GP, 0, 0, axis_index_groups=SAME_CORE)]
    dot_general x19 -> x0, matrix products: 41.6 us -> none  [the longest x2 11.7 us: absorb(): jnp.einsum('hrs,shd->hrd', expd.astype(jnp.bfloat16), values_piece, prefe...]
    pallas_call x0 -> x9, Pallas kernels: none -> 28.6 us  [the longest x1 8.87 us: local(): pl.pallas_call(attend_kernel, in_specs=[SMEM] + [pl.BlockSpec()] * 3, out...]
    all_to_all x1 -> x3, waiting for transfers between devices: 0.01 us -> 19.3 us  [the longest x1 15.8 us: local(): queries = lax.all_to_all(q_msg, 'ha', 0, 0, axis_index_groups=RINGS)]
    ppermute x0 -> x2, starting transfers between devices: none -> 10.5 us  [gather_features(): return (own, lax.ppermute(own, 'pb', OTHER_CORE))]
    unnamed x42 -> x28, local copies, waits for them, and re-layouts: 16.5 us -> 8.3 us
    all_to_all x1 -> x3, starting transfers between devices: 10 us -> 17.1 us  [the longest x1 10.2 us: local(): lax.all_to_all(gated_t.reshape(16, 16, 256), 'ha', 0, 0).reshape(256, 256)]
  transfers between devices with their start and end apart: 7 -> 5, of which waited for: 6 -> 3; matrix products, arithmetic and copies ran while one was open for 11% -> 1% of each run, Pallas kernels for 0% -> 5%
where the time goes in v2:
time: 167 us; the launch traced here: 165 us
  blocking collectives  77.4 us (46%)
  Pallas kernels  28.6 us (17%)
  starting transfers between devices  27.6 us (17%)
  waiting for transfers between devices  20 us (12%)
  local copies, waits for them, and re-layouts  9.28 us (6%)
    all_to_all x2, blocking collectives, gather_features(): own = lax.all_to_all(copies, GP, 0, 0, axis_index_groups=SAME_CORE)  35.7 us
    all_to_all x1, blocking collectives, local(): got = lax.all_to_all(partial, 'ha', 0, 0, axis_index_groups=RINGS)  18.9 us
    all_to_all x1, waiting for transfers between devices, local(): queries = lax.all_to_all(q_msg, 'ha', 0, 0, axis_index_groups=RINGS)  15.8 us
    all_to_all x1, blocking collectives, local(): lax.all_to_all(conv.reshape(16, 16, 256), 'ha', 0, 0).reshape(256, 256)  11.7 us
    all_to_all x1, blocking collectives, local(): new = lax.all_to_all(kv_msg, 'ha', 0, 0, axis_index_groups=QUADS)  11.1 us
    ppermute x2, starting transfers between devices, gather_features(): return (own, lax.ppermute(own, 'pb', OTHER_CORE))  10.5 us
    all_to_all x1, starting transfers between devices, local(): lax.all_to_all(gated_t.reshape(16, 16, 256), 'ha', 0, 0).reshape(256, 256)  10.2 us
    pallas_call x1, Pallas kernels, local(): pl.pallas_call(attend_kernel, in_specs=[SMEM] + [pl.BlockSpec()] * 3, out...  8.87 us
  transfers between devices with their start and end apart: 5, of which 3 were waited for; matrix products, arithmetic and copies ran while one was open for 1% of the time, Pallas kernels for 5%

profile of v2, /device:TPU:1, one launch (start us, length us, event | category | flops | bytes accessed | tf_op | source)
XLA Modules:
  0.0 164.5 jit_solution(1813869785979170893)
XLA Ops:
  0.6 1.8 %gate.1 = bf16[256,256]{1,0:T(8,128)(2,1)} custom-call(bf16[3,256,256]{2,1,0:T(8,128)(2,1)} %proj_ref.3), custom_call_target="tpu_custom_call" | custom-call | tf_op jit(solution)/shard_map/gate/pallas_call | solution.py:300
  2.4 0.0 copy-start.11
  2.4 10.2 %all-to-all-start = ((bf16[16,16,256]{2,1,0:T(8,128)(2,1)}), bf16[16,16,256]{2,1,0:T(8,128)(2,1)S(1)}, u32[]{:S(2)}, u32[]{:S(2)}) async-start(bf16[16,16,256]{2,1,0:T(8,128)(2,1)} %bitcast.25), calls=%async_computation | async-start | bytes 262144 | tf_op jit(solution)/shard_map/all_to_all | solution.py:301
  12.6 0.0 copy-start.3
  12.6 1.4 copy-done.3
  14.0 0.0 copy-start.4
  14.0 1.2 copy-done.4
  15.2 0.0 copy-start.5
  15.2 0.0 copy-start.6
  15.2 1.3 prepare.1.prep_ref
  16.5 3.5 %all-to-all-done = bf16[16,16,256]{2,1,0:T(8,128)(2,1)S(1)} async-done(((bf16[16,16,256]{2,1,0:T(8,128)(2,1)}), bf16[16,16,256]{2,1,0:T(8,128)(2,1)S(1)}, u32[]{:S(2)}, u32[]{:S(2)}) %all-to-all-start) | async-done | bytes 131104 | tf_op jit(solution)/shard_map/all_to_all | solution.py:301
  20.0 0.0 copy-done.11
  20.0 0.0 copy-done.5
  20.0 0.0 copy-done.6
  20.0 0.0 copy-start.7
  20.0 1.0 copy-done.7
  21.1 0.0 copy-start.8
  21.1 1.0 copy-done.8
  22.1 3.1 %convolve.1 = (bf16[256,256]{1,0:T(8,128)(2,1)S(1)}, f32[2,512,128]{2,1,0:T(8,128)S(1)}) custom-call(bf16[256,256]{1,0:T(8,128)(2,1)S(1)} %bitcast.21, f32[4,512,128]{2,1,0:T(8,128)S(1)} %prepare.1.prep_ref, bf16[2,1024,256]{2,1,0:T(8,128)(2,1)S(1)} %copy-done.5, bf16[2,512,256]{2,1,0:T(8,128)(2,1)S(1)} %copy-done.7, bf16[2,256,512]{2,1,0:T(8,128)(2,1)S(1)} %copy-done.8, ...), custom_call_target="tpu_custom_call" | custom-call | tf_op jit(solution)/shard_map/convolve/pallas_call | solution.py:305
  25.3 0.0 copy-start.9
  25.3 0.8 copy-done.9
  26.0 0.0 copy-start.13
  26.0 11.7 %all_to_all.40 = bf16[16,16,256]{2,1,0:T(8,128)(2,1)} all-to-all(bf16[16,16,256]{2,1,0:T(8,128)(2,1)S(1)} %bitcast.22), channel_id=1, replica_groups=mesh['grp'=2,'pb'=8,'ha'=16] {'ha'}, dimensions={0} | all-to-all | bytes 262144 | tf_op jit(solution)/shard_map/all_to_all | solution.py:311
  37.8 2.2 %hyena.1.hyena_ref = bf16[8,256,256]{2,1,0:T(8,128)(2,1)} custom-call(bf16[256,256]{1,0:T(8,128)(2,1)} %bitcast.26, bf16[3,256,256]{2,1,0:T(8,128)(2,1)} %proj_ref.3, f32[1,256]{1,0:T(1,128)} %bitcast.27), custom_call_target="tpu_custom_call" | custom-call | tf_op jit(solution)/shard_map/hyena/pallas_call | solution.py:315
  40.0 19.6 %all_to_all.41.own_ref = bf16[8,256,256]{2,1,0:T(8,128)(2,1)S(1)} all-to-all(bf16[8,256,256]{2,1,0:T(8,128)(2,1)} %hyena.1.hyena_ref), channel_id=1, replica_groups={{0,32,64,96,128,160,192,224},{16,48,80,112,144,176,208,240},{1,33,65,97..., dimensions={0} | all-to-all | bytes 2097152 | tf_op jit(solution)/shard_map/all_to_all | solution.py:283
  59.6 4.8 %collective-permute-start = (bf16[8,256,256]{2,1,0:T(8,128)(2,1)S(1)}, bf16[8,256,256]{2,1,0:T(8,128)(2,1)S(1)}, u32[]{:S(2)}, u32[]{:S(2)}) collective-permute-start(bf16[8,256,256]{2,1,0:T(8,128)(2,1)S(1)} %all_to_all.41.own_ref), channel_id=1, source_target_pairs={{0,16},{16,0},{32,48},{48,32},{64,80},{80,64},{96,112},{112,96},{1... | collective-permute-start | bytes 3145736 | tf_op jit(solution)/shard_map/ppermute | solution.py:284
  64.4 0.0 copy-done.13
  64.5 0.1 reshape.57
  64.5 0.0 copy-start.12
  64.6 0.9 broadcast_in_dim.2
  65.4 3.5 %all-to-all-start.4 = ((bf16[4,2,256,128]{3,2,1,0:T(8,128)(2,1)}), bf16[4,2,256,128]{3,2,1,0:T(8,128)(2,1)S(1)}, u32[]{:S(2)}, u32[]{:S(2)}) async-start(bf16[4,2,256,128]{3,2,1,0:T(8,128)(2,1)} %bitcast.14), calls=%async_computation.4 | async-start | bytes 1048576 | tf_op jit(solution)/shard_map/all_to_all | solution.py:351
  69.0 0.5 multiply_cosine_fusion
  69.5 0.1 maximum_bitcast_fusion
  69.7 0.0 collective-permute-done.other_ref
  69.7 0.0 copy-done.12
  69.7 0.0 copy-start.1
  69.7 2.8 %copy-done.1 = bf16[4096,3,256]{2,0,1:T(8,128)(2,1)S(1)} copy-done((bf16[4096,3,256]{2,0,1:T(8,128)(2,1)S(1)}, bf16[4096,3,256]{2,0,1:T(8,128)(2,1)}, u32[]{:S(2)}) %copy-start.1) | copy-done | bytes 6291480
  72.5 4.7 %project.1 = (bf16[8,256,128]{2,1,0:T(8,128)(2,1)}, bf16[4,2,256,128]{3,2,1,0:T(8,128)(2,1)S(1)}) custom-call(s32[1]{0:T(128)} %bitcast.core_ref, bf16[8,256,256]{2,1,0:T(8,128)(2,1)S(1)} %all_to_all.41.own_ref, bf16[8,256,256]{2,1,0:T(8,128)(2,1)S(1)} %collective-permute-done.other_ref, bf16[3,8,2,256,256]{4,3,2,1,0:T(8,128)(2,1)S(1)} %bitcast.19, ...), custom_call_target="tpu_custom_call" | custom-call | tf_op jit(solution)/shard_map/project/pallas_call | solution.py:321
  77.2 0.0 all-to-all-done.4.old_ref
  77.2 11.1 %all_to_all.42.new_ref = bf16[4,2,256,128]{3,2,1,0:T(8,128)(2,1)S(1)} all-to-all(bf16[4,2,256,128]{3,2,1,0:T(8,128)(2,1)S(1)} %get-tuple-element.8), channel_id=1, replica_groups={{0,1,8,9},{2,3,10,11},{4,5,12,13},{6,7,14,15},{16,17,24,25},{18,19,26,2..., dimensions={0} | all-to-all | bytes 1048576 | tf_op jit(solution)/shard_map/all_to_all | solution.py:353
  88.3 3.5 %all-to-all-start.3 = ((bf16[8,256,128]{2,1,0:T(8,128)(2,1)}), bf16[8,256,128]{2,1,0:T(8,128)(2,1)S(1)}, u32[]{:S(2)}, u32[]{:S(2)}) async-start(bf16[8,256,128]{2,1,0:T(8,128)(2,1)} %get-tuple-element.7), calls=%async_computation.3 | async-start | bytes 1048576 | tf_op jit(solution)/shard_map/all_to_all | solution.py:352
  91.9 0.1 pad_add_fusion.place_ref
  91.9 15.8 %all-to-all-done.3.q_ref = bf16[8,256,128]{2,1,0:T(8,128)(2,1)S(1)} async-done(((bf16[8,256,128]{2,1,0:T(8,128)(2,1)}), bf16[8,256,128]{2,1,0:T(8,128)(2,1)S(1)}, u32[]{:S(2)}, u32[]{:S(2)}) %all-to-all-start.3) | async-done | bytes 524320 | tf_op jit(solution)/shard_map/all_to_all | solution.py:352
  107.7 8.9 %attend.1 = bf16[8,144,256]{2,1,0:T(8,128)(2,1)S(1)} custom-call(s32[2]{0:T(128)S(1)} %pad_add_fusion.place_ref, bf16[8,256,128]{2,1,0:T(8,128)(2,1)S(1)} %all-to-all-done.3.q_ref, bf16[4,2,256,128]{3,2,1,0:T(8,128)(2,1)S(1)} %all-to-all-done.4.old_ref, bf16[4,2,256,128]{3,2,1,0:T(8,128)(2,1)S(1)} %all_to_all.42.new_ref), custom_call_target="tpu_custom_call" | custom-call | tf_op jit(solution)/shard_map/attend/pallas_call | solution.py:354
  116.6 18.9 %all_to_all.43.got_ref = bf16[8,144,256]{2,1,0:T(8,128)(2,1)} all-to-all(bf16[8,144,256]{2,1,0:T(8,128)(2,1)S(1)} %attend.1), channel_id=1, replica_groups={{0,1,2,3,4,5,6,7},{8,9,10,11,12,13,14,15},{16,17,18,19,20,21,22,23},{24..., dimensions={0} | all-to-all | bytes 1179648 | tf_op jit(solution)/shard_map/all_to_all | solution.py:362
  135.4 0.0 copy-start
  135.4 0.0 copy-start.2
  135.5 2.5 %combine.1 = bf16[8,256,256]{2,1,0:T(8,128)(2,1)} custom-call(bf16[8,144,256]{2,1,0:T(8,128)(2,1)} %all_to_all.43.got_ref), custom_call_target="tpu_custom_call" | custom-call | tf_op jit(solution)/shard_map/combine/pallas_call | solution.py:363
  137.9 0.0 copy-start.10
  137.9 16.0 %all_to_all.44.own_ref = bf16[8,256,256]{2,1,0:T(8,128)(2,1)S(1)} all-to-all(bf16[8,256,256]{2,1,0:T(8,128)(2,1)} %combine.1), channel_id=1, replica_groups={{0,32,64,96,128,160,192,224},{16,48,80,112,144,176,208,240},{1,33,65,97..., dimensions={0} | all-to-all | bytes 2097152 | tf_op jit(solution)/shard_map/all_to_all | solution.py:283
  154.0 5.6 %collective-permute-start.1 = (bf16[8,256,256]{2,1,0:T(8,128)(2,1)S(1)}, bf16[8,256,256]{2,1,0:T(8,128)(2,1)S(1)}, u32[]{:S(2)}, u32[]{:S(2)}) collective-permute-start(bf16[8,256,256]{2,1,0:T(8,128)(2,1)S(1)} %all_to_all.44.own_ref), channel_id=1, source_target_pairs={{0,16},{16,0},{32,48},{48,32},{64,80},{80,64},{96,112},{112,96},{1... | collective-permute-start | bytes 3145736 | tf_op jit(solution)/shard_map/ppermute | solution.py:284
  159.6 0.0 copy-done.10
  159.6 1.5 restore.1
  161.2 0.7 collective-permute-done.1.other_ref
  161.9 0.0 copy-done
  161.9 0.0 copy-done.2
  161.9 2.6 %output.1 = bf16[256,256]{1,0:T(8,128)(2,1)} custom-call(s32[1]{0:T(128)} %bitcast.core_ref, bf16[8,256,256]{2,1,0:T(8,128)(2,1)S(1)} %all_to_all.44.own_ref, bf16[8,256,256]{2,1,0:T(8,128)(2,1)S(1)} %collective-permute-done.1.other_ref, bf16[8,2,256,256]{3,2,1,0:T(8,128)(2,1)S(1)} %bitcast.20, bf16[8,256,256]{2,1,0:T(8,128)(2,1)S(1)} %copy-done), custom_call_target="tpu_custom_call" | custom-call | tf_op jit(solution)/shard_map/output/pallas_call | solution.py:365
  (4 shorter events, 0.1 us)
Async XLA Ops:
  2.4 17.6 %copy-start.11 = (f32[2,32,256]{2,1,0:T(8,128)S(1)}, f32[2,32,256]{2,1,0:T(8,128)}, u32[]{:S(2)}) copy-start(f32[2,32,256]{2,1,0:T(8,128)} %constant.75.clone.turn_ref) | copy-start | bytes 196612
  2.4 17.6 %all-to-all-start = ((bf16[16,16,256]{2,1,0:T(8,128)(2,1)}), bf16[16,16,256]{2,1,0:T(8,128)(2,1)S(1)}, u32[]{:S(2)}, u32[]{:S(2)}) async-start(bf16[16,16,256]{2,1,0:T(8,128)(2,1)} %bitcast.25), calls=%async_computation | async-start | bytes 262144 | tf_op jit(solution)/shard_map/all_to_all | solution.py:301
  12.6 1.4 copy-start.3
  14.0 1.2 copy-start.4
  15.2 4.8 %copy-start.5 = (bf16[2,1024,256]{2,1,0:T(8,128)(2,1)S(1)}, bf16[2,1024,256]{2,1,0:T(8,128)(2,1)}, u32[]{:S(2)}) copy-start(bf16[2,1024,256]{2,1,0:T(8,128)(2,1)} %constant.71.clone.first_ref) | copy-start | bytes 3145732
  15.2 4.8 %copy-start.6 = (bf16[2,256,1024]{2,1,0:T(8,128)(2,1)S(1)}, bf16[2,256,1024]{2,1,0:T(8,128)(2,1)}, u32[]{:S(2)}) copy-start(bf16[2,256,1024]{2,1,0:T(8,128)(2,1)} %constant.74.clone.fourth_ref) | copy-start | bytes 3145732
  20.0 1.0 copy-start.7
  21.1 1.0 copy-start.8
  25.3 0.8 copy-start.9
  26.0 38.4 %copy-start.13 = (bf16[2,256,256]{2,1,0:T(8,128)(2,1)S(1)}, bf16[2,256,256]{2,1,0:T(8,128)(2,1)}, u32[]{:S(2)}) copy-start(bf16[2,256,256]{2,1,0:T(8,128)(2,1)} %param.17) | copy-start | bytes 786436
  59.6 10.0 %collective-permute-start = (bf16[8,256,256]{2,1,0:T(8,128)(2,1)S(1)}, bf16[8,256,256]{2,1,0:T(8,128)(2,1)S(1)}, u32[]{:S(2)}, u32[]{:S(2)}) collective-permute-start(bf16[8,256,256]{2,1,0:T(8,128)(2,1)S(1)} %all_to_all.41.own_ref), channel_id=1, source_target_pairs={{0,16},{16,0},{32,48},{48,32},{64,80},{80,64},{96,112},{112,96},{1... | collective-permute-start | bytes 3145736 | tf_op jit(solution)/shard_map/ppermute | solution.py:284
  64.5 5.2 %copy-start.12 = (f32[4096]{0:T(1024)S(1)}, f32[4096]{0:T(1024)}, u32[]{:S(2)}) copy-start(f32[4096]{0:T(1024)} %param.18) | copy-start | bytes 49156
  65.4 11.8 %all-to-all-start.4 = ((bf16[4,2,256,128]{3,2,1,0:T(8,128)(2,1)}), bf16[4,2,256,128]{3,2,1,0:T(8,128)(2,1)S(1)}, u32[]{:S(2)}, u32[]{:S(2)}) async-start(bf16[4,2,256,128]{3,2,1,0:T(8,128)(2,1)} %bitcast.14), calls=%async_computation.4 | async-start | bytes 1048576 | tf_op jit(solution)/shard_map/all_to_all | solution.py:351
  69.7 2.8 %copy-start.1 = (bf16[4096,3,256]{2,0,1:T(8,128)(2,1)S(1)}, bf16[4096,3,256]{2,0,1:T(8,128)(2,1)}, u32[]{:S(2)}) copy-start(bf16[4096,3,256]{2,0,1:T(8,128)(2,1)} %param.19) | copy-start | bytes 18874372
  88.3 19.4 %all-to-all-start.3 = ((bf16[8,256,128]{2,1,0:T(8,128)(2,1)}), bf16[8,256,128]{2,1,0:T(8,128)(2,1)S(1)}, u32[]{:S(2)}, u32[]{:S(2)}) async-start(bf16[8,256,128]{2,1,0:T(8,128)(2,1)} %get-tuple-element.7), calls=%async_computation.3 | async-start | bytes 1048576 | tf_op jit(solution)/shard_map/all_to_all | solution.py:352
  135.4 26.4 %copy-start = (bf16[8,256,256]{2,1,0:T(8,128)(2,1)S(1)}, bf16[8,256,256]{2,1,0:T(8,128)(2,1)}, u32[]{:S(2)}) copy-start(bf16[8,256,256]{2,1,0:T(8,128)(2,1)} %hyena.1.hyena_ref) | copy-start | bytes 3145732
  135.4 26.4 %copy-start.2 = (bf16[4096,256]{1,0:T(8,128)(2,1)S(1)}, bf16[4096,256]{1,0:T(8,128)(2,1)}, u32[]{:S(2)}) copy-start(bf16[4096,256]{1,0:T(8,128)(2,1)} %param.20) | copy-start | bytes 6291460
  137.9 21.7 %copy-start.10 = (f32[2,512,128]{2,1,0:T(8,128)S(1)}, f32[2,512,128]{2,1,0:T(8,128)}, u32[]{:S(2)}) copy-start(f32[2,512,128]{2,1,0:T(8,128)} %copy-done.9) | copy-start | bytes 1572868
  154.0 7.9 %collective-permute-start.1 = (bf16[8,256,256]{2,1,0:T(8,128)(2,1)S(1)}, bf16[8,256,256]{2,1,0:T(8,128)(2,1)S(1)}, u32[]{:S(2)}, u32[]{:S(2)}) collective-permute-start(bf16[8,256,256]{2,1,0:T(8,128)(2,1)S(1)} %all_to_all.44.own_ref), channel_id=1, source_target_pairs={{0,16},{16,0},{32,48},{48,32},{64,80},{80,64},{96,112},{112,96},{1... | collective-permute-start | bytes 3145736 | tf_op jit(solution)/shard_map/ppermute | solution.py:284

commit v3 on v2

v3 whole, which is shorter than its diff:
```python
import functools
import math

import jax
import jax.numpy as jnp
import ml_dtypes
import numpy as np
from jax import lax
from jax.experimental import pallas as pl
from jax.experimental.pallas import tpu as pltpu
from jax.sharding import PartitionSpec as P

HEAD = 128
BF = jnp.bfloat16
F32 = jnp.float32
GP = ("grp", "pb")
NEAR = [[8 * x + k for x in range(2) for k in range(4)], [8 * x + 7 - k for x in range(2) for k in range(4)]]
SAME_CORE = [[8 * g + 2 * y + c for g in range(2) for y in range(4)] for c in range(2)]
OTHER_CORE = [(j, j ^ 1) for j in range(8)]
SMEM = pl.BlockSpec(memory_space=pltpu.SMEM)


def params(mib):
    return pltpu.CompilerParams(vmem_limit_bytes=mib * 2**20)


def pair(table):
    high = table.astype(ml_dtypes.bfloat16)
    low = (table - high.astype(np.float64)).astype(ml_dtypes.bfloat16)
    return high, low


@functools.cache
def tables():
    s, k1, t = np.arange(16), np.arange(32), np.arange(256)
    eye = np.eye(16)
    angle = 2 * np.pi / 32 * (np.outer(k1, s) % 32)
    compact = np.stack([np.cos(angle), -np.sin(angle)])
    first = np.einsum("rks,cd->rcksd", compact, eye).reshape(1024, 256)
    angle = 2 * np.pi / 8192 * np.outer(k1, t)
    turn = np.stack([np.cos(angle), np.sin(angle)])
    k2 = (4 * np.arange(32)[None, :] + np.arange(4)[:, None]).reshape(-1)
    angle = 2 * np.pi / 256 * (np.outer(t, k2) % 256)
    cos, sin = np.cos(angle), np.sin(angle)
    second = np.block([[cos, -sin], [sin, cos]])
    compact = np.repeat(compact.reshape(64, 16), 16, axis=1)
    fourth = (first.T / 4096.0).reshape(256, 4, 256).transpose(1, 0, 2).reshape(1024, 256)
    rows = [part for table in (compact, turn.reshape(64, 256), second, fourth) for part in pair(table)]
    return np.concatenate(rows)


def split(values):
    high = values.astype(BF)
    return high, (values - high.astype(F32)).astype(BF)


def mul(a, b):
    return jnp.dot(a, b, preferred_element_type=F32)


def mul_t(a, b):
    return lax.dot_general(a, b, (((1,), (1,)), ((), ())), preferred_element_type=F32)


def gate_kernel(proj_ref, turned_ref):
    gated = (proj_ref[1].astype(F32) * proj_ref[2].astype(F32)).astype(BF)
    turned_ref[...] = gated.astype(F32).T.astype(BF)


def to_tiles(nat):
    out = []
    cube = nat.reshape(16, 32, 128)
    for g in range(4):
        tile = cube[4 * g : 4 * g + 4].reshape(128, 128).T
        for c in range(4):
            out.append(
                jnp.concatenate(
                    [tile[32 * q : 32 * q + 32, 32 * c : 32 * c + 32] for q in range(4)], axis=1
                )
            )
    return jnp.concatenate(out, axis=0)


def from_tiles(tiles):
    out = []
    for g in range(4):
        part = tiles[128 * g : 128 * g + 128]
        swapped = jnp.concatenate(
            [
                jnp.concatenate(
                    [part[32 * c : 32 * c + 32, 32 * q : 32 * q + 32] for c in range(4)], axis=1
                )
                for q in range(4)
            ],
            axis=0,
        )
        out.append(swapped.T.reshape(4, 32, 128))
    return jnp.concatenate(out, axis=0).reshape(16, 4096)


def prepare_kernel(filters_ref, resident_ref, proj_ref, out_ref, outer_ref, gated_ref):
    outer_ref[...] = proj_ref[0]
    gated_ref[...] = (proj_ref[1].astype(F32) * proj_ref[2].astype(F32)).astype(BF)
    lane = lax.broadcasted_iota(jnp.int32, (512, 128), 1)
    row = lax.broadcasted_iota(jnp.int32, (512, 128), 0)
    weight = jnp.where((lane == 0) & (row % 32 == 0), 0.5, 1.0)
    real = jnp.zeros((16, 4096), F32)
    imag = jnp.zeros((16, 4096), F32)
    for m in range(2):
        ar, ai = resident_ref[m, 0], resident_ref[m, 1]
        br, bi = filters_ref[m + 1, 0], filters_ref[m + 1, 1]
        real = real + ar * br - ai * bi
        imag = imag + ar * bi + ai * br
    out_ref[0] = to_tiles(filters_ref[0, 0]) * weight
    out_ref[1] = to_tiles(filters_ref[0, 1]) * weight
    out_ref[2] = to_tiles(real) * weight
    out_ref[3] = to_tiles(imag) * weight


def restore_kernel(tiles_ref, after_ref, out_ref, token_ref):
    token_ref[...] = jnp.zeros_like(token_ref)
    out_ref[0] = from_tiles(tiles_ref[0])
    out_ref[1] = from_tiles(tiles_ref[1])


def conv_kernel(x_ref, prep_ref, table_ref, after_ref, conv_ref, spec_ref):
    x = x_ref[...]
    channel = lax.broadcasted_iota(jnp.int32, (2, 16, 32, 256), 1)
    lane = lax.broadcasted_iota(jnp.int32, (2, 16, 32, 256), 3)
    own = lane % 16 == channel
    part = jnp.zeros((1024, 256), F32)
    for n in range(2):
        block = table_ref[64 * n : 64 * n + 64].astype(F32).reshape(2, 1, 32, 256)
        block = jnp.where(own, block, 0.0).reshape(1024, 256).astype(BF)
        part = part + mul(block, x)
    turn = table_ref[128:192].astype(F32) + table_ref[192:256].astype(F32)
    cos, sin = turn[:32], turn[32:]
    second = [table_ref[256 + 512 * n : 768 + 512 * n] for n in range(2)]
    real = part[:512].reshape(16, 32, 256)
    imag = part[512:].reshape(16, 32, 256)
    turned = jnp.concatenate(
        [(real * cos + imag * sin).reshape(512, 256), (imag * cos - real * sin).reshape(512, 256)], axis=1
    )
    high, low = split(turned)
    spec = mul(high, second[0]) + mul(low, second[0]) + mul(high, second[1])
    real, imag = spec[:, :128], spec[:, 128:]
    spec_ref[0] = real
    spec_ref[1] = imag
    z = jnp.concatenate(
        [
            real * prep_ref[0] - imag * prep_ref[1] + prep_ref[2],
            real * prep_ref[1] + imag * prep_ref[0] + prep_ref[3],
        ],
        axis=1,
    )
    high, low = split(z)
    back = mul_t(high, second[0]) + mul_t(low, second[0]) + mul_t(high, second[1])
    real = back[:, :256].reshape(16, 32, 256)
    imag = back[:, 256:].reshape(16, 32, 256)
    turned = jnp.concatenate(
        [(real * cos - imag * sin).reshape(512, 256), (real * sin + imag * cos).reshape(512, 256)], axis=0
    )
    high, low = split(turned)
    fourth = [
        jnp.concatenate([table_ref[1280 + 1024 * n + 256 * j : 1536 + 1024 * n + 256 * j] for j in range(4)], axis=1)
        for n in range(2)
    ]
    conv = mul(fourth[0], high) + mul(fourth[0], low) + mul(fourth[1], high)
    conv_ref[...] = conv.astype(BF)


def hyena_kernel(conv_ref, gated_ref, outer_ref, dskip_ref, out_ref, value_ref):
    conv = conv_ref[...].astype(F32).T
    value = outer_ref[...].astype(F32) * (conv + dskip_ref[...] * gated_ref[...].astype(F32))
    value = value.astype(BF)
    value_ref[...] = value
    for copy in range(8):
        out_ref[copy] = value


def pick_kernel(place_ref, cache_ref, after_ref, mine_ref, theirs_ref):
    own = place_ref[0]
    for ref, head in ((mine_ref, own), (theirs_ref, 1 - own)):
        ref[...] = cache_ref[:, :, pl.ds(pl.multiple_of(head * HEAD, HEAD), HEAD)]


def rotated(values, cos, sin):
    return values * cos + pltpu.roll(values, 64, 1) * sin


def qkv_kernel(
    place_ref, own_ref, other_ref, w_ref, gain_ref, turn_ref, token_ref,
    q_ref, scale_ref, mine_ref, theirs_ref, acc_ref, square_ref,
):
    step = pl.program_id(0)
    own_head, core = place_ref[0], place_ref[3]

    @pl.when(step == 0)
    def _():
        acc_ref[...] = jnp.zeros_like(acc_ref)
        square_ref[...] = jnp.zeros_like(square_ref)

    a, b = own_ref[0].astype(F32), other_ref[0].astype(F32)
    square_ref[...] += a * a + b * b
    a = (a * gain_ref[2 * step + core]).astype(BF)
    b = (b * gain_ref[2 * step + 1 - core]).astype(BF)
    for part in range(3):
        acc_ref[part] += mul(a, w_ref[part, 0, core]) + mul(b, w_ref[part, 0, 1 - core])

    @pl.when(step == 7)
    def _():
        scale = lax.rsqrt(jnp.sum(square_ref[...], axis=1, keepdims=True) / 4096.0 + 1e-05)
        cos, sin = turn_ref[0], turn_ref[1]
        q_ref[...] = acc_ref[0]
        scale_ref[...] = jnp.broadcast_to(scale, (256, 128))
        first = own_head == 0
        for slot in range(2):
            low, high = (acc_ref[slot + 1, :, 128 * h : 128 * h + 128] * scale for h in range(2))
            mine = jnp.where(first, low, high)
            theirs = jnp.where(first, high, low)
            if slot == 0:
                mine = rotated(mine, cos, sin)
                theirs = rotated(theirs, cos, sin)
            mine_ref[slot] = mine.astype(BF)
            theirs_ref[slot] = theirs.astype(BF)


def queries_kernel(raw_ref, scale_ref, turn_ref, q_ref):
    scale = scale_ref[...] * (math.log2(math.e) / math.sqrt(HEAD))
    for h in range(2):
        q = raw_ref[:, 128 * h : 128 * h + 128] * scale
        q = rotated(q, turn_ref[0], turn_ref[1]).astype(BF)
        for dest in range(4):
            q_ref[4 * h + dest] = q


def stage_kernel(*refs):
    keys_ref, values_ref = refs[4:]
    for n, piece in enumerate(refs[:4]):
        keys_ref[256 * n : 256 * n + 256] = piece[0]
        values_ref[:, 256 * n : 256 * n + 256] = piece[1].astype(F32).T.astype(BF)


def attend_kernel(place_ref, q_ref, keys_ref, values_ref, *rest):
    pieces, (out_ref, new_keys, new_values) = rest[:4], rest[4:]
    x, q, k = place_ref[0], place_ref[1], place_ref[2]
    slots = (2 * x + q, 2 * x + 1 - q, 2 * (1 - x) + q, 2 * (1 - x) + 1 - q)
    for slot, piece in zip(slots, pieces):
        spot = pl.ds(pl.multiple_of(slot * 256, 256), 256)
        new_keys[spot, :] = piece[0]
        new_values[:, spot] = piece[1].astype(F32).T.astype(BF)
    sub = lax.broadcasted_iota(jnp.int32, (256, 256), 0)
    lane = lax.broadcasted_iota(jnp.int32, (256, 256), 1)
    row16 = lax.broadcasted_iota(jnp.int32, (16, 256), 0)

    def block_of(i):
        near = i % 4
        return 8 * (i // 4) + jnp.where(q == 0, near, 7 - near)

    def scores_of(i, used):
        scores = [mul_t(keys_ref[...], q_ref[i])]
        if used:
            now = mul_t(new_keys[: 256 * used], q_ref[i])
            block = (k, 7 - k, 8 + k, 15 - k)[used - 1]
            ahead = (block - block_of(i)) * 256
            last = jnp.where(sub + ahead <= lane, now[256 * used - 256 :], -1e30)
            scores += [now[: 256 * used - 256], last] if used > 1 else [last]
        return jnp.concatenate(scores, axis=0)

    def finish(i, top, total, part):
        out_ref[i, :128] = (part / total).astype(BF)
        level = top + jnp.log2(total)
        a = level.astype(BF).astype(F32)
        b = (level - a).astype(BF).astype(F32)
        c = (level - a - b).astype(BF).astype(F32)
        rows = jnp.where(row16 == 0, a, jnp.where(row16 == 1, b, jnp.where(row16 == 2, c, 0.0)))
        out_ref[i, 128:] = rows.astype(BF)

    def two(tiles, used):
        found = []
        for i, n in zip(tiles, used):
            scores = scores_of(i, n)
            found.append((scores, jnp.max(scores, axis=0, keepdims=True)))
        done = []
        for (scores, top), n in zip(found, used):
            expd = jnp.exp2(scores - top)
            total = jnp.sum(expd, axis=0, keepdims=True)
            expd = expd.astype(BF)
            part = mul(values_ref[...], expd[:1024])
            if n:
                part = part + mul(new_values[:, : 256 * n], expd[1024:])
            done.append((top, total, part))
        for i, results in zip(tiles, done):
            finish(i, *results)

    def used_by(i):
        return sum(jnp.where(block <= block_of(i), 1, 0) for block in (k, 7 - k, 8 + k, 15 - k))

    def body(j, carry):
        tiles = (2 * j + q, 2 * j + 1 - q)
        low, high = (used_by(i) for i in tiles)
        for n in range(5):
            for more in (0, 1) if n < 4 else (0,):
                pl.when((low == n) & (high == n + more))(functools.partial(two, tiles, (n, n + more)))
        return carry

    lax.fori_loop(0, 4, body, 0)


def combine_kernel(got_ref, out_ref):
    outs = []
    for h in range(2):
        levels = [
            jnp.sum(got_ref[4 * h + k, 128:].astype(F32), axis=0, keepdims=True) for k in range(4)
        ]
        top = jnp.maximum(jnp.maximum(levels[0], levels[1]), jnp.maximum(levels[2], levels[3]))
        shares = [jnp.exp2(level - top) for level in levels]
        total = shares[0] + shares[1] + shares[2] + shares[3]
        acc = jnp.zeros((128, 256), F32)
        for k in range(4):
            acc = acc + got_ref[4 * h + k, :128].astype(F32) * (shares[k] / total)
        outs.append(acc.T)
    value = jnp.concatenate(outs, axis=1).astype(BF)
    for copy in range(8):
        out_ref[copy] = value


def output_own_kernel(place_ref, own_ref, w_ref, hyena_ref, out_ref):
    core = place_ref[3]
    acc = hyena_ref[...].astype(F32)
    for s in range(8):
        acc = acc + mul(own_ref[s], w_ref[2 * s + core])
    out_ref[...] = acc


def output_kernel(place_ref, other_ref, w_ref, part_ref, out_ref):
    core = 1 - place_ref[3]
    acc = part_ref[...]
    for s in range(8):
        acc = acc + mul(other_ref[s], w_ref[2 * s + core])
    out_ref[...] = acc.astype(BF)


def shape(*dims, dtype=BF):
    return jax.ShapeDtypeStruct(dims, dtype)


def rotation(rows, ha_index):
    freqs = 10000.0 ** (-jnp.arange(64, dtype=F32) / 64)
    places = 16 * rows + ha_index * rows + jnp.arange(rows, dtype=jnp.int32)
    angles = places.astype(F32)[:, None] * freqs[None, :]
    cos, sin = jnp.cos(angles), jnp.sin(angles)
    return jnp.stack([jnp.concatenate([cos, cos], 1), jnp.concatenate([-sin, sin], 1)])


X_FLIP = [(i, i ^ 8) for i in range(16)]
Q_FLIP = [(i, i ^ 7) for i in range(16)]
XQ_FLIP = [(i, i ^ 15) for i in range(16)]


def trade(mine, theirs):
    return (
        mine,
        lax.ppermute(mine, "ha", Q_FLIP),
        lax.ppermute(theirs, "ha", X_FLIP),
        lax.ppermute(theirs, "ha", XQ_FLIP),
    )


WHOLE = pl.BlockSpec()
FAR = pl.BlockSpec(memory_space=pltpu.HBM)


def gather_same_core(copies):
    return lax.all_to_all(copies, GP, 0, 0, axis_index_groups=SAME_CORE)


def local(hyena_proj, dskip, filters, resident, cache_kv, norm_gain, w_qkv, w_out):
    ha_index = lax.axis_index("ha")
    core = lax.axis_index("pb") % 2
    z = ha_index % 8
    query_half = z // 4
    place = jnp.stack([ha_index // 8, query_half, jnp.where(query_half == 0, z, 7 - z), core]).astype(jnp.int32)

    gated_t = pl.pallas_call(
        gate_kernel, out_shape=shape(256, 256), name="gate", compiler_params=params(4)
    )(hyena_proj)
    columns = lax.all_to_all(gated_t.reshape(16, 16, 256), "ha", 0, 0).reshape(256, 256)
    turn = rotation(256, ha_index)
    prep, outer, gated = pl.pallas_call(
        prepare_kernel,
        out_shape=(shape(4, 512, 128, dtype=F32), shape(256, 256), shape(256, 256)),
        name="prepare",
        compiler_params=params(16),
    )(filters, resident, hyena_proj)
    conv, tiles = pl.pallas_call(
        conv_kernel,
        out_shape=(shape(256, 256), shape(2, 512, 128, dtype=F32)),
        in_specs=[WHOLE] * 3 + [FAR],
        name="convolve",
        compiler_params=params(24),
    )(columns, prep, jnp.asarray(tables()), turn)
    conv = lax.all_to_all(conv.reshape(16, 16, 256), "ha", 0, 0).reshape(256, 256)
    copies, hyena_out = pl.pallas_call(
        hyena_kernel,

        out_shape=(shape(8, 256, 256), shape(256, 256)),
        name="hyena",
        compiler_params=params(6),
    )(conv, gated, outer, dskip.reshape(1, 256))

    own = gather_same_core(copies)
    mine, theirs = pl.pallas_call(
        pick_kernel,
        in_specs=[SMEM, WHOLE, FAR],
        out_shape=(shape(2, 256, 128), shape(2, 256, 128)),
        name="pick",
        compiler_params=params(4),
    )(place, cache_kv, hyena_out)
    own, old = lax.optimization_barrier((own, trade(mine, theirs)))
    other = lax.ppermute(own, "pb", OTHER_CORE)
    block_spectrum, token = pl.pallas_call(
        restore_kernel,
        in_specs=[WHOLE, FAR],
        out_shape=(shape(2, 16, 4096, dtype=F32), shape(8, 128, dtype=F32)),
        name="restore",
        compiler_params=params(8),
    )(tiles, own)
    block = pl.BlockSpec((1, 256, 256), lambda s: (s, 0, 0))
    trio = lambda *dims: pl.BlockSpec(dims, lambda s: (0,) * len(dims))
    raw, scale, mine, theirs = pl.pallas_call(
        qkv_kernel,
        grid=(8,),
        in_specs=[
            SMEM,
            block,
            block,
            pl.BlockSpec((3, 1, 2, 256, 256), lambda s: (0, s, 0, 0, 0)),
            trio(16, 1, 256),
            trio(2, 256, 128),
            FAR,
        ],
        out_specs=(trio(256, 256), trio(256, 128), trio(2, 256, 128), trio(2, 256, 128)),
        out_shape=(
            shape(256, 256, dtype=F32),
            shape(256, 128, dtype=F32),
            shape(2, 256, 128),
            shape(2, 256, 128),
        ),
        scratch_shapes=[pltpu.VMEM((3, 256, 256), F32), pltpu.VMEM((256, 256), F32)],
        name="project",
        compiler_params=params(16),
    )(
        place,
        own,
        other,
        jnp.transpose(w_qkv, (1, 0, 2)).reshape(3, 8, 2, 256, 256),
        norm_gain.reshape(16, 1, 256),
        turn,
        token,
    )
    new = trade(mine, theirs)
    q_msg = pl.pallas_call(
        queries_kernel, out_shape=shape(8, 256, 128), name="queries", compiler_params=params(4)
    )(raw, scale, turn)
    queries = lax.all_to_all(q_msg, "ha", 0, 0, axis_index_groups=NEAR)
    keys, values = pl.pallas_call(
        stage_kernel, out_shape=(shape(1024, 128), shape(128, 1024)), name="stage", compiler_params=params(8)
    )(*old)
    partial = pl.pallas_call(
        attend_kernel,
        in_specs=[SMEM] + [WHOLE] * 7,
        out_shape=shape(8, 144, 256),
        scratch_shapes=[pltpu.VMEM((1024, 128), BF), pltpu.VMEM((128, 1024), BF)],
        name="attend",
        compiler_params=params(20),
    )(place, queries, keys, values, *new)
    got = lax.all_to_all(partial, "ha", 0, 0, axis_index_groups=NEAR)
    copies_out = pl.pallas_call(
        combine_kernel, out_shape=shape(8, 256, 256), name="combine", compiler_params=params(8)
    )(got)
    own = gather_same_core(copies_out)
    other = lax.ppermute(own, "pb", OTHER_CORE)
    w_blocks = w_out.reshape(16, 256, 256)
    part = pl.pallas_call(
        output_own_kernel,
        in_specs=[SMEM, WHOLE, WHOLE, WHOLE],
        out_shape=shape(256, 256, dtype=F32),
        name="output_own",
        compiler_params=params(8),
    )(place, own, w_blocks, hyena_out)
    mixed = pl.pallas_call(
        output_kernel,
        in_specs=[SMEM] + [WHOLE] * 3,
        out_shape=shape(256, 256),
        name="output",
        compiler_params=params(8),
    )(place, other, w_blocks, part)
    return (mixed, block_spectrum)


def solution(mesh):
    return jax.shard_map(
        local,
        mesh=mesh,
        in_specs=(
            P(None, "ha", ("grp", "pb")),
            P(("grp", "pb")),
            P(None, None, ("grp", "pb", "ha"), None),
            P(None, None, ("grp", "pb", "ha"), None),
            P(None, "ha", ("grp", "pb")),
            P(),
            P(None, None, ("grp", "pb")),
            P(None, ("grp", "pb")),
        ),
        out_specs=(P("ha", ("grp", "pb")), P(None, ("grp", "pb", "ha"), None)),
        check_vma=False,
    )
```

time: 167 us -> 153 us (0.916); the launches traced: 165 us -> 152 us
  blocking collectives: 77.4 us -> 56.1 us
  starting transfers between devices: 27.6 us -> 37.9 us
  Pallas kernels: 28.6 us -> 23.2 us
  waiting for transfers between devices: 20 us -> 23.9 us
    all_to_all x4 -> x2, blocking collectives: 65.7 us -> 42.4 us  [the longest x1 22.1 us: local(): got = lax.all_to_all(partial, 'ha', 0, 0, axis_index_groups=NEAR)]
    ppermute x2 -> x8, waiting for transfers between devices: 0.74 us -> 20.4 us  [the longest x2 15.3 us: trade(): lax.ppermute(theirs, 'ha', XQ_FLIP)]
    all_to_all x2, waiting for transfers between devices: 15.8 us -> 2.33 us  [the longest x1 2.32 us: local(): queries = lax.all_to_all(q_msg, 'ha', 0, 0, axis_index_groups=NEAR)]
    ppermute x2 -> x8, starting transfers between devices: 10.5 us -> 17.9 us  [the longest x2 9.98 us: local(): other = lax.ppermute(own, 'pb', OTHER_CORE)]
    pallas_call x7 -> x11, Pallas kernels: 20.7 us -> 15.6 us  [the longest x1 6.25 us: local(): pl.pallas_call(attend_kernel, in_specs=[SMEM] + [WHOLE] * 7, out_shape=sh...]
    all_to_all x2, starting transfers between devices: 6.96 us -> 9.98 us  [the longest x1 6.49 us: gather_same_core(): return lax.all_to_all(copies, GP, 0, 0, axis_index_groups=SAME_CORE)]
    all_to_all x1, waiting for transfers between devices: 3.5 us -> 1.2 us  [local(): lax.all_to_all(gated_t.reshape(16, 16, 256), 'ha', 0, 0).reshape(256, 256)]
    all_to_all x1, blocking collectives: 11.7 us -> 13.7 us  [local(): lax.all_to_all(conv.reshape(16, 16, 256), 'ha', 0, 0).reshape(256, 256)]
  transfers between devices with their start and end apart: 5 -> 11, of which waited for: 3 -> 8; matrix products, arithmetic and copies ran while one was open for 1% -> 1% of each run, Pallas kernels for 5% -> 3%
where the time goes in v3:
time: 153 us; the launch traced here: 152 us
  blocking collectives  56.1 us (37%)
  starting transfers between devices  37.9 us (25%)
  waiting for transfers between devices  23.9 us (16%)
  Pallas kernels  23.2 us (15%)
  local copies, waits for them, and re-layouts  9.52 us (6%)
    all_to_all x1, blocking collectives, local(): got = lax.all_to_all(partial, 'ha', 0, 0, axis_index_groups=NEAR)  22.1 us
    all_to_all x1, blocking collectives, gather_same_core(): return lax.all_to_all(copies, GP, 0, 0, axis_index_groups=SAME_CORE)  20.3 us
    ppermute x2, waiting for transfers between devices, trade(): lax.ppermute(theirs, 'ha', XQ_FLIP)  15.3 us
    all_to_all x1, blocking collectives, local(): lax.all_to_all(conv.reshape(16, 16, 256), 'ha', 0, 0).reshape(256, 256)  13.7 us
    all_to_all x1, starting transfers between devices, local(): lax.all_to_all(gated_t.reshape(16, 16, 256), 'ha', 0, 0).reshape(256, 256)  10 us
    ppermute x2, starting transfers between devices, local(): other = lax.ppermute(own, 'pb', OTHER_CORE)  9.98 us
    unnamed x32, local copies, waits for them, and re-layouts  9.52 us
    all_to_all x1, starting transfers between devices, gather_same_core(): return lax.all_to_all(copies, GP, 0, 0, axis_index_groups=SAME_CORE)  6.49 us
  transfers between devices with their start and end apart: 11, of which 8 were waited for; matrix products, arithmetic and copies ran while one was open for 1% of the time, Pallas kernels for 3%

profile of v3, /device:TPU:1, one launch (start us, length us, event | category | flops | bytes accessed | tf_op | source)
XLA Modules:
  0.0 152.3 jit_solution(8886291208330409042)
XLA Ops:
  0.6 0.0 copy-start.4
  0.6 1.0 copy-done.4
  1.6 0.8 gate.1
  2.4 10.0 %all-to-all-start = ((bf16[16,16,256]{2,1,0:T(8,128)(2,1)}), bf16[16,16,256]{2,1,0:T(8,128)(2,1)S(1)}, u32[]{:S(2)}, u32[]{:S(2)}) async-start(bf16[16,16,256]{2,1,0:T(8,128)(2,1)} %bitcast.4), calls=%async_computation | async-start | bytes 262144 | tf_op jit(solution)/shard_map/all_to_all | solution.py:388
  12.5 0.5 multiply_cosine_fusion
  13.0 0.0 copy-start.3
  13.0 1.4 copy-done.3
  14.4 0.0 copy-start.5
  14.4 1.0 copy-done.5
  15.4 1.2 copy-done.6
  16.7 1.3 prepare.1
  18.0 0.0 copy-start.10
  18.0 0.0 copy-start.12
  18.0 0.1 maximum_bitcast_fusion
  18.1 0.0 copy-start.15
  18.1 0.5 copy-done.10
  18.6 0.1 copy-done.12
  18.7 1.2 all-to-all-done
  19.9 0.7 copy-done.7
  20.5 0.0 copy-done.2
  20.5 0.9 copy-done.8
  21.4 3.1 %convolve.1 = (bf16[256,256]{1,0:T(8,128)(2,1)S(1)}, f32[2,512,128]{2,1,0:T(8,128)S(1)}) custom-call(bf16[256,256]{1,0:T(8,128)(2,1)S(1)} %bitcast.21, f32[4,512,128]{2,1,0:T(8,128)S(1)} %get-tuple-element.24.prep_ref, bf16[3328,256]{1,0:T(8,128)(2,1)S(1)} %copy-done.2, f32[2,256,128]{2,1,0:T(8,128)S(1)} %pad_maximum_fusion.after_ref.turn_ref), custom_call_target="tpu_custom_call" | custom-call | tf_op jit(solution)/shard_map/convolve/pallas_call | solution.py:396
  24.6 0.0 copy-start.9
  24.6 13.7 %all_to_all.30 = bf16[16,16,256]{2,1,0:T(8,128)(2,1)S(1)} all-to-all(bf16[16,16,256]{2,1,0:T(8,128)(2,1)S(1)} %bitcast.23), channel_id=1, replica_groups=mesh['grp'=2,'pb'=8,'ha'=16] {'ha'}, dimensions={0} | all-to-all | bytes 262144 | tf_op jit(solution)/shard_map/all_to_all | solution.py:403
  38.3 0.0 copy-done.15
  38.3 0.0 copy-done.11
  38.3 0.0 copy-done.13
  38.3 1.2 hyena.1
  39.5 6.5 %all-to-all-start.2 = ((bf16[8,256,256]{2,1,0:T(8,128)(2,1)}), bf16[8,256,256]{2,1,0:T(8,128)(2,1)S(1)}, u32[]{:S(2)}, u32[]{:S(2)}) async-start(bf16[8,256,256]{2,1,0:T(8,128)(2,1)} %get-tuple-element.28), calls=%async_computation.2 | async-start | bytes 2097152 | tf_op jit(solution)/shard_map/all_to_all | solution.py:375
  46.0 0.1 pad_add_fusion.place_ref
  46.1 0.0 copy-done.9
  46.1 0.6 pick.1
  46.7 1.5 %collective-permute-start = (bf16[2,256,128]{2,1,0:T(8,128)(2,1)S(1)}, bf16[2,256,128]{2,1,0:T(8,128)(2,1)S(1)}, u32[]{:S(2)}, u32[]{:S(2)}) collective-permute-start(bf16[2,256,128]{2,1,0:T(8,128)(2,1)S(1)} %get-tuple-element.37.refs_0_), channel_id=1, source_target_pairs={{0,7},{1,6},{2,5},{3,4},{4,3},{5,2},{6,1},{7,0},{8,15},{9,14},{10,... | collective-permute-start | bytes 393224 | tf_op jit(solution)/shard_map/ppermute | solution.py:364
  48.2 1.0 collective-permute-start.2
  49.2 1.4 collective-permute-start.1
  50.6 1.2 collective-permute-done.refs_1_
  51.8 8.3 %collective-permute-done.2.refs_3_ = bf16[2,256,128]{2,1,0:T(8,128)(2,1)S(1)} collective-permute-done((bf16[2,256,128]{2,1,0:T(8,128)(2,1)S(1)}, bf16[2,256,128]{2,1,0:T(8,128)(2,1)S(1)}, u32[]{:S(2)}, u32[]{:S(2)}) %collective-permute-start.2) | collective-permute-done | bytes 131104 | tf_op jit(solution)/shard_map/ppermute | solution.py:366
  60.1 0.0 collective-permute-done.1.refs_2_
  60.1 0.0 all-to-all-done.2.after_ref.own_ref
  60.1 6.1 %collective-permute-start.3 = (bf16[8,256,256]{2,1,0:T(8,128)(2,1)S(1)}, bf16[8,256,256]{2,1,0:T(8,128)(2,1)S(1)}, u32[]{:S(2)}, u32[]{:S(2)}) collective-permute-start(bf16[8,256,256]{2,1,0:T(8,128)(2,1)S(1)} %all-to-all-done.2.after_ref.own_ref), channel_id=1, source_target_pairs={{0,16},{16,0},{32,48},{48,32},{64,80},{80,64},{96,112},{112,96},{1... | collective-permute-start | bytes 3145736 | tf_op jit(solution)/shard_map/ppermute | solution.py:421
  66.2 1.5 %restore.1 = (f32[2,16,4096]{2,1,0:T(8,128)}, f32[8,128]{1,0:T(8,128)S(1)}) custom-call(f32[2,512,128]{2,1,0:T(8,128)S(1)} %get-tuple-element.33.tiles_ref, bf16[8,256,256]{2,1,0:T(8,128)(2,1)S(1)} %all-to-all-done.2.after_ref.own_ref), custom_call_target="tpu_custom_call" | custom-call | tf_op jit(solution)/shard_map/restore/pallas_call | solution.py:422
  67.8 0.7 collective-permute-done.3.other_ref
  68.5 0.0 copy-done.14
  68.5 2.8 %copy-done.1 = bf16[4096,3,256]{2,0,1:T(8,128)(2,1)S(1)} copy-done((bf16[4096,3,256]{2,0,1:T(8,128)(2,1)S(1)}, bf16[4096,3,256]{2,0,1:T(8,128)(2,1)}, u32[]{:S(2)}) %copy-start.1) | copy-done | bytes 6291480
  71.3 4.4 %project.1 = (f32[256,256]{1,0:T(8,128)S(1)}, f32[256,128]{1,0:T(8,128)S(1)}, bf16[2,256,128]{2,1,0:T(8,128)(2,1)S(1)}, bf16[2,256,128]{2,1,0:T(8,128)(2,1)S(1)}) custom-call(s32[4]{0:T(128)S(1)} %pad_add_fusion.place_ref, bf16[8,256,256]{2,1,0:T(8,128)(2,1)S(1)} %all-to-all-done.2.after_ref.own_ref, ...), custom_call_target="tpu_custom_call" | custom-call | tf_op jit(solution)/shard_map/project/pallas_call | solution.py:431
  75.8 0.9 queries.1
  76.7 3.5 %all-to-all-start.3 = ((bf16[8,256,128]{2,1,0:T(8,128)(2,1)}), bf16[8,256,128]{2,1,0:T(8,128)(2,1)S(1)}, u32[]{:S(2)}, u32[]{:S(2)}) async-start(bf16[8,256,128]{2,1,0:T(8,128)(2,1)} %queries.1), calls=%async_computation.3 | async-start | bytes 1048576 | tf_op jit(solution)/shard_map/all_to_all | solution.py:466
  80.2 1.5 %collective-permute-start.4 = (bf16[2,256,128]{2,1,0:T(8,128)(2,1)S(1)}, bf16[2,256,128]{2,1,0:T(8,128)(2,1)S(1)}, u32[]{:S(2)}, u32[]{:S(2)}) collective-permute-start(bf16[2,256,128]{2,1,0:T(8,128)(2,1)S(1)} %get-tuple-element.43.rest_0_), channel_id=1, source_target_pairs={{0,7},{1,6},{2,5},{3,4},{4,3},{5,2},{6,1},{7,0},{8,15},{9,14},{10,... | collective-permute-start | bytes 393224 | tf_op jit(solution)/shard_map/ppermute | solution.py:364
  81.7 2.2 %collective-permute-start.6 = (bf16[2,256,128]{2,1,0:T(8,128)(2,1)S(1)}, bf16[2,256,128]{2,1,0:T(8,128)(2,1)S(1)}, u32[]{:S(2)}, u32[]{:S(2)}) collective-permute-start(bf16[2,256,128]{2,1,0:T(8,128)(2,1)S(1)} %get-tuple-element.44), channel_id=1, source_target_pairs={{0,15},{1,14},{2,13},{3,12},{4,11},{5,10},{6,9},{7,8},{8,7},{9,6},... | collective-permute-start | bytes 393224 | tf_op jit(solution)/shard_map/ppermute | solution.py:366
  84.0 0.2 collective-permute-start.5
  84.2 0.1 stage.1
  84.3 1.9 %collective-permute-done.4.rest_1_ = bf16[2,256,128]{2,1,0:T(8,128)(2,1)S(1)} collective-permute-done((bf16[2,256,128]{2,1,0:T(8,128)(2,1)S(1)}, bf16[2,256,128]{2,1,0:T(8,128)(2,1)S(1)}, u32[]{:S(2)}, u32[]{:S(2)}) %collective-permute-start.4) | collective-permute-done | bytes 131104 | tf_op jit(solution)/shard_map/ppermute | solution.py:364
  86.2 7.0 %collective-permute-done.6.rest_3_ = bf16[2,256,128]{2,1,0:T(8,128)(2,1)S(1)} collective-permute-done((bf16[2,256,128]{2,1,0:T(8,128)(2,1)S(1)}, bf16[2,256,128]{2,1,0:T(8,128)(2,1)S(1)}, u32[]{:S(2)}, u32[]{:S(2)}) %collective-permute-start.6) | collective-permute-done | bytes 131104 | tf_op jit(solution)/shard_map/ppermute | solution.py:366
  93.2 0.0 collective-permute-done.5.rest_2_
  93.2 2.3 %all-to-all-done.3.q_ref = bf16[8,256,128]{2,1,0:T(8,128)(2,1)S(1)} async-done(((bf16[8,256,128]{2,1,0:T(8,128)(2,1)}), bf16[8,256,128]{2,1,0:T(8,128)(2,1)S(1)}, u32[]{:S(2)}, u32[]{:S(2)}) %all-to-all-start.3) | async-done | bytes 524320 | tf_op jit(solution)/shard_map/all_to_all | solution.py:466
  95.5 6.3 %attend.1 = bf16[8,144,256]{2,1,0:T(8,128)(2,1)S(1)} custom-call(s32[4]{0:T(128)S(1)} %pad_add_fusion.place_ref, bf16[8,256,128]{2,1,0:T(8,128)(2,1)S(1)} %all-to-all-done.3.q_ref, bf16[1024,128]{1,0:T(8,128)(2,1)S(1)} %get-tuple-element.41.keys_ref, bf16[128,1024]{1,0:T(8,128)(2,1)S(1)} %get-tuple-element.42.values_ref, ...), custom_call_target="tpu_custom_call" | custom-call | tf_op jit(solution)/shard_map/attend/pallas_call | solution.py:470
  101.8 22.1 %all_to_all.31.got_ref = bf16[8,144,256]{2,1,0:T(8,128)(2,1)S(1)} all-to-all(bf16[8,144,256]{2,1,0:T(8,128)(2,1)S(1)} %attend.1), channel_id=1, replica_groups={{0,1,2,3,8,9,10,11},{7,6,5,4,15,14,13,12},{16,17,18,19,24,25,26,27},{23..., dimensions={0} | all-to-all | bytes 1179648 | tf_op jit(solution)/shard_map/all_to_all | solution.py:478
  123.9 0.3 combine.1
  124.2 20.3 %all_to_all.32.own_ref = bf16[8,256,256]{2,1,0:T(8,128)(2,1)S(1)} all-to-all(bf16[8,256,256]{2,1,0:T(8,128)(2,1)S(1)} %combine.1), channel_id=1, replica_groups={{0,32,64,96,128,160,192,224},{16,48,80,112,144,176,208,240},{1,33,65,97..., dimensions={0} | all-to-all | bytes 2097152 | tf_op jit(solution)/shard_map/all_to_all | solution.py:375
  144.5 3.8 %collective-permute-start.7 = (bf16[8,256,256]{2,1,0:T(8,128)(2,1)S(1)}, bf16[8,256,256]{2,1,0:T(8,128)(2,1)S(1)}, u32[]{:S(2)}, u32[]{:S(2)}) collective-permute-start(bf16[8,256,256]{2,1,0:T(8,128)(2,1)S(1)} %all_to_all.32.own_ref), channel_id=1, source_target_pairs={{0,16},{16,0},{32,48},{48,32},{64,80},{80,64},{96,112},{112,96},{1... | collective-permute-start | bytes 3145736 | tf_op jit(solution)/shard_map/ppermute | solution.py:483
  148.3 0.0 copy-done
  148.3 1.0 output_own.1.part_ref
  149.3 1.3 collective-permute-done.7.other_ref
  150.6 1.6 %output.1 = bf16[256,256]{1,0:T(8,128)(2,1)} custom-call(s32[4]{0:T(128)S(1)} %pad_add_fusion.place_ref, bf16[8,256,256]{2,1,0:T(8,128)(2,1)S(1)} %collective-permute-done.7.other_ref, bf16[16,256,256]{2,1,0:T(8,128)(2,1)S(1)} %bitcast.19, f32[256,256]{1,0:T(8,128)S(1)} %output_own.1.part_ref), custom_call_target="tpu_custom_call" | custom-call | tf_op jit(solution)/shard_map/output/pallas_call | solution.py:492
  (12 shorter events, 0.0 us)
Async XLA Ops:
  0.6 1.0 copy-start.4
  2.4 17.5 %all-to-all-start = ((bf16[16,16,256]{2,1,0:T(8,128)(2,1)}), bf16[16,16,256]{2,1,0:T(8,128)(2,1)S(1)}, u32[]{:S(2)}, u32[]{:S(2)}) async-start(bf16[16,16,256]{2,1,0:T(8,128)(2,1)} %bitcast.4), calls=%async_computation | async-start | bytes 262144 | tf_op jit(solution)/shard_map/all_to_all | solution.py:388
  13.0 1.4 copy-start.3
  14.4 1.0 copy-start.5
  15.4 1.2 copy-start.6
  16.7 3.9 %copy-start.2 = (bf16[3328,256]{1,0:T(8,128)(2,1)S(1)}, bf16[3328,256]{1,0:T(8,128)(2,1)}, u32[]{:S(2)}) copy-start(bf16[3328,256]{1,0:T(8,128)(2,1)} %constant.66.clone.table_ref) | copy-start | bytes 5111812
  18.0 0.6 copy-start.10
  18.0 0.7 copy-start.12
  18.1 20.2 %copy-start.15 = (f32[256]{0:T(256)S(1)}, f32[256]{0:T(256)}, u32[]{:S(2)}) copy-start(f32[256]{0:T(256)} %param.10) | copy-start | bytes 3076
  19.9 0.7 copy-start.7
  20.5 0.9 copy-start.8
  21.4 16.9 %copy-start.11 = (bf16[256,256]{1,0:T(8,128)(2,1)S(1)}, bf16[256,256]{1,0:T(8,128)(2,1)}, u32[]{:S(2)}) copy-start(bf16[256,256]{1,0:T(8,128)(2,1)} %copy-done.10) | copy-start | bytes 393220
  21.4 16.9 %copy-start.13 = (bf16[256,256]{1,0:T(8,128)(2,1)S(1)}, bf16[256,256]{1,0:T(8,128)(2,1)}, u32[]{:S(2)}) copy-start(bf16[256,256]{1,0:T(8,128)(2,1)} %copy-done.12) | copy-start | bytes 393220
  24.6 21.5 %copy-start.9 = (bf16[2,256,256]{2,1,0:T(8,128)(2,1)S(1)}, bf16[2,256,256]{2,1,0:T(8,128)(2,1)}, u32[]{:S(2)}) copy-start(bf16[2,256,256]{2,1,0:T(8,128)(2,1)} %cache_ref.1) | copy-start | bytes 786436
  39.5 29.0 %copy-start.14 = (f32[4096]{0:T(1024)S(1)}, f32[4096]{0:T(1024)}, u32[]{:S(2)}) copy-start(f32[4096]{0:T(1024)} %param.14) | copy-start | bytes 49156
  39.5 20.6 %all-to-all-start.2 = ((bf16[8,256,256]{2,1,0:T(8,128)(2,1)}), bf16[8,256,256]{2,1,0:T(8,128)(2,1)S(1)}, u32[]{:S(2)}, u32[]{:S(2)}) async-start(bf16[8,256,256]{2,1,0:T(8,128)(2,1)} %get-tuple-element.28), calls=%async_computation.2 | async-start | bytes 2097152 | tf_op jit(solution)/shard_map/all_to_all | solution.py:375
  46.7 5.1 %collective-permute-start = (bf16[2,256,128]{2,1,0:T(8,128)(2,1)S(1)}, bf16[2,256,128]{2,1,0:T(8,128)(2,1)S(1)}, u32[]{:S(2)}, u32[]{:S(2)}) collective-permute-start(bf16[2,256,128]{2,1,0:T(8,128)(2,1)S(1)} %get-tuple-element.37.refs_0_), channel_id=1, source_target_pairs={{0,7},{1,6},{2,5},{3,4},{4,3},{5,2},{6,1},{7,0},{8,15},{9,14},{10,... | collective-permute-start | bytes 393224 | tf_op jit(solution)/shard_map/ppermute | solution.py:364
  48.2 11.9 %collective-permute-start.2 = (bf16[2,256,128]{2,1,0:T(8,128)(2,1)S(1)}, bf16[2,256,128]{2,1,0:T(8,128)(2,1)S(1)}, u32[]{:S(2)}, u32[]{:S(2)}) collective-permute-start(bf16[2,256,128]{2,1,0:T(8,128)(2,1)S(1)} %get-tuple-element.31), channel_id=1, source_target_pairs={{0,15},{1,14},{2,13},{3,12},{4,11},{5,10},{6,9},{7,8},{8,7},{9,6},... | collective-permute-start | bytes 393224 | tf_op jit(solution)/shard_map/ppermute | solution.py:366
  49.2 10.9 %collective-permute-start.1 = (bf16[2,256,128]{2,1,0:T(8,128)(2,1)S(1)}, bf16[2,256,128]{2,1,0:T(8,128)(2,1)S(1)}, u32[]{:S(2)}, u32[]{:S(2)}) collective-permute-start(bf16[2,256,128]{2,1,0:T(8,128)(2,1)S(1)} %get-tuple-element.31), channel_id=1, source_target_pairs={{0,8},{1,9},{2,10},{3,11},{4,12},{5,13},{6,14},{7,15},{8,0},{9,1},... | collective-permute-start | bytes 393224 | tf_op jit(solution)/shard_map/ppermute | solution.py:365
  60.1 8.4 %collective-permute-start.3 = (bf16[8,256,256]{2,1,0:T(8,128)(2,1)S(1)}, bf16[8,256,256]{2,1,0:T(8,128)(2,1)S(1)}, u32[]{:S(2)}, u32[]{:S(2)}) collective-permute-start(bf16[8,256,256]{2,1,0:T(8,128)(2,1)S(1)} %all-to-all-done.2.after_ref.own_ref), channel_id=1, source_target_pairs={{0,16},{16,0},{32,48},{48,32},{64,80},{80,64},{96,112},{112,96},{1... | collective-permute-start | bytes 3145736 | tf_op jit(solution)/shard_map/ppermute | solution.py:421
  68.5 2.8 %copy-start.1 = (bf16[4096,3,256]{2,0,1:T(8,128)(2,1)S(1)}, bf16[4096,3,256]{2,0,1:T(8,128)(2,1)}, u32[]{:S(2)}) copy-start(bf16[4096,3,256]{2,0,1:T(8,128)(2,1)} %param.15) | copy-start | bytes 18874372
  76.7 18.8 %all-to-all-start.3 = ((bf16[8,256,128]{2,1,0:T(8,128)(2,1)}), bf16[8,256,128]{2,1,0:T(8,128)(2,1)S(1)}, u32[]{:S(2)}, u32[]{:S(2)}) async-start(bf16[8,256,128]{2,1,0:T(8,128)(2,1)} %queries.1), calls=%async_computation.3 | async-start | bytes 1048576 | tf_op jit(solution)/shard_map/all_to_all | solution.py:466
  80.2 6.0 %collective-permute-start.4 = (bf16[2,256,128]{2,1,0:T(8,128)(2,1)S(1)}, bf16[2,256,128]{2,1,0:T(8,128)(2,1)S(1)}, u32[]{:S(2)}, u32[]{:S(2)}) collective-permute-start(bf16[2,256,128]{2,1,0:T(8,128)(2,1)S(1)} %get-tuple-element.43.rest_0_), channel_id=1, source_target_pairs={{0,7},{1,6},{2,5},{3,4},{4,3},{5,2},{6,1},{7,0},{8,15},{9,14},{10,... | collective-permute-start | bytes 393224 | tf_op jit(solution)/shard_map/ppermute | solution.py:364
  81.7 11.5 %collective-permute-start.6 = (bf16[2,256,128]{2,1,0:T(8,128)(2,1)S(1)}, bf16[2,256,128]{2,1,0:T(8,128)(2,1)S(1)}, u32[]{:S(2)}, u32[]{:S(2)}) collective-permute-start(bf16[2,256,128]{2,1,0:T(8,128)(2,1)S(1)} %get-tuple-element.44), channel_id=1, source_target_pairs={{0,15},{1,14},{2,13},{3,12},{4,11},{5,10},{6,9},{7,8},{8,7},{9,6},... | collective-permute-start | bytes 393224 | tf_op jit(solution)/shard_map/ppermute | solution.py:366
  84.0 9.2 %collective-permute-start.5 = (bf16[2,256,128]{2,1,0:T(8,128)(2,1)S(1)}, bf16[2,256,128]{2,1,0:T(8,128)(2,1)S(1)}, u32[]{:S(2)}, u32[]{:S(2)}) collective-permute-start(bf16[2,256,128]{2,1,0:T(8,128)(2,1)S(1)} %get-tuple-element.44), channel_id=1, source_target_pairs={{0,8},{1,9},{2,10},{3,11},{4,12},{5,13},{6,14},{7,15},{8,0},{9,1},... | collective-permute-start | bytes 393224 | tf_op jit(solution)/shard_map/ppermute | solution.py:365
  123.9 24.4 %copy-start = (bf16[4096,256]{1,0:T(8,128)(2,1)S(1)}, bf16[4096,256]{1,0:T(8,128)(2,1)}, u32[]{:S(2)}) copy-start(bf16[4096,256]{1,0:T(8,128)(2,1)} %param.16) | copy-start | bytes 6291460
  144.5 6.1 %collective-permute-start.7 = (bf16[8,256,256]{2,1,0:T(8,128)(2,1)S(1)}, bf16[8,256,256]{2,1,0:T(8,128)(2,1)S(1)}, u32[]{:S(2)}, u32[]{:S(2)}) collective-permute-start(bf16[8,256,256]{2,1,0:T(8,128)(2,1)S(1)} %all_to_all.32.own_ref), channel_id=1, source_target_pairs={{0,16},{16,0},{32,48},{48,32},{64,80},{80,64},{96,112},{112,96},{1... | collective-permute-start | bytes 3145736 | tf_op jit(solution)/shard_map/ppermute | solution.py:483

commit v4 on v3

--- a/solution.py
+++ b/solution.py
@@ -123,7 +123,7 @@
     out_ref[1] = from_tiles(tiles_ref[1])
 
 
-def conv_kernel(x_ref, prep_ref, table_ref, after_ref, conv_ref, spec_ref):
+def conv_kernel(x_ref, prep_ref, table_ref, conv_ref, spec_ref):
     x = x_ref[...]
     channel = lax.broadcasted_iota(jnp.int32, (2, 16, 32, 256), 1)
     lane = lax.broadcasted_iota(jnp.int32, (2, 16, 32, 256), 3)
@@ -188,48 +188,36 @@
     return values * cos + pltpu.roll(values, 64, 1) * sin
 
 
-def qkv_kernel(
-    place_ref, own_ref, other_ref, w_ref, gain_ref, turn_ref, token_ref,
-    q_ref, scale_ref, mine_ref, theirs_ref, acc_ref, square_ref,
-):
-    step = pl.program_id(0)
-    own_head, core = place_ref[0], place_ref[3]
-
-    @pl.when(step == 0)
-    def _():
-        acc_ref[...] = jnp.zeros_like(acc_ref)
-        square_ref[...] = jnp.zeros_like(square_ref)
-
-    a, b = own_ref[0].astype(F32), other_ref[0].astype(F32)
-    square_ref[...] += a * a + b * b
-    a = (a * gain_ref[2 * step + core]).astype(BF)
-    b = (b * gain_ref[2 * step + 1 - core]).astype(BF)
-    for part in range(3):
-        acc_ref[part] += mul(a, w_ref[part, 0, core]) + mul(b, w_ref[part, 0, 1 - core])
-
-    @pl.when(step == 7)
-    def _():
-        scale = lax.rsqrt(jnp.sum(square_ref[...], axis=1, keepdims=True) / 4096.0 + 1e-05)
-        cos, sin = turn_ref[0], turn_ref[1]
-        q_ref[...] = acc_ref[0]
-        scale_ref[...] = jnp.broadcast_to(scale, (256, 128))
-        first = own_head == 0
-        for slot in range(2):
-            low, high = (acc_ref[slot + 1, :, 128 * h : 128 * h + 128] * scale for h in range(2))
-            mine = jnp.where(first, low, high)
-            theirs = jnp.where(first, high, low)
-            if slot == 0:
-                mine = rotated(mine, cos, sin)
-                theirs = rotated(theirs, cos, sin)
-            mine_ref[slot] = mine.astype(BF)
-            theirs_ref[slot] = theirs.astype(BF)
-
-
-def queries_kernel(raw_ref, scale_ref, turn_ref, q_ref):
+def scale_kernel(place_ref, own_ref, other_ref, gain_ref, token_ref, x_ref, scale_ref):
+    core = place_ref[3]
+    square = jnp.zeros((256, 256), F32)
+    for s in range(8):
+        for ref, which in ((own_ref, core), (other_ref, 1 - core)):
+            x = ref[s].astype(F32)
+            square = square + x * x
+            place = 2 * s + which
+            x_ref[:, pl.ds(pl.multiple_of(place * 256, 256), 256)] = (x * gain_ref[place]).astype(BF)
+    scale = lax.rsqrt(jnp.sum(square, axis=1, keepdims=True) / 4096.0 + 1e-05)
+    scale_ref[...] = jnp.broadcast_to(scale, (256, 128))
+
+
+def qkv_kernel(place_ref, x_ref, scale_ref, w_ref, turn_ref, q_ref, mine_ref, theirs_ref):
+    first = place_ref[0] == 0
+    cos, sin = turn_ref[0], turn_ref[1]
+    for slot in range(2):
+        part = mul(x_ref[...], w_ref[slot + 1])
+        low, high = (part[:, 128 * h : 128 * h + 128] * scale_ref[...] for h in range(2))
+        mine = jnp.where(first, low, high)
+        theirs = jnp.where(first, high, low)
+        if slot == 0:
+            mine = rotated(mine, cos, sin)
+            theirs = rotated(theirs, cos, sin)
+        mine_ref[slot] = mine.astype(BF)
+        theirs_ref[slot] = theirs.astype(BF)
+    part = mul(x_ref[...], w_ref[0])
     scale = scale_ref[...] * (math.log2(math.e) / math.sqrt(HEAD))
     for h in range(2):
-        q = raw_ref[:, 128 * h : 128 * h + 128] * scale
-        q = rotated(q, turn_ref[0], turn_ref[1]).astype(BF)
+        q = rotated(part[:, 128 * h : 128 * h + 128] * scale, cos, sin).astype(BF)
         for dest in range(4):
             q_ref[4 * h + dest] = q
 
@@ -386,7 +374,6 @@
         gate_kernel, out_shape=shape(256, 256), name="gate", compiler_params=params(4)
     )(hyena_proj)
     columns = lax.all_to_all(gated_t.reshape(16, 16, 256), "ha", 0, 0).reshape(256, 256)
-    turn = rotation(256, ha_index)
     prep, outer, gated = pl.pallas_call(
         prepare_kernel,
         out_shape=(shape(4, 512, 128, dtype=F32), shape(256, 256), shape(256, 256)),
@@ -396,10 +383,9 @@
     conv, tiles = pl.pallas_call(
         conv_kernel,
         out_shape=(shape(256, 256), shape(2, 512, 128, dtype=F32)),
-        in_specs=[WHOLE] * 3 + [FAR],
         name="convolve",
         compiler_params=params(24),
-    )(columns, prep, jnp.asarray(tables()), turn)
+    )(columns, prep, jnp.asarray(tables()))
     conv = lax.all_to_all(conv.reshape(16, 16, 256), "ha", 0, 0).reshape(256, 256)
     copies, hyena_out = pl.pallas_call(
         hyena_kernel,
@@ -417,7 +403,7 @@
         name="pick",
         compiler_params=params(4),
     )(place, cache_kv, hyena_out)
-    own, old = lax.optimization_barrier((own, trade(mine, theirs)))
+    own, old, turn = lax.optimization_barrier((own, trade(mine, theirs), rotation(256, ha_index)))
     other = lax.ppermute(own, "pb", OTHER_CORE)
     block_spectrum, token = pl.pallas_call(
         restore_kernel,
@@ -426,43 +412,21 @@
         name="restore",
         compiler_params=params(8),
     )(tiles, own)
-    block = pl.BlockSpec((1, 256, 256), lambda s: (s, 0, 0))
-    trio = lambda *dims: pl.BlockSpec(dims, lambda s: (0,) * len(dims))
-    raw, scale, mine, theirs = pl.pallas_call(
+    scaled, scale = pl.pallas_call(
+        scale_kernel,
+        in_specs=[SMEM] + [WHOLE] * 3 + [FAR],
+        out_shape=(shape(256, 4096), shape(256, 128, dtype=F32)),
+        name="scale",
+        compiler_params=params(8),
+    )(place, own, other, norm_gain.reshape(16, 1, 256), token)
+    q_msg, mine, theirs = pl.pallas_call(
         qkv_kernel,
-        grid=(8,),
-        in_specs=[
-            SMEM,
-            block,
-            block,
-            pl.BlockSpec((3, 1, 2, 256, 256), lambda s: (0, s, 0, 0, 0)),
-            trio(16, 1, 256),
-            trio(2, 256, 128),
-            FAR,
-        ],
-        out_specs=(trio(256, 256), trio(256, 128), trio(2, 256, 128), trio(2, 256, 128)),
-        out_shape=(
-            shape(256, 256, dtype=F32),
-            shape(256, 128, dtype=F32),
-            shape(2, 256, 128),
-            shape(2, 256, 128),
-        ),
-        scratch_shapes=[pltpu.VMEM((3, 256, 256), F32), pltpu.VMEM((256, 256), F32)],
+        in_specs=[SMEM] + [WHOLE] * 4,
+        out_shape=(shape(8, 256, 128), shape(2, 256, 128), shape(2, 256, 128)),
         name="project",
         compiler_params=params(16),
-    )(
-        place,
-        own,
-        other,
-        jnp.transpose(w_qkv, (1, 0, 2)).reshape(3, 8, 2, 256, 256),
-        norm_gain.reshape(16, 1, 256),
-        turn,
-        token,
-    )
+    )(place, scaled, scale, jnp.transpose(w_qkv, (1, 0, 2)), turn)
     new = trade(mine, theirs)
-    q_msg = pl.pallas_call(
-        queries_kernel, out_shape=shape(8, 256, 128), name="queries", compiler_params=params(4)
-    )(raw, scale, turn)
     queries = lax.all_to_all(q_msg, "ha", 0, 0, axis_index_groups=NEAR)
     keys, values = pl.pallas_call(
         stage_kernel, out_shape=(shape(1024, 128), shape(128, 1024)), name="stage", compiler_params=params(8)

time: 153 us -> 150 us (0.980)
    ppermute x2, waiting for transfers between devices: 15.3 us -> 7.16 us  [trade(): lax.ppermute(theirs, 'ha', XQ_FLIP)]
    ppermute x2, waiting for transfers between devices: 3.08 us -> 9.9 us  [trade(): lax.ppermute(mine, 'ha', Q_FLIP)]
    unnamed x32 -> x24, local copies, waits for them, and re-layouts: 9.52 us -> 8.2 us
where the time goes in v4:
time: 150 us; the launch traced here: 149 us
  blocking collectives  54.7 us (36%)
  starting transfers between devices  38.5 us (26%)
  waiting for transfers between devices  23.9 us (16%)
  Pallas kernels  22.5 us (15%)
  local copies, waits for them, and re-layouts  8.2 us (5%)
    all_to_all x1, blocking collectives, local(): got = lax.all_to_all(partial, 'ha', 0, 0, axis_index_groups=NEAR)  22.1 us
    all_to_all x1, blocking collectives, gather_same_core(): return lax.all_to_all(copies, GP, 0, 0, axis_index_groups=SAME_CORE)  19.6 us
    all_to_all x1, blocking collectives, local(): lax.all_to_all(conv.reshape(16, 16, 256), 'ha', 0, 0).reshape(256, 256)  13.1 us
    ppermute x2, starting transfers between devices, local(): other = lax.ppermute(own, 'pb', OTHER_CORE)  10.7 us
    all_to_all x1, starting transfers between devices, local(): lax.all_to_all(gated_t.reshape(16, 16, 256), 'ha', 0, 0).reshape(256, 256)  10 us
    ppermute x2, waiting for transfers between devices, trade(): lax.ppermute(mine, 'ha', Q_FLIP)  9.9 us
    unnamed x24, local copies, waits for them, and re-layouts  8.2 us
    ppermute x2, waiting for transfers between devices, trade(): lax.ppermute(theirs, 'ha', XQ_FLIP)  7.16 us
  transfers between devices with their start and end apart: 11, of which 8 were waited for; matrix products, arithmetic and copies ran while one was open for 1% of the time, Pallas kernels for 3%

profile of v4, /device:TPU:1, one launch (start us, length us, event | category | flops | bytes accessed | tf_op | source)
XLA Modules:
  0.0 149.4 jit_solution(7661152796723369652)
XLA Ops:
  0.6 0.0 copy-start.2
  0.6 0.0 copy-start.4
  0.7 1.1 copy-done.4
  1.8 0.8 gate.1
  2.5 10.0 %all-to-all-start = ((bf16[16,16,256]{2,1,0:T(8,128)(2,1)}), bf16[16,16,256]{2,1,0:T(8,128)(2,1)S(1)}, u32[]{:S(2)}, u32[]{:S(2)}) async-start(bf16[16,16,256]{2,1,0:T(8,128)(2,1)} %bitcast.4), calls=%async_computation | async-start | bytes 262144 | tf_op jit(solution)/shard_map/all_to_all | solution.py:376
  12.6 0.0 copy-start.3
  12.6 1.4 copy-done.3
  14.0 0.0 copy-start.5
  14.0 1.0 copy-done.5
  15.0 0.0 copy-start.6
  15.0 1.2 copy-done.6
  16.2 1.3 prepare.1
  17.5 0.0 copy-start.8
  17.5 0.6 copy-done.8
  18.2 0.0 copy-start.11
  18.2 1.8 %all-to-all-done = bf16[16,16,256]{2,1,0:T(8,128)(2,1)S(1)} async-done(((bf16[16,16,256]{2,1,0:T(8,128)(2,1)}), bf16[16,16,256]{2,1,0:T(8,128)(2,1)S(1)}, u32[]{:S(2)}, u32[]{:S(2)}) %all-to-all-start) | async-done | bytes 131104 | tf_op jit(solution)/shard_map/all_to_all | solution.py:376
  20.0 0.0 copy-start.9
  20.0 0.0 copy-done.2
  20.0 3.1 %convolve.1 = (bf16[256,256]{1,0:T(8,128)(2,1)S(1)}, f32[2,512,128]{2,1,0:T(8,128)S(1)}) custom-call(bf16[256,256]{1,0:T(8,128)(2,1)S(1)} %bitcast.19, f32[4,512,128]{2,1,0:T(8,128)S(1)} %get-tuple-element.26.prep_ref, bf16[3328,256]{1,0:T(8,128)(2,1)S(1)} %copy-done.2), custom_call_target="tpu_custom_call" | custom-call | tf_op jit(solution)/shard_map/convolve/pallas_call | solution.py:383
  23.2 0.0 copy-start.7
  23.2 13.1 %all_to_all.30 = bf16[16,16,256]{2,1,0:T(8,128)(2,1)S(1)} all-to-all(bf16[16,16,256]{2,1,0:T(8,128)(2,1)S(1)} %bitcast.21), channel_id=1, replica_groups=mesh['grp'=2,'pb'=8,'ha'=16] {'ha'}, dimensions={0} | all-to-all | bytes 262144 | tf_op jit(solution)/shard_map/all_to_all | solution.py:389
  36.3 0.0 copy-done.11
  36.3 0.0 copy-done.9
  36.3 1.2 hyena.1
  37.4 6.4 %all-to-all-start.2 = ((bf16[8,256,256]{2,1,0:T(8,128)(2,1)}), bf16[8,256,256]{2,1,0:T(8,128)(2,1)S(1)}, u32[]{:S(2)}, u32[]{:S(2)}) async-start(bf16[8,256,256]{2,1,0:T(8,128)(2,1)} %get-tuple-element.30), calls=%async_computation.2 | async-start | bytes 2097152 | tf_op jit(solution)/shard_map/all_to_all | solution.py:363
  43.8 0.0 copy-start.10
  43.9 0.1 pad_add_fusion.place_ref
  44.0 0.5 multiply_cosine_fusion
  44.5 0.0 copy-done.7
  44.5 0.6 pick.1
  45.1 1.3 collective-permute-start.2
  46.4 1.4 collective-permute-start.1
  47.8 1.2 collective-permute-start
  49.1 0.1 maximum_bitcast_fusion
  49.2 8.0 %collective-permute-done.refs_1_ = bf16[2,256,128]{2,1,0:T(8,128)(2,1)S(1)} collective-permute-done((bf16[2,256,128]{2,1,0:T(8,128)(2,1)S(1)}, bf16[2,256,128]{2,1,0:T(8,128)(2,1)S(1)}, u32[]{:S(2)}, u32[]{:S(2)}) %collective-permute-start) | collective-permute-done | bytes 131104 | tf_op jit(solution)/shard_map/ppermute | solution.py:352
  57.2 0.0 collective-permute-done.2.refs_3_
  57.2 0.7 collective-permute-done.1.refs_2_
  57.9 0.0 all-to-all-done.2.after_ref.own_ref
  57.9 6.8 %collective-permute-start.3 = (bf16[8,256,256]{2,1,0:T(8,128)(2,1)S(1)}, bf16[8,256,256]{2,1,0:T(8,128)(2,1)S(1)}, u32[]{:S(2)}, u32[]{:S(2)}) collective-permute-start(bf16[8,256,256]{2,1,0:T(8,128)(2,1)S(1)} %all-to-all-done.2.after_ref.own_ref), channel_id=1, source_target_pairs={{0,16},{16,0},{32,48},{48,32},{64,80},{80,64},{96,112},{112,96},{1... | collective-permute-start | bytes 3145736 | tf_op jit(solution)/shard_map/ppermute | solution.py:407
  64.8 1.5 %restore.1 = (f32[2,16,4096]{2,1,0:T(8,128)}, f32[8,128]{1,0:T(8,128)S(1)}) custom-call(f32[2,512,128]{2,1,0:T(8,128)S(1)} %get-tuple-element.35.tiles_ref, bf16[8,256,256]{2,1,0:T(8,128)(2,1)S(1)} %all-to-all-done.2.after_ref.own_ref), custom_call_target="tpu_custom_call" | custom-call | tf_op jit(solution)/shard_map/restore/pallas_call | solution.py:408
  66.3 0.7 collective-permute-done.3.other_ref
  67.0 0.0 copy-done.10
  67.1 1.5 %scale.1 = (bf16[256,4096]{1,0:T(8,128)(2,1)S(1)}, f32[256,128]{1,0:T(8,128)S(1)}) custom-call(s32[4]{0:T(128)S(1)} %pad_add_fusion.place_ref, bf16[8,256,256]{2,1,0:T(8,128)(2,1)S(1)} %all-to-all-done.2.after_ref.own_ref, bf16[8,256,256]{2,1,0:T(8,128)(2,1)S(1)} %collective-permute-done.3.other_ref, f32[16,1,256]{2,1,0:T(1,128)S(1)} %bitcast.22, ...), custom_call_target="tpu_custom_call" | custom-call | tf_op jit(solution)/shard_map/scale/pallas_call | solution.py:415
  68.6 0.0 copy-start.1
  68.6 2.8 %copy-done.1 = bf16[4096,3,256]{2,0,1:T(8,128)(2,1)S(1)} copy-done((bf16[4096,3,256]{2,0,1:T(8,128)(2,1)S(1)}, bf16[4096,3,256]{2,0,1:T(8,128)(2,1)}, u32[]{:S(2)}) %copy-start.1) | copy-done | bytes 6291480
  71.3 3.2 %project.1 = (bf16[8,256,128]{2,1,0:T(8,128)(2,1)}, bf16[2,256,128]{2,1,0:T(8,128)(2,1)S(1)}, bf16[2,256,128]{2,1,0:T(8,128)(2,1)S(1)}) custom-call(s32[4]{0:T(128)S(1)} %pad_add_fusion.place_ref, bf16[256,4096]{1,0:T(8,128)(2,1)S(1)} %get-tuple-element.37.x_ref, f32[256,128]{1,0:T(8,128)S(1)} %get-tuple-element.38.scale_ref, ...), custom_call_target="tpu_custom_call" | custom-call | tf_op jit(solution)/shard_map/project/pallas_call | solution.py:422
  74.5 3.5 %all-to-all-start.3 = ((bf16[8,256,128]{2,1,0:T(8,128)(2,1)}), bf16[8,256,128]{2,1,0:T(8,128)(2,1)S(1)}, u32[]{:S(2)}, u32[]{:S(2)}) async-start(bf16[8,256,128]{2,1,0:T(8,128)(2,1)} %get-tuple-element.40), calls=%async_computation.3 | async-start | bytes 1048576 | tf_op jit(solution)/shard_map/all_to_all | solution.py:430
  78.0 1.5 %collective-permute-start.4 = (bf16[2,256,128]{2,1,0:T(8,128)(2,1)S(1)}, bf16[2,256,128]{2,1,0:T(8,128)(2,1)S(1)}, u32[]{:S(2)}, u32[]{:S(2)}) collective-permute-start(bf16[2,256,128]{2,1,0:T(8,128)(2,1)S(1)} %get-tuple-element.47.rest_0_), channel_id=1, source_target_pairs={{0,7},{1,6},{2,5},{3,4},{4,3},{5,2},{6,1},{7,0},{8,15},{9,14},{10,... | collective-permute-start | bytes 393224 | tf_op jit(solution)/shard_map/ppermute | solution.py:352
  79.6 2.2 %collective-permute-start.6 = (bf16[2,256,128]{2,1,0:T(8,128)(2,1)S(1)}, bf16[2,256,128]{2,1,0:T(8,128)(2,1)S(1)}, u32[]{:S(2)}, u32[]{:S(2)}) collective-permute-start(bf16[2,256,128]{2,1,0:T(8,128)(2,1)S(1)} %get-tuple-element.48), channel_id=1, source_target_pairs={{0,15},{1,14},{2,13},{3,12},{4,11},{5,10},{6,9},{7,8},{8,7},{9,6},... | collective-permute-start | bytes 393224 | tf_op jit(solution)/shard_map/ppermute | solution.py:354
  81.8 0.2 collective-permute-start.5
  82.0 0.1 stage.1
  82.1 1.9 %collective-permute-done.4.rest_1_ = bf16[2,256,128]{2,1,0:T(8,128)(2,1)S(1)} collective-permute-done((bf16[2,256,128]{2,1,0:T(8,128)(2,1)S(1)}, bf16[2,256,128]{2,1,0:T(8,128)(2,1)S(1)}, u32[]{:S(2)}, u32[]{:S(2)}) %collective-permute-start.4) | collective-permute-done | bytes 131104 | tf_op jit(solution)/shard_map/ppermute | solution.py:352
  84.1 7.2 %collective-permute-done.6.rest_3_ = bf16[2,256,128]{2,1,0:T(8,128)(2,1)S(1)} collective-permute-done((bf16[2,256,128]{2,1,0:T(8,128)(2,1)S(1)}, bf16[2,256,128]{2,1,0:T(8,128)(2,1)S(1)}, u32[]{:S(2)}, u32[]{:S(2)}) %collective-permute-start.6) | collective-permute-done | bytes 131104 | tf_op jit(solution)/shard_map/ppermute | solution.py:354
  91.2 0.0 collective-permute-done.5.rest_2_
  91.2 2.2 %all-to-all-done.3.q_ref = bf16[8,256,128]{2,1,0:T(8,128)(2,1)S(1)} async-done(((bf16[8,256,128]{2,1,0:T(8,128)(2,1)}), bf16[8,256,128]{2,1,0:T(8,128)(2,1)S(1)}, u32[]{:S(2)}, u32[]{:S(2)}) %all-to-all-start.3) | async-done | bytes 524320 | tf_op jit(solution)/shard_map/all_to_all | solution.py:430
  93.4 6.3 %attend.1 = bf16[8,144,256]{2,1,0:T(8,128)(2,1)S(1)} custom-call(s32[4]{0:T(128)S(1)} %pad_add_fusion.place_ref, bf16[8,256,128]{2,1,0:T(8,128)(2,1)S(1)} %all-to-all-done.3.q_ref, bf16[1024,128]{1,0:T(8,128)(2,1)S(1)} %get-tuple-element.45.keys_ref, bf16[128,1024]{1,0:T(8,128)(2,1)S(1)} %get-tuple-element.46.values_ref, ...), custom_call_target="tpu_custom_call" | custom-call | tf_op jit(solution)/shard_map/attend/pallas_call | solution.py:434
  99.7 22.1 %all_to_all.31.got_ref = bf16[8,144,256]{2,1,0:T(8,128)(2,1)S(1)} all-to-all(bf16[8,144,256]{2,1,0:T(8,128)(2,1)S(1)} %attend.1), channel_id=1, replica_groups={{0,1,2,3,8,9,10,11},{7,6,5,4,15,14,13,12},{16,17,18,19,24,25,26,27},{23..., dimensions={0} | all-to-all | bytes 1179648 | tf_op jit(solution)/shard_map/all_to_all | solution.py:442
  121.7 0.3 combine.1
  122.0 19.6 %all_to_all.32.own_ref = bf16[8,256,256]{2,1,0:T(8,128)(2,1)S(1)} all-to-all(bf16[8,256,256]{2,1,0:T(8,128)(2,1)S(1)} %combine.1), channel_id=1, replica_groups={{0,32,64,96,128,160,192,224},{16,48,80,112,144,176,208,240},{1,33,65,97..., dimensions={0} | all-to-all | bytes 2097152 | tf_op jit(solution)/shard_map/all_to_all | solution.py:363
  141.6 3.8 %collective-permute-start.7 = (bf16[8,256,256]{2,1,0:T(8,128)(2,1)S(1)}, bf16[8,256,256]{2,1,0:T(8,128)(2,1)S(1)}, u32[]{:S(2)}, u32[]{:S(2)}) collective-permute-start(bf16[8,256,256]{2,1,0:T(8,128)(2,1)S(1)} %all_to_all.32.own_ref), channel_id=1, source_target_pairs={{0,16},{16,0},{32,48},{48,32},{64,80},{80,64},{96,112},{112,96},{1... | collective-permute-start | bytes 3145736 | tf_op jit(solution)/shard_map/ppermute | solution.py:447
  145.5 0.0 copy-done
  145.5 1.0 output_own.1.part_ref
  146.5 1.3 collective-permute-done.7.other_ref
  147.7 1.6 %output.1 = bf16[256,256]{1,0:T(8,128)(2,1)} custom-call(s32[4]{0:T(128)S(1)} %pad_add_fusion.place_ref, bf16[8,256,256]{2,1,0:T(8,128)(2,1)S(1)} %collective-permute-done.7.other_ref, bf16[16,256,256]{2,1,0:T(8,128)(2,1)S(1)} %bitcast.17, f32[256,256]{1,0:T(8,128)S(1)} %output_own.1.part_ref), custom_call_target="tpu_custom_call" | custom-call | tf_op jit(solution)/shard_map/output/pallas_call | solution.py:456
  (4 shorter events, 0.0 us)
Async XLA Ops:
  0.6 19.4 %copy-start.2 = (bf16[3328,256]{1,0:T(8,128)(2,1)S(1)}, bf16[3328,256]{1,0:T(8,128)(2,1)}, u32[]{:S(2)}) copy-start(bf16[3328,256]{1,0:T(8,128)(2,1)} %constant.66.clone.table_ref) | copy-start | bytes 5111812
  0.6 1.1 copy-start.4
  2.5 17.5 %all-to-all-start = ((bf16[16,16,256]{2,1,0:T(8,128)(2,1)}), bf16[16,16,256]{2,1,0:T(8,128)(2,1)S(1)}, u32[]{:S(2)}, u32[]{:S(2)}) async-start(bf16[16,16,256]{2,1,0:T(8,128)(2,1)} %bitcast.4), calls=%async_computation | async-start | bytes 262144 | tf_op jit(solution)/shard_map/all_to_all | solution.py:376
  12.6 1.4 copy-start.3
  14.0 1.0 copy-start.5
  15.0 1.2 copy-start.6
  17.5 0.7 copy-start.8
  18.2 18.1 %copy-start.11 = (f32[256]{0:T(256)S(1)}, f32[256]{0:T(256)}, u32[]{:S(2)}) copy-start(f32[256]{0:T(256)} %param.10) | copy-start | bytes 3076
  20.0 16.2 %copy-start.9 = (bf16[256,256]{1,0:T(8,128)(2,1)S(1)}, bf16[256,256]{1,0:T(8,128)(2,1)}, u32[]{:S(2)}) copy-start(bf16[256,256]{1,0:T(8,128)(2,1)} %copy-done.8) | copy-start | bytes 393220
  23.2 21.3 %copy-start.7 = (bf16[2,256,256]{2,1,0:T(8,128)(2,1)S(1)}, bf16[2,256,256]{2,1,0:T(8,128)(2,1)}, u32[]{:S(2)}) copy-start(bf16[2,256,256]{2,1,0:T(8,128)(2,1)} %cache_ref.1) | copy-start | bytes 786436
  37.4 20.5 %all-to-all-start.2 = ((bf16[8,256,256]{2,1,0:T(8,128)(2,1)}), bf16[8,256,256]{2,1,0:T(8,128)(2,1)S(1)}, u32[]{:S(2)}, u32[]{:S(2)}) async-start(bf16[8,256,256]{2,1,0:T(8,128)(2,1)} %get-tuple-element.30), calls=%async_computation.2 | async-start | bytes 2097152 | tf_op jit(solution)/shard_map/all_to_all | solution.py:363
  43.8 23.3 %copy-start.10 = (f32[4096]{0:T(1024)S(1)}, f32[4096]{0:T(1024)}, u32[]{:S(2)}) copy-start(f32[4096]{0:T(1024)} %param.14) | copy-start | bytes 49156
  45.1 12.1 %collective-permute-start.2 = (bf16[2,256,128]{2,1,0:T(8,128)(2,1)S(1)}, bf16[2,256,128]{2,1,0:T(8,128)(2,1)S(1)}, u32[]{:S(2)}, u32[]{:S(2)}) collective-permute-start(bf16[2,256,128]{2,1,0:T(8,128)(2,1)S(1)} %get-tuple-element.33), channel_id=1, source_target_pairs={{0,15},{1,14},{2,13},{3,12},{4,11},{5,10},{6,9},{7,8},{8,7},{9,6},... | collective-permute-start | bytes 393224 | tf_op jit(solution)/shard_map/ppermute | solution.py:354
  46.4 11.6 %collective-permute-start.1 = (bf16[2,256,128]{2,1,0:T(8,128)(2,1)S(1)}, bf16[2,256,128]{2,1,0:T(8,128)(2,1)S(1)}, u32[]{:S(2)}, u32[]{:S(2)}) collective-permute-start(bf16[2,256,128]{2,1,0:T(8,128)(2,1)S(1)} %get-tuple-element.33), channel_id=1, source_target_pairs={{0,8},{1,9},{2,10},{3,11},{4,12},{5,13},{6,14},{7,15},{8,0},{9,1},... | collective-permute-start | bytes 393224 | tf_op jit(solution)/shard_map/ppermute | solution.py:353
  47.8 9.4 %collective-permute-start = (bf16[2,256,128]{2,1,0:T(8,128)(2,1)S(1)}, bf16[2,256,128]{2,1,0:T(8,128)(2,1)S(1)}, u32[]{:S(2)}, u32[]{:S(2)}) collective-permute-start(bf16[2,256,128]{2,1,0:T(8,128)(2,1)S(1)} %get-tuple-element.41.refs_0_), channel_id=1, source_target_pairs={{0,7},{1,6},{2,5},{3,4},{4,3},{5,2},{6,1},{7,0},{8,15},{9,14},{10,... | collective-permute-start | bytes 393224 | tf_op jit(solution)/shard_map/ppermute | solution.py:352
  57.9 9.1 %collective-permute-start.3 = (bf16[8,256,256]{2,1,0:T(8,128)(2,1)S(1)}, bf16[8,256,256]{2,1,0:T(8,128)(2,1)S(1)}, u32[]{:S(2)}, u32[]{:S(2)}) collective-permute-start(bf16[8,256,256]{2,1,0:T(8,128)(2,1)S(1)} %all-to-all-done.2.after_ref.own_ref), channel_id=1, source_target_pairs={{0,16},{16,0},{32,48},{48,32},{64,80},{80,64},{96,112},{112,96},{1... | collective-permute-start | bytes 3145736 | tf_op jit(solution)/shard_map/ppermute | solution.py:407
  68.6 2.8 %copy-start.1 = (bf16[4096,3,256]{2,0,1:T(8,128)(2,1)S(1)}, bf16[4096,3,256]{2,0,1:T(8,128)(2,1)}, u32[]{:S(2)}) copy-start(bf16[4096,3,256]{2,0,1:T(8,128)(2,1)} %param.15) | copy-start | bytes 18874372
  74.5 18.9 %all-to-all-start.3 = ((bf16[8,256,128]{2,1,0:T(8,128)(2,1)}), bf16[8,256,128]{2,1,0:T(8,128)(2,1)S(1)}, u32[]{:S(2)}, u32[]{:S(2)}) async-start(bf16[8,256,128]{2,1,0:T(8,128)(2,1)} %get-tuple-element.40), calls=%async_computation.3 | async-start | bytes 1048576 | tf_op jit(solution)/shard_map/all_to_all | solution.py:430
  78.0 6.0 %collective-permute-start.4 = (bf16[2,256,128]{2,1,0:T(8,128)(2,1)S(1)}, bf16[2,256,128]{2,1,0:T(8,128)(2,1)S(1)}, u32[]{:S(2)}, u32[]{:S(2)}) collective-permute-start(bf16[2,256,128]{2,1,0:T(8,128)(2,1)S(1)} %get-tuple-element.47.rest_0_), channel_id=1, source_target_pairs={{0,7},{1,6},{2,5},{3,4},{4,3},{5,2},{6,1},{7,0},{8,15},{9,14},{10,... | collective-permute-start | bytes 393224 | tf_op jit(solution)/shard_map/ppermute | solution.py:352
  79.6 11.7 %collective-permute-start.6 = (bf16[2,256,128]{2,1,0:T(8,128)(2,1)S(1)}, bf16[2,256,128]{2,1,0:T(8,128)(2,1)S(1)}, u32[]{:S(2)}, u32[]{:S(2)}) collective-permute-start(bf16[2,256,128]{2,1,0:T(8,128)(2,1)S(1)} %get-tuple-element.48), channel_id=1, source_target_pairs={{0,15},{1,14},{2,13},{3,12},{4,11},{5,10},{6,9},{7,8},{8,7},{9,6},... | collective-permute-start | bytes 393224 | tf_op jit(solution)/shard_map/ppermute | solution.py:354
  81.8 9.4 %collective-permute-start.5 = (bf16[2,256,128]{2,1,0:T(8,128)(2,1)S(1)}, bf16[2,256,128]{2,1,0:T(8,128)(2,1)S(1)}, u32[]{:S(2)}, u32[]{:S(2)}) collective-permute-start(bf16[2,256,128]{2,1,0:T(8,128)(2,1)S(1)} %get-tuple-element.48), channel_id=1, source_target_pairs={{0,8},{1,9},{2,10},{3,11},{4,12},{5,13},{6,14},{7,15},{8,0},{9,1},... | collective-permute-start | bytes 393224 | tf_op jit(solution)/shard_map/ppermute | solution.py:353
  121.7 23.7 %copy-start = (bf16[4096,256]{1,0:T(8,128)(2,1)S(1)}, bf16[4096,256]{1,0:T(8,128)(2,1)}, u32[]{:S(2)}) copy-start(bf16[4096,256]{1,0:T(8,128)(2,1)} %param.16) | copy-start | bytes 6291460
  141.6 6.1 %collective-permute-start.7 = (bf16[8,256,256]{2,1,0:T(8,128)(2,1)S(1)}, bf16[8,256,256]{2,1,0:T(8,128)(2,1)S(1)}, u32[]{:S(2)}, u32[]{:S(2)}) collective-permute-start(bf16[8,256,256]{2,1,0:T(8,128)(2,1)S(1)} %all_to_all.32.own_ref), channel_id=1, source_target_pairs={{0,16},{16,0},{32,48},{48,32},{64,80},{80,64},{96,112},{112,96},{1... | collective-permute-start | bytes 3145736 | tf_op jit(solution)/shard_map/ppermute | solution.py:447

commit v5 on v4

--- a/solution.py
+++ b/solution.py
@@ -117,8 +117,10 @@
     out_ref[3] = to_tiles(imag) * weight
 
 
-def restore_kernel(tiles_ref, after_ref, out_ref, token_ref):
+def restore_kernel(tiles_ref, cache_ref, far_ref, after_ref, out_ref, token_ref, pack_ref):
     token_ref[...] = jnp.zeros_like(token_ref)
+    pack_ref[:2] = cache_ref[2:]
+    pack_ref[2:] = far_ref[2:]
     out_ref[0] = from_tiles(tiles_ref[0])
     out_ref[1] = from_tiles(tiles_ref[1])
 
@@ -178,10 +180,10 @@
         out_ref[copy] = value
 
 
-def pick_kernel(place_ref, cache_ref, after_ref, mine_ref, theirs_ref):
+def pick_kernel(place_ref, cache_ref, after_ref, out_ref):
     own = place_ref[0]
-    for ref, head in ((mine_ref, own), (theirs_ref, 1 - own)):
-        ref[...] = cache_ref[:, :, pl.ds(pl.multiple_of(head * HEAD, HEAD), HEAD)]
+    for n, head in enumerate((own, 1 - own)):
+        out_ref[2 * n : 2 * n + 2] = cache_ref[:, :, pl.ds(pl.multiple_of(head * HEAD, HEAD), HEAD)]
 
 
 def rotated(values, cos, sin):
@@ -222,11 +224,11 @@
             q_ref[4 * h + dest] = q
 
 
-def stage_kernel(*refs):
-    keys_ref, values_ref = refs[4:]
-    for n, piece in enumerate(refs[:4]):
-        keys_ref[256 * n : 256 * n + 256] = piece[0]
-        values_ref[:, 256 * n : 256 * n + 256] = piece[1].astype(F32).T.astype(BF)
+def stage_kernel(cache_ref, far_ref, across_ref, keys_ref, values_ref):
+    pieces = ((cache_ref, 0), (far_ref, 0), (across_ref, 0), (across_ref, 2))
+    for n, (ref, at) in enumerate(pieces):
+        keys_ref[256 * n : 256 * n + 256] = ref[at]
+        values_ref[:, 256 * n : 256 * n + 256] = ref[at + 1].astype(F32).T.astype(BF)
 
 
 def attend_kernel(place_ref, q_ref, keys_ref, values_ref, *rest):
@@ -396,22 +398,25 @@
     )(conv, gated, outer, dskip.reshape(1, 256))
 
     own = gather_same_core(copies)
-    mine, theirs = pl.pallas_call(
+    cache = pl.pallas_call(
         pick_kernel,
         in_specs=[SMEM, WHOLE, FAR],
-        out_shape=(shape(2, 256, 128), shape(2, 256, 128)),
+        out_shape=shape(4, 256, 128),
         name="pick",
         compiler_params=params(4),
     )(place, cache_kv, hyena_out)
-    own, old, turn = lax.optimization_barrier((own, trade(mine, theirs), rotation(256, ha_index)))
+    own, far, turn = lax.optimization_barrier(
+        (own, lax.ppermute(cache, "ha", Q_FLIP), rotation(256, ha_index))
+    )
     other = lax.ppermute(own, "pb", OTHER_CORE)
-    block_spectrum, token = pl.pallas_call(
+    block_spectrum, token, pack = pl.pallas_call(
         restore_kernel,
-        in_specs=[WHOLE, FAR],
-        out_shape=(shape(2, 16, 4096, dtype=F32), shape(8, 128, dtype=F32)),
+        in_specs=[WHOLE] * 3 + [FAR],
+        out_shape=(shape(2, 16, 4096, dtype=F32), shape(8, 128, dtype=F32), shape(4, 256, 128)),
         name="restore",
         compiler_params=params(8),
-    )(tiles, own)
+    )(tiles, cache, far, own)
+    across = lax.ppermute(pack, "ha", X_FLIP)
     scaled, scale = pl.pallas_call(
         scale_kernel,
         in_specs=[SMEM] + [WHOLE] * 3 + [FAR],
@@ -430,7 +435,7 @@
     queries = lax.all_to_all(q_msg, "ha", 0, 0, axis_index_groups=NEAR)
     keys, values = pl.pallas_call(
         stage_kernel, out_shape=(shape(1024, 128), shape(128, 1024)), name="stage", compiler_params=params(8)
-    )(*old)
+    )(cache, far, across)
     partial = pl.pallas_call(
         attend_kernel,
         in_specs=[SMEM] + [WHOLE] * 7,

time: 150 us -> 148 us (0.987)
  starting transfers between devices: 38.5 us -> 33.5 us
  waiting for transfers between devices: 23.9 us -> 28.4 us
    ppermute x0 -> x2, waiting for transfers between devices: none -> 17.2 us  [the longest x1 11.1 us: local(): lax.ppermute(cache, 'ha', Q_FLIP)]
    ppermute x2 -> x1, waiting for transfers between devices: 9.9 us -> 0.01 us  [trade(): lax.ppermute(mine, 'ha', Q_FLIP)]
    ppermute x2 -> x1, waiting for transfers between devices: 7.16 us -> 2.88 us  [trade(): lax.ppermute(theirs, 'ha', XQ_FLIP)]
    ppermute x2, starting transfers between devices: 10.7 us -> 6.88 us  [local(): other = lax.ppermute(own, 'pb', OTHER_CORE)]
    ppermute x2 -> x1, waiting for transfers between devices: 0.75 us -> 4.46 us  [trade(): lax.ppermute(theirs, 'ha', X_FLIP)]
    ppermute x0 -> x2, starting transfers between devices: none -> 2.91 us  [the longest x1 1.53 us: local(): lax.ppermute(cache, 'ha', Q_FLIP)]
    ppermute x2 -> x1, starting transfers between devices: 3.51 us -> 1.12 us  [trade(): lax.ppermute(theirs, 'ha', XQ_FLIP)]
    all_to_all x1, waiting for transfers between devices: 2.17 us -> 0.01 us  [local(): queries = lax.all_to_all(q_msg, 'ha', 0, 0, axis_index_groups=NEAR)]
  transfers between devices with their start and end apart: 11 -> 10, of which waited for: 8 -> 7; matrix products, arithmetic and copies ran while one was open for 1% -> 1% of each run, Pallas kernels for 3% -> 3%
where the time goes in v5:
time: 148 us; the launch traced here: 147 us
  blocking collectives  53.3 us (36%)
  starting transfers between devices  33.5 us (23%)
  waiting for transfers between devices  28.4 us (19%)
  Pallas kernels  22.5 us (15%)
  local copies, waits for them, and re-layouts  8.2 us (6%)
    all_to_all x1, blocking collectives, gather_same_core(): return lax.all_to_all(copies, GP, 0, 0, axis_index_groups=SAME_CORE)  20.1 us
    all_to_all x1, blocking collectives, local(): got = lax.all_to_all(partial, 'ha', 0, 0, axis_index_groups=NEAR)  20.1 us
    all_to_all x1, blocking collectives, local(): lax.all_to_all(conv.reshape(16, 16, 256), 'ha', 0, 0).reshape(256, 256)  13.1 us
    ppermute x1, waiting for transfers between devices, local(): lax.ppermute(cache, 'ha', Q_FLIP)  11.1 us
    all_to_all x1, starting transfers between devices, local(): lax.all_to_all(gated_t.reshape(16, 16, 256), 'ha', 0, 0).reshape(256, 256)  10 us
    unnamed x24, local copies, waits for them, and re-layouts  8.2 us
    ppermute x2, starting transfers between devices, local(): other = lax.ppermute(own, 'pb', OTHER_CORE)  6.88 us
    all_to_all x1, starting transfers between devices, gather_same_core(): return lax.all_to_all(copies, GP, 0, 0, axis_index_groups=SAME_CORE)  6.36 us
  transfers between devices with their start and end apart: 10, of which 7 were waited for; matrix products, arithmetic and copies ran while one was open for 1% of the time, Pallas kernels for 3%

profile of v5, /device:TPU:1, one launch (start us, length us, event | category | flops | bytes accessed | tf_op | source)
XLA Modules:
  0.0 147.5 jit_solution(3496311142536774237)
XLA Ops:
  0.6 0.0 copy-start.2
  0.6 0.0 copy-start.4
  0.7 1.1 copy-done.4
  1.8 0.8 gate.1
  2.5 10.0 %all-to-all-start = ((bf16[16,16,256]{2,1,0:T(8,128)(2,1)}), bf16[16,16,256]{2,1,0:T(8,128)(2,1)S(1)}, u32[]{:S(2)}, u32[]{:S(2)}) async-start(bf16[16,16,256]{2,1,0:T(8,128)(2,1)} %bitcast.4), calls=%async_computation | async-start | bytes 262144 | tf_op jit(solution)/shard_map/all_to_all | solution.py:378
  12.6 0.0 copy-start.3
  12.6 1.4 copy-done.3
  14.0 0.0 copy-start.5
  14.0 1.0 copy-done.5
  15.0 0.0 copy-start.6
  15.0 1.2 copy-done.6
  16.2 1.3 prepare.1
  17.5 0.0 copy-start.8
  17.5 0.6 copy-done.8
  18.2 0.0 copy-start.11
  18.2 1.8 %all-to-all-done = bf16[16,16,256]{2,1,0:T(8,128)(2,1)S(1)} async-done(((bf16[16,16,256]{2,1,0:T(8,128)(2,1)}), bf16[16,16,256]{2,1,0:T(8,128)(2,1)S(1)}, u32[]{:S(2)}, u32[]{:S(2)}) %all-to-all-start) | async-done | bytes 131104 | tf_op jit(solution)/shard_map/all_to_all | solution.py:378
  20.0 0.0 copy-start.9
  20.0 0.0 copy-done.2
  20.0 3.1 %convolve.1 = (bf16[256,256]{1,0:T(8,128)(2,1)S(1)}, f32[2,512,128]{2,1,0:T(8,128)S(1)}) custom-call(bf16[256,256]{1,0:T(8,128)(2,1)S(1)} %bitcast.19, f32[4,512,128]{2,1,0:T(8,128)S(1)} %get-tuple-element.22.prep_ref, bf16[3328,256]{1,0:T(8,128)(2,1)S(1)} %copy-done.2), custom_call_target="tpu_custom_call" | custom-call | tf_op jit(solution)/shard_map/convolve/pallas_call | solution.py:385
  23.2 0.0 copy-start.7
  23.2 13.1 %all_to_all.30 = bf16[16,16,256]{2,1,0:T(8,128)(2,1)S(1)} all-to-all(bf16[16,16,256]{2,1,0:T(8,128)(2,1)S(1)} %bitcast.21), channel_id=1, replica_groups=mesh['grp'=2,'pb'=8,'ha'=16] {'ha'}, dimensions={0} | all-to-all | bytes 262144 | tf_op jit(solution)/shard_map/all_to_all | solution.py:391
  36.3 0.0 copy-done.11
  36.3 0.0 copy-done.9
  36.3 1.2 hyena.1
  37.4 6.4 %all-to-all-start.2 = ((bf16[8,256,256]{2,1,0:T(8,128)(2,1)}), bf16[8,256,256]{2,1,0:T(8,128)(2,1)S(1)}, u32[]{:S(2)}, u32[]{:S(2)}) async-start(bf16[8,256,256]{2,1,0:T(8,128)(2,1)} %get-tuple-element.26), calls=%async_computation.2 | async-start | bytes 2097152 | tf_op jit(solution)/shard_map/all_to_all | solution.py:365
  43.8 0.1 pad_add_fusion.place_ref
  43.9 0.0 copy-done.7
  43.9 0.0 copy-start.10
  43.9 0.6 pick.1.cache_ref
  44.5 1.5 %collective-permute-start = (bf16[4,256,128]{2,1,0:T(8,128)(2,1)S(1)}, bf16[4,256,128]{2,1,0:T(8,128)(2,1)S(1)}, u32[]{:S(2)}, u32[]{:S(2)}) collective-permute-start(bf16[4,256,128]{2,1,0:T(8,128)(2,1)S(1)} %pick.1.cache_ref), channel_id=1, source_target_pairs={{0,7},{1,6},{2,5},{3,4},{4,3},{5,2},{6,1},{7,0},{8,15},{9,14},{10,... | collective-permute-start | bytes 786440 | tf_op jit(solution)/shard_map/ppermute | solution.py:409
  46.0 0.5 multiply_cosine_fusion
  46.6 0.1 maximum_bitcast_fusion
  46.7 11.1 %collective-permute-done.far_ref = bf16[4,256,128]{2,1,0:T(8,128)(2,1)S(1)} collective-permute-done((bf16[4,256,128]{2,1,0:T(8,128)(2,1)S(1)}, bf16[4,256,128]{2,1,0:T(8,128)(2,1)S(1)}, u32[]{:S(2)}, u32[]{:S(2)}) %collective-permute-start) | collective-permute-done | bytes 262176 | tf_op jit(solution)/shard_map/ppermute | solution.py:409
  57.8 0.0 all-to-all-done.2.after_ref.own_ref
  57.8 3.0 %collective-permute-start.1 = (bf16[8,256,256]{2,1,0:T(8,128)(2,1)S(1)}, bf16[8,256,256]{2,1,0:T(8,128)(2,1)S(1)}, u32[]{:S(2)}, u32[]{:S(2)}) collective-permute-start(bf16[8,256,256]{2,1,0:T(8,128)(2,1)S(1)} %all-to-all-done.2.after_ref.own_ref), channel_id=1, source_target_pairs={{0,16},{16,0},{32,48},{48,32},{64,80},{80,64},{96,112},{112,96},{1... | collective-permute-start | bytes 3145736 | tf_op jit(solution)/shard_map/ppermute | solution.py:411
  60.8 1.5 %restore.1 = (f32[2,16,4096]{2,1,0:T(8,128)}, f32[8,128]{1,0:T(8,128)S(1)}, bf16[4,256,128]{2,1,0:T(8,128)(2,1)S(1)}) custom-call(f32[2,512,128]{2,1,0:T(8,128)S(1)} %get-tuple-element.29.tiles_ref, bf16[4,256,128]{2,1,0:T(8,128)(2,1)S(1)} %pick.1.cache_ref, bf16[4,256,128]{2,1,0:T(8,128)(2,1)S(1)} %collective-permute-done.far_ref, ...), custom_call_target="tpu_custom_call" | custom-call | tf_op jit(solution)/shard_map/restore/pallas_call | solution.py:412
  62.4 0.7 collective-permute-done.1.other_ref
  63.1 0.0 copy-done.10
  63.1 1.5 %scale.1 = (bf16[256,4096]{1,0:T(8,128)(2,1)S(1)}, f32[256,128]{1,0:T(8,128)S(1)}) custom-call(s32[4]{0:T(128)S(1)} %pad_add_fusion.place_ref, bf16[8,256,256]{2,1,0:T(8,128)(2,1)S(1)} %all-to-all-done.2.after_ref.own_ref, bf16[8,256,256]{2,1,0:T(8,128)(2,1)S(1)} %collective-permute-done.1.other_ref, f32[16,1,256]{2,1,0:T(1,128)S(1)} %bitcast.22, ...), custom_call_target="tpu_custom_call" | custom-call | tf_op jit(solution)/shard_map/scale/pallas_call | solution.py:420
  64.6 0.0 copy-start.1
  64.6 2.8 %copy-done.1 = bf16[4096,3,256]{2,0,1:T(8,128)(2,1)S(1)} copy-done((bf16[4096,3,256]{2,0,1:T(8,128)(2,1)S(1)}, bf16[4096,3,256]{2,0,1:T(8,128)(2,1)}, u32[]{:S(2)}) %copy-start.1) | copy-done | bytes 6291480
  67.4 3.2 %project.1 = (bf16[8,256,128]{2,1,0:T(8,128)(2,1)}, bf16[2,256,128]{2,1,0:T(8,128)(2,1)S(1)}, bf16[2,256,128]{2,1,0:T(8,128)(2,1)S(1)}) custom-call(s32[4]{0:T(128)S(1)} %pad_add_fusion.place_ref, bf16[256,4096]{1,0:T(8,128)(2,1)S(1)} %get-tuple-element.32.x_ref, f32[256,128]{1,0:T(8,128)S(1)} %get-tuple-element.33.scale_ref, ...), custom_call_target="tpu_custom_call" | custom-call | tf_op jit(solution)/shard_map/project/pallas_call | solution.py:427
  70.6 3.5 %all-to-all-start.3 = ((bf16[8,256,128]{2,1,0:T(8,128)(2,1)}), bf16[8,256,128]{2,1,0:T(8,128)(2,1)S(1)}, u32[]{:S(2)}, u32[]{:S(2)}) async-start(bf16[8,256,128]{2,1,0:T(8,128)(2,1)} %get-tuple-element.35), calls=%async_computation.3 | async-start | bytes 1048576 | tf_op jit(solution)/shard_map/all_to_all | solution.py:435
  74.1 1.4 collective-permute-start.2
  75.5 1.4 collective-permute-start.3
  76.9 1.1 collective-permute-start.5
  78.1 1.3 collective-permute-start.4
  79.4 6.1 %collective-permute-done.2.across_ref = bf16[4,256,128]{2,1,0:T(8,128)(2,1)S(1)} collective-permute-done((bf16[4,256,128]{2,1,0:T(8,128)(2,1)S(1)}, bf16[4,256,128]{2,1,0:T(8,128)(2,1)S(1)}, u32[]{:S(2)}, u32[]{:S(2)}) %collective-permute-start.2) | collective-permute-done | bytes 262176 | tf_op jit(solution)/shard_map/ppermute | solution.py:419
  85.5 0.1 stage.1
  85.6 0.0 collective-permute-done.3.rest_1_
  85.6 2.9 %collective-permute-done.5.rest_3_ = bf16[2,256,128]{2,1,0:T(8,128)(2,1)S(1)} collective-permute-done((bf16[2,256,128]{2,1,0:T(8,128)(2,1)S(1)}, bf16[2,256,128]{2,1,0:T(8,128)(2,1)S(1)}, u32[]{:S(2)}, u32[]{:S(2)}) %collective-permute-start.5) | collective-permute-done | bytes 131104 | tf_op jit(solution)/shard_map/ppermute | solution.py:356
  88.5 4.5 %collective-permute-done.4.rest_2_ = bf16[2,256,128]{2,1,0:T(8,128)(2,1)S(1)} collective-permute-done((bf16[2,256,128]{2,1,0:T(8,128)(2,1)S(1)}, bf16[2,256,128]{2,1,0:T(8,128)(2,1)S(1)}, u32[]{:S(2)}, u32[]{:S(2)}) %collective-permute-start.4) | collective-permute-done | bytes 131104 | tf_op jit(solution)/shard_map/ppermute | solution.py:355
  93.0 0.0 all-to-all-done.3.q_ref
  93.0 6.2 %attend.1 = bf16[8,144,256]{2,1,0:T(8,128)(2,1)S(1)} custom-call(s32[4]{0:T(128)S(1)} %pad_add_fusion.place_ref, bf16[8,256,128]{2,1,0:T(8,128)(2,1)S(1)} %all-to-all-done.3.q_ref, bf16[1024,128]{1,0:T(8,128)(2,1)S(1)} %get-tuple-element.37.keys_ref, bf16[128,1024]{1,0:T(8,128)(2,1)S(1)} %get-tuple-element.38.values_ref, ...), custom_call_target="tpu_custom_call" | custom-call | tf_op jit(solution)/shard_map/attend/pallas_call | solution.py:439
  99.2 20.1 %all_to_all.31.got_ref = bf16[8,144,256]{2,1,0:T(8,128)(2,1)S(1)} all-to-all(bf16[8,144,256]{2,1,0:T(8,128)(2,1)S(1)} %attend.1), channel_id=1, replica_groups={{0,1,2,3,8,9,10,11},{7,6,5,4,15,14,13,12},{16,17,18,19,24,25,26,27},{23..., dimensions={0} | all-to-all | bytes 1179648 | tf_op jit(solution)/shard_map/all_to_all | solution.py:447
  119.3 0.0 copy-start
  119.3 0.3 combine.1
  119.6 20.1 %all_to_all.32.own_ref = bf16[8,256,256]{2,1,0:T(8,128)(2,1)S(1)} all-to-all(bf16[8,256,256]{2,1,0:T(8,128)(2,1)S(1)} %combine.1), channel_id=1, replica_groups={{0,32,64,96,128,160,192,224},{16,48,80,112,144,176,208,240},{1,33,65,97..., dimensions={0} | all-to-all | bytes 2097152 | tf_op jit(solution)/shard_map/all_to_all | solution.py:365
  139.7 3.8 %collective-permute-start.6 = (bf16[8,256,256]{2,1,0:T(8,128)(2,1)S(1)}, bf16[8,256,256]{2,1,0:T(8,128)(2,1)S(1)}, u32[]{:S(2)}, u32[]{:S(2)}) collective-permute-start(bf16[8,256,256]{2,1,0:T(8,128)(2,1)S(1)} %all_to_all.32.own_ref), channel_id=1, source_target_pairs={{0,16},{16,0},{32,48},{48,32},{64,80},{80,64},{96,112},{112,96},{1... | collective-permute-start | bytes 3145736 | tf_op jit(solution)/shard_map/ppermute | solution.py:452
  143.5 0.0 copy-done
  143.5 1.0 output_own.1.part_ref
  144.5 1.3 collective-permute-done.6.other_ref
  145.8 1.6 %output.1 = bf16[256,256]{1,0:T(8,128)(2,1)} custom-call(s32[4]{0:T(128)S(1)} %pad_add_fusion.place_ref, bf16[8,256,256]{2,1,0:T(8,128)(2,1)S(1)} %collective-permute-done.6.other_ref, bf16[16,256,256]{2,1,0:T(8,128)(2,1)S(1)} %bitcast.17, f32[256,256]{1,0:T(8,128)S(1)} %output_own.1.part_ref), custom_call_target="tpu_custom_call" | custom-call | tf_op jit(solution)/shard_map/output/pallas_call | solution.py:461
  (3 shorter events, 0.0 us)
Async XLA Ops:
  0.6 19.4 %copy-start.2 = (bf16[3328,256]{1,0:T(8,128)(2,1)S(1)}, bf16[3328,256]{1,0:T(8,128)(2,1)}, u32[]{:S(2)}) copy-start(bf16[3328,256]{1,0:T(8,128)(2,1)} %constant.66.clone.table_ref) | copy-start | bytes 5111812
  0.6 1.1 copy-start.4
  2.5 17.5 %all-to-all-start = ((bf16[16,16,256]{2,1,0:T(8,128)(2,1)}), bf16[16,16,256]{2,1,0:T(8,128)(2,1)S(1)}, u32[]{:S(2)}, u32[]{:S(2)}) async-start(bf16[16,16,256]{2,1,0:T(8,128)(2,1)} %bitcast.4), calls=%async_computation | async-start | bytes 262144 | tf_op jit(solution)/shard_map/all_to_all | solution.py:378
  12.6 1.4 copy-start.3
  14.0 1.0 copy-start.5
  15.0 1.2 copy-start.6
  17.5 0.7 copy-start.8
  18.2 18.1 %copy-start.11 = (f32[256]{0:T(256)S(1)}, f32[256]{0:T(256)}, u32[]{:S(2)}) copy-start(f32[256]{0:T(256)} %param.10) | copy-start | bytes 3076
  20.0 16.2 %copy-start.9 = (bf16[256,256]{1,0:T(8,128)(2,1)S(1)}, bf16[256,256]{1,0:T(8,128)(2,1)}, u32[]{:S(2)}) copy-start(bf16[256,256]{1,0:T(8,128)(2,1)} %copy-done.8) | copy-start | bytes 393220
  23.2 20.7 %copy-start.7 = (bf16[2,256,256]{2,1,0:T(8,128)(2,1)S(1)}, bf16[2,256,256]{2,1,0:T(8,128)(2,1)}, u32[]{:S(2)}) copy-start(bf16[2,256,256]{2,1,0:T(8,128)(2,1)} %cache_ref.1) | copy-start | bytes 786436
  37.4 20.4 %all-to-all-start.2 = ((bf16[8,256,256]{2,1,0:T(8,128)(2,1)}), bf16[8,256,256]{2,1,0:T(8,128)(2,1)S(1)}, u32[]{:S(2)}, u32[]{:S(2)}) async-start(bf16[8,256,256]{2,1,0:T(8,128)(2,1)} %get-tuple-element.26), calls=%async_computation.2 | async-start | bytes 2097152 | tf_op jit(solution)/shard_map/all_to_all | solution.py:365
  43.9 19.2 %copy-start.10 = (f32[4096]{0:T(1024)S(1)}, f32[4096]{0:T(1024)}, u32[]{:S(2)}) copy-start(f32[4096]{0:T(1024)} %param.14) | copy-start | bytes 49156
  44.5 13.3 %collective-permute-start = (bf16[4,256,128]{2,1,0:T(8,128)(2,1)S(1)}, bf16[4,256,128]{2,1,0:T(8,128)(2,1)S(1)}, u32[]{:S(2)}, u32[]{:S(2)}) collective-permute-start(bf16[4,256,128]{2,1,0:T(8,128)(2,1)S(1)} %pick.1.cache_ref), channel_id=1, source_target_pairs={{0,7},{1,6},{2,5},{3,4},{4,3},{5,2},{6,1},{7,0},{8,15},{9,14},{10,... | collective-permute-start | bytes 786440 | tf_op jit(solution)/shard_map/ppermute | solution.py:409
  57.8 5.3 %collective-permute-start.1 = (bf16[8,256,256]{2,1,0:T(8,128)(2,1)S(1)}, bf16[8,256,256]{2,1,0:T(8,128)(2,1)S(1)}, u32[]{:S(2)}, u32[]{:S(2)}) collective-permute-start(bf16[8,256,256]{2,1,0:T(8,128)(2,1)S(1)} %all-to-all-done.2.after_ref.own_ref), channel_id=1, source_target_pairs={{0,16},{16,0},{32,48},{48,32},{64,80},{80,64},{96,112},{112,96},{1... | collective-permute-start | bytes 3145736 | tf_op jit(solution)/shard_map/ppermute | solution.py:411
  64.6 2.8 %copy-start.1 = (bf16[4096,3,256]{2,0,1:T(8,128)(2,1)S(1)}, bf16[4096,3,256]{2,0,1:T(8,128)(2,1)}, u32[]{:S(2)}) copy-start(bf16[4096,3,256]{2,0,1:T(8,128)(2,1)} %param.15) | copy-start | bytes 18874372
  70.6 22.4 %all-to-all-start.3 = ((bf16[8,256,128]{2,1,0:T(8,128)(2,1)}), bf16[8,256,128]{2,1,0:T(8,128)(2,1)S(1)}, u32[]{:S(2)}, u32[]{:S(2)}) async-start(bf16[8,256,128]{2,1,0:T(8,128)(2,1)} %get-tuple-element.35), calls=%async_computation.3 | async-start | bytes 1048576 | tf_op jit(solution)/shard_map/all_to_all | solution.py:435
  74.1 11.4 %collective-permute-start.2 = (bf16[4,256,128]{2,1,0:T(8,128)(2,1)S(1)}, bf16[4,256,128]{2,1,0:T(8,128)(2,1)S(1)}, u32[]{:S(2)}, u32[]{:S(2)}) collective-permute-start(bf16[4,256,128]{2,1,0:T(8,128)(2,1)S(1)} %get-tuple-element.36), channel_id=1, source_target_pairs={{0,8},{1,9},{2,10},{3,11},{4,12},{5,13},{6,14},{7,15},{8,0},{9,1},... | collective-permute-start | bytes 786440 | tf_op jit(solution)/shard_map/ppermute | solution.py:419
  75.5 10.1 %collective-permute-start.3 = (bf16[2,256,128]{2,1,0:T(8,128)(2,1)S(1)}, bf16[2,256,128]{2,1,0:T(8,128)(2,1)S(1)}, u32[]{:S(2)}, u32[]{:S(2)}) collective-permute-start(bf16[2,256,128]{2,1,0:T(8,128)(2,1)S(1)} %get-tuple-element.39.rest_0_), channel_id=1, source_target_pairs={{0,7},{1,6},{2,5},{3,4},{4,3},{5,2},{6,1},{7,0},{8,15},{9,14},{10,... | collective-permute-start | bytes 393224 | tf_op jit(solution)/shard_map/ppermute | solution.py:354
  76.9 11.6 %collective-permute-start.5 = (bf16[2,256,128]{2,1,0:T(8,128)(2,1)S(1)}, bf16[2,256,128]{2,1,0:T(8,128)(2,1)S(1)}, u32[]{:S(2)}, u32[]{:S(2)}) collective-permute-start(bf16[2,256,128]{2,1,0:T(8,128)(2,1)S(1)} %get-tuple-element.40), channel_id=1, source_target_pairs={{0,15},{1,14},{2,13},{3,12},{4,11},{5,10},{6,9},{7,8},{8,7},{9,6},... | collective-permute-start | bytes 393224 | tf_op jit(solution)/shard_map/ppermute | solution.py:356
  78.1 14.9 %collective-permute-start.4 = (bf16[2,256,128]{2,1,0:T(8,128)(2,1)S(1)}, bf16[2,256,128]{2,1,0:T(8,128)(2,1)S(1)}, u32[]{:S(2)}, u32[]{:S(2)}) collective-permute-start(bf16[2,256,128]{2,1,0:T(8,128)(2,1)S(1)} %get-tuple-element.40), channel_id=1, source_target_pairs={{0,8},{1,9},{2,10},{3,11},{4,12},{5,13},{6,14},{7,15},{8,0},{9,1},... | collective-permute-start | bytes 393224 | tf_op jit(solution)/shard_map/ppermute | solution.py:355
  119.3 24.2 %copy-start = (bf16[4096,256]{1,0:T(8,128)(2,1)S(1)}, bf16[4096,256]{1,0:T(8,128)(2,1)}, u32[]{:S(2)}) copy-start(bf16[4096,256]{1,0:T(8,128)(2,1)} %param.16) | copy-start | bytes 6291460
  139.7 6.1 %collective-permute-start.6 = (bf16[8,256,256]{2,1,0:T(8,128)(2,1)S(1)}, bf16[8,256,256]{2,1,0:T(8,128)(2,1)S(1)}, u32[]{:S(2)}, u32[]{:S(2)}) collective-permute-start(bf16[8,256,256]{2,1,0:T(8,128)(2,1)S(1)} %all_to_all.32.own_ref), channel_id=1, source_target_pairs={{0,16},{16,0},{32,48},{48,32},{64,80},{80,64},{96,112},{112,96},{1... | collective-permute-start | bytes 3145736 | tf_op jit(solution)/shard_map/ppermute | solution.py:452

commit v6 on v5

--- a/solution.py
+++ b/solution.py
@@ -203,23 +203,25 @@
     scale_ref[...] = jnp.broadcast_to(scale, (256, 128))
 
 
-def qkv_kernel(place_ref, x_ref, scale_ref, w_ref, turn_ref, q_ref, mine_ref, theirs_ref):
+def keys_kernel(place_ref, x_ref, scale_ref, wk_ref, wv_ref, turn_ref, mine_ref, theirs_ref):
     first = place_ref[0] == 0
-    cos, sin = turn_ref[0], turn_ref[1]
-    for slot in range(2):
-        part = mul(x_ref[...], w_ref[slot + 1])
+    for slot, w_ref in enumerate((wk_ref, wv_ref)):
+        part = mul(x_ref[...], w_ref[...])
         low, high = (part[:, 128 * h : 128 * h + 128] * scale_ref[...] for h in range(2))
         mine = jnp.where(first, low, high)
         theirs = jnp.where(first, high, low)
         if slot == 0:
-            mine = rotated(mine, cos, sin)
-            theirs = rotated(theirs, cos, sin)
+            mine = rotated(mine, turn_ref[0], turn_ref[1])
+            theirs = rotated(theirs, turn_ref[0], turn_ref[1])
         mine_ref[slot] = mine.astype(BF)
         theirs_ref[slot] = theirs.astype(BF)
-    part = mul(x_ref[...], w_ref[0])
+
+
+def queries_kernel(x_ref, scale_ref, w_ref, turn_ref, after_ref, q_ref):
+    part = mul(x_ref[...], w_ref[...])
     scale = scale_ref[...] * (math.log2(math.e) / math.sqrt(HEAD))
     for h in range(2):
-        q = rotated(part[:, 128 * h : 128 * h + 128] * scale, cos, sin).astype(BF)
+        q = rotated(part[:, 128 * h : 128 * h + 128] * scale, turn_ref[0], turn_ref[1]).astype(BF)
         for dest in range(4):
             q_ref[4 * h + dest] = q
 
@@ -424,14 +426,22 @@
         name="scale",
         compiler_params=params(8),
     )(place, own, other, norm_gain.reshape(16, 1, 256), token)
-    q_msg, mine, theirs = pl.pallas_call(
-        qkv_kernel,
-        in_specs=[SMEM] + [WHOLE] * 4,
-        out_shape=(shape(8, 256, 128), shape(2, 256, 128), shape(2, 256, 128)),
-        name="project",
-        compiler_params=params(16),
-    )(place, scaled, scale, jnp.transpose(w_qkv, (1, 0, 2)), turn)
+    w_parts = jnp.transpose(w_qkv, (1, 0, 2))
+    mine, theirs = pl.pallas_call(
+        keys_kernel,
+        in_specs=[SMEM] + [WHOLE] * 5,
+        out_shape=(shape(2, 256, 128), shape(2, 256, 128)),
+        name="project_keys",
+        compiler_params=params(12),
+    )(place, scaled, scale, w_parts[1], w_parts[2], turn)
     new = trade(mine, theirs)
+    q_msg = pl.pallas_call(
+        queries_kernel,
+        in_specs=[WHOLE] * 4 + [FAR],
+        out_shape=shape(8, 256, 128),
+        name="project_queries",
+        compiler_params=params(12),
+    )(scaled, scale, w_parts[0], turn, mine)
     queries = lax.all_to_all(q_msg, "ha", 0, 0, axis_index_groups=NEAR)
     keys, values = pl.pallas_call(
         stage_kernel, out_shape=(shape(1024, 128), shape(128, 1024)), name="stage", compiler_params=params(8)

time: 148 us -> 148 us (level)
    ppermute x1, waiting for transfers between devices: 6.13 us -> 11.2 us  [local(): across = lax.ppermute(pack, 'ha', X_FLIP)]
    squeeze x0 -> x1, local copies, waits for them, and re-layouts: none -> 3.26 us  [local(): w_parts[2]]
    ppermute x1, waiting for transfers between devices: 2.88 us -> 0.01 us  [trade(): lax.ppermute(theirs, 'ha', XQ_FLIP)]
    unnamed x24 -> x22, local copies, waits for them, and re-layouts: 8.2 us -> 5.42 us
    ppermute x1, waiting for transfers between devices: 4.46 us -> 2.65 us  [trade(): lax.ppermute(theirs, 'ha', X_FLIP)]
    pallas_call x1 -> x2, Pallas kernels: 3.2 us -> 3.48 us  [the longest x1 1.89 us: local(): pl.pallas_call(keys_kernel, in_specs=[SMEM] + [WHOLE] * 5, out_shape=(sha...]
  transfers between devices with their start and end apart: 10 -> 10, of which waited for: 7 -> 5; matrix products, arithmetic and copies ran while one was open for 1% -> 3% of each run, Pallas kernels for 3% -> 3%
where the time goes in v6:
time: 148 us
  blocking collectives  52.9 us (36%)
  starting transfers between devices  33.6 us (23%)
  waiting for transfers between devices  28.1 us (19%)
  Pallas kernels  22.8 us (15%)
  local copies, waits for them, and re-layouts  8.68 us (6%)
    all_to_all x1, blocking collectives, gather_same_core(): return lax.all_to_all(copies, GP, 0, 0, axis_index_groups=SAME_CORE)  20.1 us
    all_to_all x1, blocking collectives, local(): got = lax.all_to_all(partial, 'ha', 0, 0, axis_index_groups=NEAR)  19.7 us
    all_to_all x1, blocking collectives, local(): lax.all_to_all(conv.reshape(16, 16, 256), 'ha', 0, 0).reshape(256, 256)  13.1 us
    ppermute x1, waiting for transfers between devices, local(): across = lax.ppermute(pack, 'ha', X_FLIP)  11.2 us
    ppermute x1, waiting for transfers between devices, local(): lax.ppermute(cache, 'ha', Q_FLIP)  11.1 us
    all_to_all x1, starting transfers between devices, local(): lax.all_to_all(gated_t.reshape(16, 16, 256), 'ha', 0, 0).reshape(256, 256)  10 us
    ppermute x2, starting transfers between devices, local(): other = lax.ppermute(own, 'pb', OTHER_CORE)  6.89 us
    all_to_all x1, starting transfers between devices, gather_same_core(): return lax.all_to_all(copies, GP, 0, 0, axis_index_groups=SAME_CORE)  6.36 us
  transfers between devices with their start and end apart: 10, of which 5 were waited for; matrix products, arithmetic and copies ran while one was open for 3% of the time, Pallas kernels for 3%

profile of v6, /device:TPU:1, one launch (start us, length us, event | category | flops | bytes accessed | tf_op | source)
XLA Modules:
  0.0 147.6 jit_solution(17302058174437441164)
XLA Ops:
  0.6 0.0 copy-start.1
  0.6 0.0 copy-start.3
  0.7 1.1 copy-done.3
  1.8 0.8 gate.1
  2.5 10.0 %all-to-all-start = ((bf16[16,16,256]{2,1,0:T(8,128)(2,1)}), bf16[16,16,256]{2,1,0:T(8,128)(2,1)S(1)}, u32[]{:S(2)}, u32[]{:S(2)}) async-start(bf16[16,16,256]{2,1,0:T(8,128)(2,1)} %bitcast.4), calls=%async_computation | async-start | bytes 262144 | tf_op jit(solution)/shard_map/all_to_all | solution.py:380
  12.6 0.0 copy-start.2
  12.6 1.4 copy-done.2
  14.0 0.0 copy-start.4
  14.0 1.0 copy-done.4
  15.0 0.0 copy-start.5
  15.0 1.2 copy-done.5
  16.2 1.3 prepare.1
  17.5 0.0 copy-start.7
  17.5 0.6 copy-done.7
  18.2 0.0 copy-start.10
  18.2 1.8 %all-to-all-done = bf16[16,16,256]{2,1,0:T(8,128)(2,1)S(1)} async-done(((bf16[16,16,256]{2,1,0:T(8,128)(2,1)}), bf16[16,16,256]{2,1,0:T(8,128)(2,1)S(1)}, u32[]{:S(2)}, u32[]{:S(2)}) %all-to-all-start) | async-done | bytes 131104 | tf_op jit(solution)/shard_map/all_to_all | solution.py:380
  20.0 0.0 copy-start.8
  20.0 0.0 copy-done.1
  20.0 3.1 %convolve.1 = (bf16[256,256]{1,0:T(8,128)(2,1)S(1)}, f32[2,512,128]{2,1,0:T(8,128)S(1)}) custom-call(bf16[256,256]{1,0:T(8,128)(2,1)S(1)} %bitcast.24, f32[4,512,128]{2,1,0:T(8,128)S(1)} %get-tuple-element.21.prep_ref, bf16[3328,256]{1,0:T(8,128)(2,1)S(1)} %copy-done.1), custom_call_target="tpu_custom_call" | custom-call | tf_op jit(solution)/shard_map/convolve/pallas_call | solution.py:387
  23.2 0.0 copy-start.6
  23.2 13.1 %all_to_all.30 = bf16[16,16,256]{2,1,0:T(8,128)(2,1)S(1)} all-to-all(bf16[16,16,256]{2,1,0:T(8,128)(2,1)S(1)} %bitcast.26), channel_id=1, replica_groups=mesh['grp'=2,'pb'=8,'ha'=16] {'ha'}, dimensions={0} | all-to-all | bytes 262144 | tf_op jit(solution)/shard_map/all_to_all | solution.py:393
  36.3 0.0 copy-done.10
  36.3 0.0 copy-done.8
  36.3 1.2 hyena.1
  37.4 6.4 %all-to-all-start.2 = ((bf16[8,256,256]{2,1,0:T(8,128)(2,1)}), bf16[8,256,256]{2,1,0:T(8,128)(2,1)S(1)}, u32[]{:S(2)}, u32[]{:S(2)}) async-start(bf16[8,256,256]{2,1,0:T(8,128)(2,1)} %get-tuple-element.25), calls=%async_computation.2 | async-start | bytes 2097152 | tf_op jit(solution)/shard_map/all_to_all | solution.py:367
  43.8 0.1 pad_add_fusion.place_ref
  43.9 0.0 copy-done.6
  43.9 0.6 pick.1.cache_ref
  44.5 1.5 %collective-permute-start = (bf16[4,256,128]{2,1,0:T(8,128)(2,1)S(1)}, bf16[4,256,128]{2,1,0:T(8,128)(2,1)S(1)}, u32[]{:S(2)}, u32[]{:S(2)}) collective-permute-start(bf16[4,256,128]{2,1,0:T(8,128)(2,1)S(1)} %pick.1.cache_ref), channel_id=1, source_target_pairs={{0,7},{1,6},{2,5},{3,4},{4,3},{5,2},{6,1},{7,0},{8,15},{9,14},{10,... | collective-permute-start | bytes 786440 | tf_op jit(solution)/shard_map/ppermute | solution.py:411
  46.0 0.5 multiply_cosine_fusion
  46.6 0.1 maximum_bitcast_fusion
  46.7 11.1 %collective-permute-done.far_ref = bf16[4,256,128]{2,1,0:T(8,128)(2,1)S(1)} collective-permute-done((bf16[4,256,128]{2,1,0:T(8,128)(2,1)S(1)}, bf16[4,256,128]{2,1,0:T(8,128)(2,1)S(1)}, u32[]{:S(2)}, u32[]{:S(2)}) %collective-permute-start) | collective-permute-done | bytes 262176 | tf_op jit(solution)/shard_map/ppermute | solution.py:411
  57.8 0.0 all-to-all-done.2.after_ref.own_ref
  57.8 3.0 %collective-permute-start.1 = (bf16[8,256,256]{2,1,0:T(8,128)(2,1)S(1)}, bf16[8,256,256]{2,1,0:T(8,128)(2,1)S(1)}, u32[]{:S(2)}, u32[]{:S(2)}) collective-permute-start(bf16[8,256,256]{2,1,0:T(8,128)(2,1)S(1)} %all-to-all-done.2.after_ref.own_ref), channel_id=1, source_target_pairs={{0,16},{16,0},{32,48},{48,32},{64,80},{80,64},{96,112},{112,96},{1... | collective-permute-start | bytes 3145736 | tf_op jit(solution)/shard_map/ppermute | solution.py:413
  60.8 3.3 %slice_bitcast_fusion = (bf16[4096,256]{1,0:T(8,128)(2,1)S(1)}, bf16[4096,256]{1,0:T(8,128)(2,1)S(1)}, bf16[4096,256]{1,0:T(8,128)(2,1)S(1)}) fusion(bf16[3,4096,256]{2,1,0:T(8,128)(2,1)} %bitcast.29), kind=kLoop, calls=%fused_computation | loop fusion | bytes 12582912 | tf_op jit(solution)/shard_map/squeeze | solution.py:436
  64.1 0.0 copy-start.9
  64.1 1.5 %restore.1 = (f32[2,16,4096]{2,1,0:T(8,128)}, f32[8,128]{1,0:T(8,128)S(1)}, bf16[4,256,128]{2,1,0:T(8,128)(2,1)S(1)}) custom-call(f32[2,512,128]{2,1,0:T(8,128)S(1)} %get-tuple-element.28.tiles_ref, bf16[4,256,128]{2,1,0:T(8,128)(2,1)S(1)} %pick.1.cache_ref, bf16[4,256,128]{2,1,0:T(8,128)(2,1)S(1)} %collective-permute-done.far_ref, ...), custom_call_target="tpu_custom_call" | custom-call | tf_op jit(solution)/shard_map/restore/pallas_call | solution.py:414
  65.7 0.0 collective-permute-done.1.other_ref
  65.7 0.0 copy-done.9
  65.7 1.5 %scale.1 = (bf16[256,4096]{1,0:T(8,128)(2,1)S(1)}, f32[256,128]{1,0:T(8,128)S(1)}) custom-call(s32[4]{0:T(128)S(1)} %pad_add_fusion.place_ref, bf16[8,256,256]{2,1,0:T(8,128)(2,1)S(1)} %all-to-all-done.2.after_ref.own_ref, bf16[8,256,256]{2,1,0:T(8,128)(2,1)S(1)} %collective-permute-done.1.other_ref, f32[16,1,256]{2,1,0:T(1,128)S(1)} %bitcast.27, ...), custom_call_target="tpu_custom_call" | custom-call | tf_op jit(solution)/shard_map/scale/pallas_call | solution.py:422
  67.2 1.9 %project_keys.1 = (bf16[2,256,128]{2,1,0:T(8,128)(2,1)S(1)}, bf16[2,256,128]{2,1,0:T(8,128)(2,1)S(1)}) custom-call(s32[4]{0:T(128)S(1)} %pad_add_fusion.place_ref, bf16[256,4096]{1,0:T(8,128)(2,1)S(1)} %get-tuple-element.31.x_ref, f32[256,128]{1,0:T(8,128)S(1)} %get-tuple-element.32.scale_ref, bf16[4096,256]{1,0:T(8,128)(2,1)S(1)} %get-tuple-element.41.wk_ref, ...), custom_call_target="tpu_custom_call" | custom-call | tf_op jit(solution)/shard_map/project_keys/pallas_call | solution.py:430
  69.1 1.6 %project_queries.1 = bf16[8,256,128]{2,1,0:T(8,128)(2,1)} custom-call(bf16[256,4096]{1,0:T(8,128)(2,1)S(1)} %get-tuple-element.31.x_ref, f32[256,128]{1,0:T(8,128)S(1)} %get-tuple-element.32.scale_ref, bf16[4096,256]{1,0:T(8,128)(2,1)S(1)} %get-tuple-element.42.w_ref, f32[2,256,128]{2,1,0:T(8,128)S(1)} %pad_maximum_fusion.turn_ref, ...), custom_call_target="tpu_custom_call" | custom-call | tf_op jit(solution)/shard_map/project_queries/pallas_call | solution.py:438
  70.6 3.5 %all-to-all-start.3 = ((bf16[8,256,128]{2,1,0:T(8,128)(2,1)}), bf16[8,256,128]{2,1,0:T(8,128)(2,1)S(1)}, u32[]{:S(2)}, u32[]{:S(2)}) async-start(bf16[8,256,128]{2,1,0:T(8,128)(2,1)} %project_queries.1), calls=%async_computation.3 | async-start | bytes 1048576 | tf_op jit(solution)/shard_map/all_to_all | solution.py:445
  74.1 1.4 collective-permute-start.2
  75.5 1.3 collective-permute-start.5
  76.9 1.3 collective-permute-start.4
  78.2 1.2 collective-permute-start.3
  79.4 11.2 %collective-permute-done.2.across_ref = bf16[4,256,128]{2,1,0:T(8,128)(2,1)S(1)} collective-permute-done((bf16[4,256,128]{2,1,0:T(8,128)(2,1)S(1)}, bf16[4,256,128]{2,1,0:T(8,128)(2,1)S(1)}, u32[]{:S(2)}, u32[]{:S(2)}) %collective-permute-start.2) | collective-permute-done | bytes 262176 | tf_op jit(solution)/shard_map/ppermute | solution.py:421
  90.6 0.1 stage.1
  90.8 0.0 collective-permute-done.5.rest_3_
  90.8 2.7 %collective-permute-done.4.rest_2_ = bf16[2,256,128]{2,1,0:T(8,128)(2,1)S(1)} collective-permute-done((bf16[2,256,128]{2,1,0:T(8,128)(2,1)S(1)}, bf16[2,256,128]{2,1,0:T(8,128)(2,1)S(1)}, u32[]{:S(2)}, u32[]{:S(2)}) %collective-permute-start.4) | collective-permute-done | bytes 131104 | tf_op jit(solution)/shard_map/ppermute | solution.py:357
  93.4 0.0 collective-permute-done.3.rest_1_
  93.4 0.0 all-to-all-done.3.q_ref
  93.4 6.3 %attend.1 = bf16[8,144,256]{2,1,0:T(8,128)(2,1)S(1)} custom-call(s32[4]{0:T(128)S(1)} %pad_add_fusion.place_ref, bf16[8,256,128]{2,1,0:T(8,128)(2,1)S(1)} %all-to-all-done.3.q_ref, bf16[1024,128]{1,0:T(8,128)(2,1)S(1)} %get-tuple-element.36.keys_ref, bf16[128,1024]{1,0:T(8,128)(2,1)S(1)} %get-tuple-element.37.values_ref, ...), custom_call_target="tpu_custom_call" | custom-call | tf_op jit(solution)/shard_map/attend/pallas_call | solution.py:449
  99.7 19.7 %all_to_all.31.got_ref = bf16[8,144,256]{2,1,0:T(8,128)(2,1)S(1)} all-to-all(bf16[8,144,256]{2,1,0:T(8,128)(2,1)S(1)} %attend.1), channel_id=1, replica_groups={{0,1,2,3,8,9,10,11},{7,6,5,4,15,14,13,12},{16,17,18,19,24,25,26,27},{23..., dimensions={0} | all-to-all | bytes 1179648 | tf_op jit(solution)/shard_map/all_to_all | solution.py:457
  119.4 0.0 copy-start
  119.4 0.3 combine.1
  119.7 20.1 %all_to_all.32.own_ref = bf16[8,256,256]{2,1,0:T(8,128)(2,1)S(1)} all-to-all(bf16[8,256,256]{2,1,0:T(8,128)(2,1)S(1)} %combine.1), channel_id=1, replica_groups={{0,32,64,96,128,160,192,224},{16,48,80,112,144,176,208,240},{1,33,65,97..., dimensions={0} | all-to-all | bytes 2097152 | tf_op jit(solution)/shard_map/all_to_all | solution.py:367
  139.8 3.8 %collective-permute-start.6 = (bf16[8,256,256]{2,1,0:T(8,128)(2,1)S(1)}, bf16[8,256,256]{2,1,0:T(8,128)(2,1)S(1)}, u32[]{:S(2)}, u32[]{:S(2)}) collective-permute-start(bf16[8,256,256]{2,1,0:T(8,128)(2,1)S(1)} %all_to_all.32.own_ref), channel_id=1, source_target_pairs={{0,16},{16,0},{32,48},{48,32},{64,80},{80,64},{96,112},{112,96},{1... | collective-permute-start | bytes 3145736 | tf_op jit(solution)/shard_map/ppermute | solution.py:462
  143.7 0.0 copy-done
  143.7 1.0 output_own.1.part_ref
  144.7 1.3 collective-permute-done.6.other_ref
  146.0 1.6 %output.1 = bf16[256,256]{1,0:T(8,128)(2,1)} custom-call(s32[4]{0:T(128)S(1)} %pad_add_fusion.place_ref, bf16[8,256,256]{2,1,0:T(8,128)(2,1)S(1)} %collective-permute-done.6.other_ref, bf16[16,256,256]{2,1,0:T(8,128)(2,1)S(1)} %bitcast.23, f32[256,256]{1,0:T(8,128)S(1)} %output_own.1.part_ref), custom_call_target="tpu_custom_call" | custom-call | tf_op jit(solution)/shard_map/output/pallas_call | solution.py:471
  (3 shorter events, 0.0 us)
Async XLA Ops:
  0.6 19.4 %copy-start.1 = (bf16[3328,256]{1,0:T(8,128)(2,1)S(1)}, bf16[3328,256]{1,0:T(8,128)(2,1)}, u32[]{:S(2)}) copy-start(bf16[3328,256]{1,0:T(8,128)(2,1)} %constant.66.clone.table_ref) | copy-start | bytes 5111812
  0.6 1.1 copy-start.3
  2.5 17.5 %all-to-all-start = ((bf16[16,16,256]{2,1,0:T(8,128)(2,1)}), bf16[16,16,256]{2,1,0:T(8,128)(2,1)S(1)}, u32[]{:S(2)}, u32[]{:S(2)}) async-start(bf16[16,16,256]{2,1,0:T(8,128)(2,1)} %bitcast.4), calls=%async_computation | async-start | bytes 262144 | tf_op jit(solution)/shard_map/all_to_all | solution.py:380
  12.6 1.4 copy-start.2
  14.0 1.0 copy-start.4
  15.0 1.2 copy-start.5
  17.5 0.7 copy-start.7
  18.2 18.1 %copy-start.10 = (f32[256]{0:T(256)S(1)}, f32[256]{0:T(256)}, u32[]{:S(2)}) copy-start(f32[256]{0:T(256)} %param.10) | copy-start | bytes 3076
  20.0 16.2 %copy-start.8 = (bf16[256,256]{1,0:T(8,128)(2,1)S(1)}, bf16[256,256]{1,0:T(8,128)(2,1)}, u32[]{:S(2)}) copy-start(bf16[256,256]{1,0:T(8,128)(2,1)} %copy-done.7) | copy-start | bytes 393220
  23.2 20.7 %copy-start.6 = (bf16[2,256,256]{2,1,0:T(8,128)(2,1)S(1)}, bf16[2,256,256]{2,1,0:T(8,128)(2,1)}, u32[]{:S(2)}) copy-start(bf16[2,256,256]{2,1,0:T(8,128)(2,1)} %cache_ref.1) | copy-start | bytes 786436
  37.4 20.4 %all-to-all-start.2 = ((bf16[8,256,256]{2,1,0:T(8,128)(2,1)}), bf16[8,256,256]{2,1,0:T(8,128)(2,1)S(1)}, u32[]{:S(2)}, u32[]{:S(2)}) async-start(bf16[8,256,256]{2,1,0:T(8,128)(2,1)} %get-tuple-element.25), calls=%async_computation.2 | async-start | bytes 2097152 | tf_op jit(solution)/shard_map/all_to_all | solution.py:367
  44.5 13.3 %collective-permute-start = (bf16[4,256,128]{2,1,0:T(8,128)(2,1)S(1)}, bf16[4,256,128]{2,1,0:T(8,128)(2,1)S(1)}, u32[]{:S(2)}, u32[]{:S(2)}) collective-permute-start(bf16[4,256,128]{2,1,0:T(8,128)(2,1)S(1)} %pick.1.cache_ref), channel_id=1, source_target_pairs={{0,7},{1,6},{2,5},{3,4},{4,3},{5,2},{6,1},{7,0},{8,15},{9,14},{10,... | collective-permute-start | bytes 786440 | tf_op jit(solution)/shard_map/ppermute | solution.py:411
  57.8 7.9 %collective-permute-start.1 = (bf16[8,256,256]{2,1,0:T(8,128)(2,1)S(1)}, bf16[8,256,256]{2,1,0:T(8,128)(2,1)S(1)}, u32[]{:S(2)}, u32[]{:S(2)}) collective-permute-start(bf16[8,256,256]{2,1,0:T(8,128)(2,1)S(1)} %all-to-all-done.2.after_ref.own_ref), channel_id=1, source_target_pairs={{0,16},{16,0},{32,48},{48,32},{64,80},{80,64},{96,112},{112,96},{1... | collective-permute-start | bytes 3145736 | tf_op jit(solution)/shard_map/ppermute | solution.py:413
  64.1 1.6 %copy-start.9 = (f32[4096]{0:T(1024)S(1)}, f32[4096]{0:T(1024)}, u32[]{:S(2)}) copy-start(f32[4096]{0:T(1024)} %param.14) | copy-start | bytes 49156
  70.6 22.8 %all-to-all-start.3 = ((bf16[8,256,128]{2,1,0:T(8,128)(2,1)}), bf16[8,256,128]{2,1,0:T(8,128)(2,1)S(1)}, u32[]{:S(2)}, u32[]{:S(2)}) async-start(bf16[8,256,128]{2,1,0:T(8,128)(2,1)} %project_queries.1), calls=%async_computation.3 | async-start | bytes 1048576 | tf_op jit(solution)/shard_map/all_to_all | solution.py:445
  74.1 16.5 %collective-permute-start.2 = (bf16[4,256,128]{2,1,0:T(8,128)(2,1)S(1)}, bf16[4,256,128]{2,1,0:T(8,128)(2,1)S(1)}, u32[]{:S(2)}, u32[]{:S(2)}) collective-permute-start(bf16[4,256,128]{2,1,0:T(8,128)(2,1)S(1)} %get-tuple-element.35), channel_id=1, source_target_pairs={{0,8},{1,9},{2,10},{3,11},{4,12},{5,13},{6,14},{7,15},{8,0},{9,1},... | collective-permute-start | bytes 786440 | tf_op jit(solution)/shard_map/ppermute | solution.py:421
  75.5 15.3 %collective-permute-start.5 = (bf16[2,256,128]{2,1,0:T(8,128)(2,1)S(1)}, bf16[2,256,128]{2,1,0:T(8,128)(2,1)S(1)}, u32[]{:S(2)}, u32[]{:S(2)}) collective-permute-start(bf16[2,256,128]{2,1,0:T(8,128)(2,1)S(1)} %get-tuple-element.38), channel_id=1, source_target_pairs={{0,15},{1,14},{2,13},{3,12},{4,11},{5,10},{6,9},{7,8},{8,7},{9,6},... | collective-permute-start | bytes 393224 | tf_op jit(solution)/shard_map/ppermute | solution.py:358
  76.9 16.6 %collective-permute-start.4 = (bf16[2,256,128]{2,1,0:T(8,128)(2,1)S(1)}, bf16[2,256,128]{2,1,0:T(8,128)(2,1)S(1)}, u32[]{:S(2)}, u32[]{:S(2)}) collective-permute-start(bf16[2,256,128]{2,1,0:T(8,128)(2,1)S(1)} %get-tuple-element.38), channel_id=1, source_target_pairs={{0,8},{1,9},{2,10},{3,11},{4,12},{5,13},{6,14},{7,15},{8,0},{9,1},... | collective-permute-start | bytes 393224 | tf_op jit(solution)/shard_map/ppermute | solution.py:357
  78.2 15.3 %collective-permute-start.3 = (bf16[2,256,128]{2,1,0:T(8,128)(2,1)S(1)}, bf16[2,256,128]{2,1,0:T(8,128)(2,1)S(1)}, u32[]{:S(2)}, u32[]{:S(2)}) collective-permute-start(bf16[2,256,128]{2,1,0:T(8,128)(2,1)S(1)} %get-tuple-element.34.after_ref.rest_0_), channel_id=1, source_target_pairs={{0,7},{1,6},{2,5},{3,4},{4,3},{5,2},{6,1},{7,0},{8,15},{9,14},{10,... | collective-permute-start | bytes 393224 | tf_op jit(solution)/shard_map/ppermute | solution.py:356
  119.4 24.2 %copy-start = (bf16[4096,256]{1,0:T(8,128)(2,1)S(1)}, bf16[4096,256]{1,0:T(8,128)(2,1)}, u32[]{:S(2)}) copy-start(bf16[4096,256]{1,0:T(8,128)(2,1)} %param.16) | copy-start | bytes 6291460
  139.8 6.1 %collective-permute-start.6 = (bf16[8,256,256]{2,1,0:T(8,128)(2,1)S(1)}, bf16[8,256,256]{2,1,0:T(8,128)(2,1)S(1)}, u32[]{:S(2)}, u32[]{:S(2)}) collective-permute-start(bf16[8,256,256]{2,1,0:T(8,128)(2,1)S(1)} %all_to_all.32.own_ref), channel_id=1, source_target_pairs={{0,16},{16,0},{32,48},{48,32},{64,80},{80,64},{96,112},{112,96},{1... | collective-permute-start | bytes 3145736 | tf_op jit(solution)/shard_map/ppermute | solution.py:462
